TPU v7x, 512 devices: a whole 4x4x16 slice. The times are simulated.
512 devices in a mesh: dp: 32 (over x, z_hi, y), tensor: 16 (over z_lo, core).
Axes of the slice: x: 4, y: 4, z: 16 (z_hi: 2, z_lo: 8; z = z_hi * 8 + z_lo), core: 2. Of those that a mesh axis runs over, the one named last changes fastest.
Arguments:
- grad_hidden: bfloat16 [131072, 4096], P(('dp', 'tensor')), may hold values from -6 to 6
- positions: int32 [16384], P(('dp', 'tensor')), may hold values from 0 to 255, as said below
- owner_ids: int32 [16384, 1], P(('dp', 'tensor')), may hold values from 0 to 31; in each aligned block of 32 rows (0 to 31, 32 to 63, ...) at most 2 rows name the same one
- w_proj: bfloat16 [4608, 4096], P('tensor', 'dp'), may hold values from -0.09375 to 0.09375
- pre_act: bfloat16 [32, 1024, 4608], P('dp', None, 'tensor'), may hold values from -5 to 5
Outputs:
- grad_pre: bfloat16 [32, 1024, 4608], P('dp', None, 'tensor')
Inputs may be any that keep to these rules, and one draw needn't show every extreme that they name: Within each aligned block of 32 entries (one device's image tokens) the positions are distinct and increasing. `owner_ids`: among the 32 image tokens of one device, at most 2 name the same owner.
All inputs are finite; a program needn't handle non-finite values.
Results may differ from a plain program's by a relative error of at most 0.001.
Values may be sent and summed in bfloat16 or wider, within the bound.
No kernel may reach another device: no remote copies, remote signals or barrier semaphores. Data moves between devices by JAX's collectives and lax.ppermute only.
A program may use at most 64 MiB of HBM per device.

v0:
```python
import jax
import jax.numpy as jnp
from jax import lax
from jax.sharding import PartitionSpec as P


def gelu_slope(value):
    return (
        0.5 * (1.0 + jax.scipy.special.erf(value * 0.7071067811865476))
        + value * jnp.exp(-0.5 * value * value) * 0.3989422804014327
    )


def slot_numbers(owner_ids, owner_count, cap_size):
    owners = owner_ids[:, 0]
    onehot = (owners[:, None] == jnp.arange(owner_count, dtype=jnp.int32)[None, :]).astype(
        jnp.int32
    )
    before = jnp.cumsum(onehot, axis=0) - onehot
    rank = jnp.sum(before * onehot, axis=1)
    return owners * cap_size + rank


def shards(grad_hidden, positions, owner_ids, w_proj, pre_act):
    owner_count = lax.axis_size("dp")
    group_size = lax.axis_size("tensor")
    slot_total = pre_act.shape[1]
    cap_size = slot_total // (owner_count * group_size)
    width = grad_hidden.shape[1]
    image_rows = jnp.take(grad_hidden, positions, axis=0)
    slots = slot_numbers(owner_ids, owner_count, cap_size)
    weights = lax.all_gather(w_proj, "dp", axis=1, tiled=True)
    contract = (((1,), (1,)), ((), ()))
    targets = jnp.arange(owner_count * cap_size, dtype=jnp.int32)
    dispatch = (slots[None, :] == targets[:, None]).astype(jnp.bfloat16)
    outgoing = jnp.dot(dispatch, image_rows, preferred_element_type=jnp.float32).astype(
        jnp.bfloat16
    )
    outgoing = outgoing.reshape(owner_count, cap_size, width)
    received = lax.all_to_all(outgoing, "dp", split_axis=0, concat_axis=0, tiled=True).reshape(
        owner_count * cap_size, width
    )
    projected = lax.dot_general(
        lax.all_gather(received, "tensor", axis=0, tiled=True),
        weights,
        contract,
        preferred_element_type=jnp.float32,
    )
    values = pre_act[0].astype(jnp.float32)
    return (gelu_slope(values) * projected).astype(jnp.bfloat16)[None]


def solution(mesh):
    return jax.shard_map(
        shards,
        mesh=mesh,
        in_specs=(
            P(("dp", "tensor"), None),
            P(("dp", "tensor")),
            P(("dp", "tensor"), None),
            P("tensor", "dp"),
            P("dp", None, "tensor"),
        ),
        out_specs=P("dp", None, "tensor"),
        check_vma=False,
    )
```

profile of v0, /device:TPU:1, one launch (start us, length us, event | category | flops | bytes accessed | tf_op | source)
XLA Modules:
  0.0 294.7 jit_solution(2767935245533594571)
XLA Ops:
  6.5 0.0 copy-start
  6.5 0.0 all-gather.5.cloned.1.call-start
  6.5 0.7 all-gather.5.cloned.1.call-update
  7.3 0.0 all-gather.3.cloned.1.call-start
  7.3 0.7 fusion.12
  8.0 0.1 reduce_window_sum.11
  8.1 0.7 compare_select_fusion
  8.8 0.0 copy-done
  8.8 0.0 copy-start.1
  8.8 0.0 copy-start.3
  8.8 0.7 gather_fusion
  9.5 0.0 copy-done.1
  9.5 0.2 select_reduce_fusion
  9.7 0.0 copy-done.3
  9.7 0.3 convolution_convert_fusion
  10.1 0.3 reshape.21
  10.4 40.0 %all_to_all.5 = bf16[32,2,4096]{2,1,0:T(2,128)(2,1)S(1)} all-to-all(bf16[32,2,4096]{2,1,0:T(2,128)(2,1)S(1)} %reshape.21), channel_id=1, replica_groups=mesh['dp'=32,'tensor'=16] {'dp'}, dimensions={0} | all-to-all | bytes 1048576 | tf_op jit(solution)/shard_map/all_to_all | solution.py:40
  50.4 0.0 copy-start.2
  50.4 1.0 reshape.22
  51.4 0.0 all-gather.3.cloned.1.call-update
  51.4 118.2 %all-gather.5.cloned.1.call-done = bf16[288,4096]{1,0:T(8,128)(2,1)} async-done(((bf16[288,128]{1,0:T(8,128)(2,1)}), bf16[288,4096]{1,0:T(8,128)(2,1)}) %all-gather.5.cloned.1.call-update) | async-done | bytes 2359312 | tf_op jit(solution)/shard_map/all_gather | solution.py:32
  169.6 110.4 %all-gather.3.cloned.1.call-done = bf16[1024,4096]{1,0:T(8,128)(2,1)} async-done(((bf16[64,4096]{1,0:T(8,128)(2,1)}), bf16[1024,4096]{1,0:T(8,128)(2,1)}) %all-gather.3.cloned.1.call-update) | async-done | bytes 8388624 | tf_op jit(solution)/shard_map/all_gather | solution.py:44
  280.0 0.0 copy-done.2
  280.0 7.8 %fusion.1 = bf16[1,1024,288]{1,2,0:T(8,128)(2,1)} fusion(bf16[1024,4096]{1,0:T(8,128)(2,1)} %all-gather.3.cloned.1.call-done, bf16[288,4096]{1,0:T(8,128)(2,1)} %all-gather.5.cloned.1.call-done, bf16[1,1024,288]{1,2,0:T(8,128)(2,1)S(1)} %copy-done.2), kind=kOutput, calls=%fused_computation.8 | convolution fusion | flops 2419163136 | bytes 11927552 | tf_op jit(solution)/shard_map/dot_general | solution.py:43
  (3 shorter events, 0.0 us)
Async XLA Ops:
  6.5 2.2 copy-start
  6.5 163.1 %all-gather.5.cloned.1.call-start = ((), (), s32[]{:S(2)}) async-start(), calls=%async_computation.2 | async-start | bytes 2433024 | tf_op jit(solution)/shard_map/all_gather | solution.py:32
  7.3 272.7 %all-gather.3.cloned.1.call-start = ((), (), s32[]{:S(2)}) async-start(), calls=%async_computation.1 | async-start | bytes 8912896 | tf_op jit(solution)/shard_map/all_gather | solution.py:44
  8.8 0.7 copy-start.1
  8.8 0.9 copy-start.3
  50.4 229.6 %copy-start.2 = (bf16[1,1024,288]{1,2,0:T(8,128)(2,1)S(1)}, bf16[1,1024,288]{1,2,0:T(8,128)(2,1)}, u32[]{:S(2)}) copy-start(bf16[1,1024,288]{1,2,0:T(8,128)(2,1)} %param.9) | copy-start | bytes 1769476
Sparse Core Ops, SparseCore 0:
  11.4 158.1 all-gather.4
  171.7 108.2 all-gather.2
where the time goes:
time: 298 us; the launch traced here: 295 us
  waiting for transfers between devices  229 us (77%)
  blocking collectives  40 us (13%)
  between operations  13.5 us (5%)
  matrix products  8.15 us (3%)
    all_gather x1, waiting for transfers between devices, shards(): weights = lax.all_gather(w_proj, 'dp', axis=1, tiled=True)  118 us
    all_gather x1, waiting for transfers between devices, shards(): lax.all_gather(received, 'tensor', axis=0, tiled=True)  110 us
    all_to_all x1, blocking collectives, shards(): lax.all_to_all(outgoing, 'dp', split_axis=0, concat_axis=0, tiled=True)  40 us
    dot_general x1, matrix products, shards(): lax.dot_general(lax.all_gather(received, 'tensor', axis=0, tiled=True), w...  7.81 us
  transfers between devices with their start and end apart: 2, of which 2 were waited for; matrix products, arithmetic and copies ran while one was open for 1% of the time, Pallas kernels for 0%

commit v1 on v0

v1 whole, which is shorter than its diff:
```python
import jax
import jax.numpy as jnp
import numpy as np
from jax import lax
from jax.experimental import pallas as pl
from jax.experimental.pallas import tpu as pltpu
from jax.sharding import Mesh, PartitionSpec as P

AXES = ("x", "zhi", "y", "zlo", "core")
SIZES = (4, 2, 4, 8, 2)
RING = ("zhi", "zlo")
PLANE = ("x", "y")
CODE_LANES = 128
GROUPS = ((0, -1, 1, -2), (2, -3, 3, -4), (4, -5, 5, -6), (6, -7, 7, 8))


def gelu_slope(value):
    return (
        0.5 * (1.0 + jax.scipy.special.erf(value * 0.7071067811865476))
        + value * jnp.exp(-0.5 * value * value) * 0.3989422804014327
    )


def slot_numbers(owner_ids, owner_count, cap_size):
    owners = owner_ids[:, 0]
    onehot = (owners[:, None] == jnp.arange(owner_count, dtype=jnp.int32)[None, :]).astype(
        jnp.int32
    )
    before = jnp.cumsum(onehot, axis=0) - onehot
    rank = jnp.sum(before * onehot, axis=1)
    return owners * cap_size + rank


def dispatch_kernel(zhi_ref, *refs):
    chunks, out_ref = refs[:-1], refs[-1]
    count = len(chunks)
    total, width = out_ref.shape
    rows = chunks[0].shape[0]
    target = lax.broadcasted_iota(jnp.int32, (rows, total), 1)
    rank = target % 2
    member = (target // 2) % count
    plane = target // (2 * count)
    wanted = (((plane // 4) * 8 + zhi_ref[0] * 4 + plane % 4) * 2 + rank).astype(jnp.float32)
    acc = None
    for at, chunk in enumerate(chunks):
        code = chunk[:, width : width + 1].astype(jnp.float32)
        pick = jnp.where((code == wanted) & (member == at), 1.0, 0.0).astype(jnp.bfloat16)
        part = lax.dot_general(
            pick,
            chunk[:, :width],
            (((0,), (0,)), ((), ())),
            preferred_element_type=jnp.float32,
        )
        acc = part if acc is None else acc + part
    out_ref[...] = acc.astype(out_ref.dtype)


def dispatch(chunks, zhi, width):
    total = 32 * len(chunks)
    return pl.pallas_call(
        dispatch_kernel,
        out_shape=jax.ShapeDtypeStruct((total, width), jnp.bfloat16),
        in_specs=[pl.BlockSpec(memory_space=pltpu.SMEM)]
        + [pl.BlockSpec(memory_space=pltpu.VMEM)] * len(chunks),
        out_specs=pl.BlockSpec(memory_space=pltpu.VMEM),
        compiler_params=pltpu.CompilerParams(vmem_limit_bytes=24 * 1024 * 1024),
        cost_estimate=pl.CostEstimate(
            flops=2 * 32 * total * width * len(chunks),
            bytes_accessed=4 * total * width,
            transcendentals=0,
        ),
    )(zhi, *chunks)


def shift(n, step):
    return [(i, (i + step) % n) for i in range(n)]


def final_slots(z, core):
    pieces = []
    for from_core in (core, 1 - core):
        for group in GROUPS:
            offset = jnp.asarray(np.array(group, np.int32))
            source = (z + offset + 16) % 16
            lead = ((source % 8) * 2 + from_core) * 32 + (source // 8) * 4
            plane = np.arange(16)
            plane = jnp.asarray(((plane // 4) * 8 + plane % 4).astype(np.int32))
            slot = (lead[None, :, None] + plane[:, None, None]) * 2 + jnp.arange(2, dtype=jnp.int32)
            pieces.append(slot.reshape(-1))
    return jnp.concatenate(pieces)


def shards(grad_hidden, positions, owner_ids, w_proj, pre_act):
    zhi, zlo, core = (lax.axis_index(name) for name in ("zhi", "zlo", "core"))
    z = zhi * 8 + zlo
    width = grad_hidden.shape[1]
    hidden = w_proj.shape[0]
    zhi_at = jnp.reshape(zhi, (1,)).astype(jnp.int32)

    rows = jnp.take(grad_hidden, positions, axis=0)
    code = slot_numbers(owner_ids, 32, 2).astype(jnp.bfloat16)
    packed = jnp.concatenate(
        [rows, jnp.broadcast_to(code[:, None], (code.shape[0], CODE_LANES))], axis=1
    )

    other = lax.ppermute(w_proj, "zhi", shift(2, 1))
    both = jnp.where(zhi == 0, jnp.stack([w_proj, other]), jnp.stack([other, w_proj]))
    weights = lax.all_gather(both, PLANE, axis=0, tiled=False)
    weights = weights.reshape(4, 4, 2, hidden, 128).transpose(3, 0, 2, 1, 4).reshape(hidden, width)

    held = {0: packed}
    for step in range(1, 8):
        held[-step] = lax.ppermute(held[1 - step], RING, shift(16, 1))
        held[step] = lax.ppermute(held[step - 1], RING, shift(16, 15))
    half = packed.shape[0] // 2
    held[8] = jnp.concatenate(
        [
            lax.ppermute(held[-7][:half], RING, shift(16, 1)),
            lax.ppermute(held[7][half:], RING, shift(16, 15)),
        ]
    )

    own, peer = [], []
    for group in GROUPS:
        count = len(group)
        outgoing = dispatch([held[offset] for offset in group], zhi_at, width)
        received = lax.all_to_all(
            outgoing.reshape(16, 2 * count, width), PLANE, split_axis=0, concat_axis=0, tiled=True
        ).reshape(32 * count, width)
        own.append(received)
        peer.append(lax.ppermute(received, "core", shift(2, 1)))

    contract = (((1,), (1,)), ((), ()))
    projected = [
        lax.dot_general(weights, part, contract, preferred_element_type=jnp.float32)
        for part in own + peer
    ]
    projected = jnp.concatenate(projected, axis=1)

    slots = final_slots(z, core)
    place = (slots[:, None] == jnp.arange(1024, dtype=jnp.int32)[None, :]).astype(jnp.bfloat16)
    values = lax.dot_general(
        pre_act[0].T, place, contract, preferred_element_type=jnp.float32
    )
    gradient = (gelu_slope(values) * projected).astype(jnp.bfloat16)
    placed = jnp.dot(gradient, place, preferred_element_type=jnp.float32).astype(jnp.bfloat16)
    return placed.T[None]


def solution(mesh):
    fine = Mesh(mesh.devices.reshape(SIZES), AXES)
    return jax.shard_map(
        shards,
        mesh=fine,
        in_specs=(
            P(AXES, None),
            P(AXES),
            P(AXES, None),
            P(("zlo", "core"), ("x", "zhi", "y")),
            P(("x", "zhi", "y"), None, ("zlo", "core")),
        ),
        out_specs=P(("x", "zhi", "y"), None, ("zlo", "core")),
        check_vma=False,
    )
```

time: 298 us -> 202 us (0.68)
  waiting for transfers between devices: 229 us -> 10.2 us
  starting transfers between devices: 0.04 us -> 117 us
  blocking collectives: 40 us -> 0 us
  matrix products: 8.15 us -> 25.5 us
  Pallas kernels: 0 us -> 10.4 us
  local copies, waits for them, and re-layouts: 2.05 us -> 12.2 us
  other arithmetic: 1.64 us -> 10.1 us
    all_gather x2 -> x1, waiting for transfers between devices: 229 us -> 0.02 us  [shards(): weights = lax.all_gather(both, PLANE, axis=0, tiled=False)]
    ppermute x0 -> x21, starting transfers between devices: none -> 90.1 us  [the longest x7 32 us: shards(): held[step] = lax.ppermute(held[step - 1], RING, shift(16, 15))]
    all_to_all x1 -> x0, blocking collectives: 40 us -> none  [shards(): lax.all_to_all(outgoing, 'dp', split_axis=0, concat_axis=0, tiled=True)]
    all_to_all x0 -> x4, starting transfers between devices: none -> 26.5 us  [shards(): lax.all_to_all(outgoing.reshape(16, 2 * count, width), PLANE, split_axis=...]
    dot_general x2 -> x9, matrix products: 8.15 us -> 25.5 us  [the longest x8 21.1 us: shards(): lax.dot_general(weights, part, contract, preferred_element_type=jnp.float32)]
    pallas_call x0 -> x4, Pallas kernels: none -> 10.4 us  [dispatch(): pl.pallas_call(dispatch_kernel, out_shape=jax.ShapeDtypeStruct((total, wi...]
    ppermute x0 -> x21, waiting for transfers between devices: none -> 9.66 us  [the longest x7 7.13 us: shards(): held[-step] = lax.ppermute(held[1 - step], RING, shift(16, 1))]
    reshape x2, local copies, waits for them, and re-layouts: 1.33 us -> 10.1 us  [shards(): weights.reshape(4, 4, 2, hidden, 128).transpose(3, 0, 2, 1, 4)]
  transfers between devices with their start and end apart: 2 -> 26, of which waited for: 2 -> 8; matrix products, arithmetic and copies ran while one was open for 1% -> 18% of each run, Pallas kernels for 0% -> 5%
where the time goes in v1:
time: 202 us; the launch traced here: 199 us
  starting transfers between devices  117 us (58%)
  matrix products  25.5 us (13%)
  between operations  14.1 us (7%)
  local copies, waits for them, and re-layouts  12.2 us (6%)
  Pallas kernels  10.4 us (5%)
  waiting for transfers between devices  10.2 us (5%)
  other arithmetic  10.1 us (5%)
    ppermute x7, starting transfers between devices, shards(): held[step] = lax.ppermute(held[step - 1], RING, shift(16, 15))  32 us
    all_to_all x4, starting transfers between devices, shards(): lax.all_to_all(outgoing.reshape(16, 2 * count, width), PLANE, split_axis=...  26.5 us
    ppermute x4, starting transfers between devices, shards(): peer.append(lax.ppermute(received, 'core', shift(2, 1)))  21.9 us
    dot_general x8, matrix products, shards(): lax.dot_general(weights, part, contract, preferred_element_type=jnp.float32)  21.1 us
    ppermute x7, starting transfers between devices, shards(): held[-step] = lax.ppermute(held[1 - step], RING, shift(16, 1))  20.8 us
    pallas_call x4, Pallas kernels, dispatch(): pl.pallas_call(dispatch_kernel, out_shape=jax.ShapeDtypeStruct((total, wi...  10.4 us
    reshape x2, local copies, waits for them, and re-layouts, shards(): weights.reshape(4, 4, 2, hidden, 128).transpose(3, 0, 2, 1, 4)  10.1 us
    ppermute x1, starting transfers between devices, shards(): other = lax.ppermute(w_proj, 'zhi', shift(2, 1))  8.89 us
  transfers between devices with their start and end apart: 26, of which 8 were waited for; matrix products, arithmetic and copies ran while one was open for 18% of the time, Pallas kernels for 5%

profile of v1, /device:TPU:1, one launch (start us, length us, event | category | flops | bytes accessed | tf_op | source)
XLA Modules:
  0.0 199.0 jit_solution(6373699233386714452)
XLA Ops:
  8.8 0.8 select_reduce_fusion
  11.3 4.4 %collective-permute-start.1 = (bf16[32,4224]{1,0:T(8,128)(2,1)S(1)}, bf16[32,4224]{1,0:T(8,128)(2,1)S(1)}, u32[]{:S(2)}, u32[]{:S(2)}) collective-permute-start(bf16[32,4224]{1,0:T(8,128)(2,1)S(1)} %pad_maximum_fusion.refs_0_), channel_id=1, source_target_pairs={{0,2},{2,4},{4,6},{6,8},{8,10},{10,12},{12,14},{14,64},{64,66},{66... | collective-permute-start | bytes 811016 | tf_op jit(solution)/shard_map/ppermute | solution.py:113
  15.6 9.5 %collective-permute-start.2 = (bf16[32,4224]{1,0:T(8,128)(2,1)S(1)}, bf16[32,4224]{1,0:T(8,128)(2,1)S(1)}, u32[]{:S(2)}, u32[]{:S(2)}) collective-permute-start(bf16[32,4224]{1,0:T(8,128)(2,1)S(1)} %pad_maximum_fusion.refs_0_), channel_id=1, source_target_pairs={{0,78},{2,0},{4,2},{6,4},{8,6},{10,8},{12,10},{14,12},{64,14},{66,... | collective-permute-start | bytes 811016 | tf_op jit(solution)/shard_map/ppermute | solution.py:114
  25.2 8.9 %collective-permute-start = (bf16[288,128]{1,0:T(8,128)(2,1)S(1)}, bf16[288,128]{1,0:T(8,128)(2,1)}, u32[]{:S(2)}, u32[]{:S(2)}) collective-permute-start(bf16[288,128]{1,0:T(8,128)(2,1)S(1)} %copy-done.4), channel_id=1, source_target_pairs={{0,64},{64,0},{1,65},{65,1},{2,66},{66,2},{3,67},{67,3},{4,68},{68... | collective-permute-start | bytes 221192 | tf_op jit(solution)/shard_map/ppermute | solution.py:106
  34.7 1.9 collective-permute-start.3
  37.2 4.6 %collective-permute-start.4 = (bf16[32,4224]{1,0:T(8,128)(2,1)S(1)}, bf16[32,4224]{1,0:T(8,128)(2,1)S(1)}, u32[]{:S(2)}, u32[]{:S(2)}) collective-permute-start(bf16[32,4224]{1,0:T(8,128)(2,1)S(1)} %collective-permute-done.2.refs_2_), channel_id=1, source_target_pairs={{0,78},{2,0},{4,2},{6,4},{8,6},{10,8},{12,10},{14,12},{64,14},{66,... | collective-permute-start | bytes 811016 | tf_op jit(solution)/shard_map/ppermute | solution.py:114
  41.8 1.6 maximum_select_fusion
  43.5 1.7 collective-permute-done.3.refs_3_
  45.2 2.3 %shard_map.199 = bf16[128,4096]{1,0:T(8,128)(2,1)} custom-call(s32[1]{0:T(128)} %bitcast.6.zhi_ref, bf16[32,4224]{1,0:T(8,128)(2,1)S(1)} %pad_maximum_fusion.refs_0_, bf16[32,4224]{1,0:T(8,128)(2,1)S(1)} %collective-permute-done.1.refs_1_, bf16[32,4224]{1,0:T(8,128)(2,1)S(1)} %collective-permute-done.2.refs_2_, ...), custom_call_target="tpu_custom_call" | custom-call | flops 134217728 | bytes 2097152 | tf_op jit(solution)/shard_map/pallas_call | solution.py:60
  47.5 7.0 %all-to-all-start = ((bf16[16,8,4096]{2,1,0:T(8,128)(2,1)}), bf16[16,8,4096]{2,1,0:T(8,128)(2,1)}, u32[]{:S(2)}, u32[]{:S(2)}) async-start(bf16[16,8,4096]{2,1,0:T(8,128)(2,1)} %bitcast.10), calls=%async_computation | async-start | bytes 2097152 | tf_op jit(solution)/shard_map/all_to_all | solution.py:127
  54.5 3.4 %collective-permute-start.5 = (bf16[32,4224]{1,0:T(8,128)(2,1)S(1)}, bf16[32,4224]{1,0:T(8,128)(2,1)S(1)}, u32[]{:S(2)}, u32[]{:S(2)}) collective-permute-start(bf16[32,4224]{1,0:T(8,128)(2,1)S(1)} %collective-permute-done.3.refs_3_), channel_id=1, source_target_pairs={{0,2},{2,4},{4,6},{6,8},{8,10},{10,12},{12,14},{14,64},{64,66},{66... | collective-permute-start | bytes 811016 | tf_op jit(solution)/shard_map/ppermute | solution.py:113
  57.9 3.1 %collective-permute-start.6 = (bf16[32,4224]{1,0:T(8,128)(2,1)S(1)}, bf16[32,4224]{1,0:T(8,128)(2,1)S(1)}, u32[]{:S(2)}, u32[]{:S(2)}) collective-permute-start(bf16[32,4224]{1,0:T(8,128)(2,1)S(1)} %collective-permute-done.4.refs_0_), channel_id=1, source_target_pairs={{0,78},{2,0},{4,2},{6,4},{8,6},{10,8},{12,10},{14,12},{64,14},{66,... | collective-permute-start | bytes 811016 | tf_op jit(solution)/shard_map/ppermute | solution.py:114
  61.1 2.4 %collective-permute-done.5.refs_1_ = bf16[32,4224]{1,0:T(8,128)(2,1)S(1)} collective-permute-done((bf16[32,4224]{1,0:T(8,128)(2,1)S(1)}, bf16[32,4224]{1,0:T(8,128)(2,1)S(1)}, u32[]{:S(2)}, u32[]{:S(2)}) %collective-permute-start.5) | collective-permute-done | bytes 270368 | tf_op jit(solution)/shard_map/ppermute | solution.py:113
  63.5 3.7 %collective-permute-start.7 = (bf16[32,4224]{1,0:T(8,128)(2,1)S(1)}, bf16[32,4224]{1,0:T(8,128)(2,1)S(1)}, u32[]{:S(2)}, u32[]{:S(2)}) collective-permute-start(bf16[32,4224]{1,0:T(8,128)(2,1)S(1)} %collective-permute-done.5.refs_1_), channel_id=1, source_target_pairs={{0,2},{2,4},{4,6},{6,8},{8,10},{10,12},{12,14},{14,64},{64,66},{66... | collective-permute-start | bytes 811016 | tf_op jit(solution)/shard_map/ppermute | solution.py:113
  67.2 2.8 %collective-permute-start.8 = (bf16[32,4224]{1,0:T(8,128)(2,1)S(1)}, bf16[32,4224]{1,0:T(8,128)(2,1)S(1)}, u32[]{:S(2)}, u32[]{:S(2)}) collective-permute-start(bf16[32,4224]{1,0:T(8,128)(2,1)S(1)} %collective-permute-done.6.refs_2_), channel_id=1, source_target_pairs={{0,78},{2,0},{4,2},{6,4},{8,6},{10,8},{12,10},{14,12},{64,14},{66,... | collective-permute-start | bytes 811016 | tf_op jit(solution)/shard_map/ppermute | solution.py:114
  70.7 1.5 collective-permute-done.7.refs_3_
  72.3 3.3 %collective-permute-start.9 = (bf16[32,4224]{1,0:T(8,128)(2,1)S(1)}, bf16[32,4224]{1,0:T(8,128)(2,1)S(1)}, u32[]{:S(2)}, u32[]{:S(2)}) collective-permute-start(bf16[32,4224]{1,0:T(8,128)(2,1)S(1)} %collective-permute-done.7.refs_3_), channel_id=1, source_target_pairs={{0,2},{2,4},{4,6},{6,8},{8,10},{10,12},{12,14},{14,64},{64,66},{66... | collective-permute-start | bytes 811016 | tf_op jit(solution)/shard_map/ppermute | solution.py:113
  75.6 3.2 %collective-permute-start.10 = (bf16[32,4224]{1,0:T(8,128)(2,1)S(1)}, bf16[32,4224]{1,0:T(8,128)(2,1)}, u32[]{:S(2)}, u32[]{:S(2)}) collective-permute-start(bf16[32,4224]{1,0:T(8,128)(2,1)S(1)} %collective-permute-done.8.refs_0_), channel_id=1, source_target_pairs={{0,78},{2,0},{4,2},{6,4},{8,6},{10,8},{12,10},{14,12},{64,14},{66,... | collective-permute-start | bytes 811016 | tf_op jit(solution)/shard_map/ppermute | solution.py:114
  78.8 2.3 %shard_map.200 = bf16[128,4096]{1,0:T(8,128)(2,1)} custom-call(s32[1]{0:T(128)} %bitcast.6.zhi_ref, bf16[32,4224]{1,0:T(8,128)(2,1)S(1)} %collective-permute-done.4.refs_0_, bf16[32,4224]{1,0:T(8,128)(2,1)S(1)} %collective-permute-done.5.refs_1_, bf16[32,4224]{1,0:T(8,128)(2,1)S(1)} %collective-permute-done.6.refs_2_, ...), custom_call_target="tpu_custom_call" | custom-call | flops 134217728 | bytes 2097152 | tf_op jit(solution)/shard_map/pallas_call | solution.py:60
  81.1 6.4 %all-to-all-start.1 = ((bf16[16,8,4096]{2,1,0:T(8,128)(2,1)}), bf16[16,8,4096]{2,1,0:T(8,128)(2,1)}, u32[]{:S(2)}, u32[]{:S(2)}) async-start(bf16[16,8,4096]{2,1,0:T(8,128)(2,1)} %bitcast.12), calls=%async_computation.1 | async-start | bytes 2097152 | tf_op jit(solution)/shard_map/all_to_all | solution.py:127
  87.7 2.2 %collective-permute-start.11 = (bf16[32,4224]{1,0:T(8,128)(2,1)S(1)}, bf16[32,4224]{1,0:T(8,128)(2,1)}, u32[]{:S(2)}, u32[]{:S(2)}) collective-permute-start(bf16[32,4224]{1,0:T(8,128)(2,1)S(1)} %collective-permute-done.9.refs_1_), channel_id=1, source_target_pairs={{0,2},{2,4},{4,6},{6,8},{8,10},{10,12},{12,14},{14,64},{64,66},{66... | collective-permute-start | bytes 811016 | tf_op jit(solution)/shard_map/ppermute | solution.py:113
  89.9 4.3 %collective-permute-start.12 = (bf16[32,4224]{1,0:T(8,128)(2,1)}, bf16[32,4224]{1,0:T(8,128)(2,1)S(1)}, u32[]{:S(2)}, u32[]{:S(2)}) collective-permute-start(bf16[32,4224]{1,0:T(8,128)(2,1)} %collective-permute-done.10.refs_2_), channel_id=1, source_target_pairs={{0,78},{2,0},{4,2},{6,4},{8,6},{10,8},{12,10},{14,12},{64,14},{66,... | collective-permute-start | bytes 811016 | tf_op jit(solution)/shard_map/ppermute | solution.py:114
  95.0 1.5 collective-permute-done.11.refs_3_
  96.5 1.9 collective-permute-start.13
  98.6 4.6 %collective-permute-start.14 = (bf16[32,4224]{1,0:T(8,128)(2,1)S(1)}, bf16[32,4224]{1,0:T(8,128)(2,1)S(1)}, u32[]{:S(2)}, u32[]{:S(2)}) collective-permute-start(bf16[32,4224]{1,0:T(8,128)(2,1)S(1)} %collective-permute-done.12.refs_0_), channel_id=1, source_target_pairs={{0,78},{2,0},{4,2},{6,4},{8,6},{10,8},{12,10},{14,12},{64,14},{66,... | collective-permute-start | bytes 811016 | tf_op jit(solution)/shard_map/ppermute | solution.py:114
  103.2 1.4 iota_add_fusion.3
  104.6 3.4 %shard_map.201 = bf16[128,4096]{1,0:T(8,128)(2,1)} custom-call(s32[1]{0:T(128)} %bitcast.6.zhi_ref, bf16[32,4224]{1,0:T(8,128)(2,1)S(1)} %collective-permute-done.8.refs_0_, bf16[32,4224]{1,0:T(8,128)(2,1)S(1)} %collective-permute-done.9.refs_1_, bf16[32,4224]{1,0:T(8,128)(2,1)} %collective-permute-done.10.refs_2_, ...), custom_call_target="tpu_custom_call" | custom-call | flops 134217728 | bytes 2097152 | tf_op jit(solution)/shard_map/pallas_call | solution.py:60
  108.0 6.8 %all-to-all-start.2 = ((bf16[16,8,4096]{2,1,0:T(8,128)(2,1)}), bf16[16,8,4096]{2,1,0:T(8,128)(2,1)}, u32[]{:S(2)}, u32[]{:S(2)}) async-start(bf16[16,8,4096]{2,1,0:T(8,128)(2,1)} %bitcast.14), calls=%async_computation.2 | async-start | bytes 2097152 | tf_op jit(solution)/shard_map/all_to_all | solution.py:127
  114.9 1.9 collective-permute-start.15
  116.9 4.6 %collective-permute-start.16 = (bf16[16,4224]{1,0:T(8,128)(2,1)S(1)}, bf16[16,4224]{1,0:T(8,128)(2,1)S(1)}, u32[]{:S(2)}, u32[]{:S(2)}) collective-permute-start(bf16[16,4224]{1,0:T(8,128)(2,1)S(1)} %slice.11), channel_id=1, source_target_pairs={{0,78},{2,0},{4,2},{6,4},{8,6},{10,8},{12,10},{14,12},{64,14},{66,... | collective-permute-start | bytes 405512 | tf_op jit(solution)/shard_map/ppermute | solution.py:119
  121.9 1.9 collective-permute-done.16
  123.8 2.4 %shard_map.202 = bf16[128,4096]{1,0:T(8,128)(2,1)} custom-call(s32[1]{0:T(128)} %bitcast.6.zhi_ref, bf16[32,4224]{1,0:T(8,128)(2,1)S(1)} %collective-permute-done.12.refs_0_, bf16[32,4224]{1,0:T(8,128)(2,1)S(1)} %collective-permute-done.13.refs_1_, bf16[32,4224]{1,0:T(8,128)(2,1)S(1)} %collective-permute-done.14.refs_2_, ...), custom_call_target="tpu_custom_call" | custom-call | flops 134217728 | bytes 2097152 | tf_op jit(solution)/shard_map/pallas_call | solution.py:60
  126.7 6.4 %all-to-all-start.3 = ((bf16[16,8,4096]{2,1,0:T(8,128)(2,1)}), bf16[16,8,4096]{2,1,0:T(8,128)(2,1)S(1)}, u32[]{:S(2)}, u32[]{:S(2)}) async-start(bf16[16,8,4096]{2,1,0:T(8,128)(2,1)} %bitcast.16), calls=%async_computation.3 | async-start | bytes 2097152 | tf_op jit(solution)/shard_map/all_to_all | solution.py:127
  134.5 10.3 %collective-permute-start.17 = (bf16[128,4096]{1,0:T(8,128)(2,1)}, bf16[128,4096]{1,0:T(8,128)(2,1)}, u32[]{:S(2)}, u32[]{:S(2)}) collective-permute-start(bf16[128,4096]{1,0:T(8,128)(2,1)} %bitcast.11), channel_id=1, source_target_pairs={{0,1},{1,0},{2,3},{3,2},{4,5},{5,4},{6,7},{7,6},{8,9},{9,8},{10,11... | collective-permute-start | bytes 3145736 | tf_op jit(solution)/shard_map/ppermute | solution.py:131
  144.8 1.9 collective-permute-start.18
  146.7 2.4 %collective-permute-start.19 = (bf16[128,4096]{1,0:T(8,128)(2,1)}, bf16[128,4096]{1,0:T(8,128)(2,1)}, u32[]{:S(2)}, u32[]{:S(2)}) collective-permute-start(bf16[128,4096]{1,0:T(8,128)(2,1)} %bitcast.15), channel_id=1, source_target_pairs={{0,1},{1,0},{2,3},{3,2},{4,5},{5,4},{6,7},{7,6},{8,9},{9,8},{10,11... | collective-permute-start | bytes 3145736 | tf_op jit(solution)/shard_map/ppermute | solution.py:131
  149.2 7.3 %collective-permute-start.20 = (bf16[128,4096]{1,0:T(8,128)(2,1)S(1)}, bf16[128,4096]{1,0:T(8,128)(2,1)}, u32[]{:S(2)}, u32[]{:S(2)}) collective-permute-start(bf16[128,4096]{1,0:T(8,128)(2,1)S(1)} %bitcast.57), channel_id=1, source_target_pairs={{0,1},{1,0},{2,3},{3,2},{4,5},{5,4},{6,7},{7,6},{8,9},{9,8},{10,11... | collective-permute-start | bytes 3145736 | tf_op jit(solution)/shard_map/ppermute | solution.py:131
  156.5 4.9 %copy.25 = bf16[4,4,2,288,128]{4,1,2,0,3:T(4,128)(2,1)} copy(bf16[4,4,2,288,128]{4,3,2,1,0:T(8,128)(2,1)} %bitcast.58) | data formatting | bytes 4718592 | tf_op jit(solution)/shard_map/reshape | solution.py:109
  161.4 5.2 %reshape.404 = bf16[288,4096]{1,0:T(8,128)(2,1)} reshape(bf16[288,4,2,4,128]{4,3,2,1,0:T(4,128)(2,1)} %bitcast.56) | data formatting | bytes 4718592 | tf_op jit(solution)/shard_map/reshape | solution.py:109
  166.6 3.5 %convolution_dynamic-update-slice_fusion.7 = f32[288,1024]{1,0:T(8,128)} fusion(bf16[288,4096]{1,0:T(8,128)(2,1)} %reshape.404, bf16[16,8,4096]{2,1,0:T(8,128)(2,1)} %all-to-all-done), kind=kOutput, calls=%fused_computation.24 | convolution fusion | flops 301989888 | bytes 3555328 | tf_op jit(solution)/shard_map/dot_general | solution.py:135
  170.1 2.7 %convolution_dynamic-update-slice_fusion.6 = f32[288,1024]{1,0:T(8,128)} fusion(f32[288,1024]{1,0:T(8,128)} %convolution_dynamic-update-slice_fusion.7, bf16[288,4096]{1,0:T(8,128)(2,1)S(1)} %copy-done.1, bf16[16,8,4096]{2,1,0:T(8,128)(2,1)} %all-to-all-done.1), kind=kOutput, calls=%fused_computation.23 | convolution fusion | flops 301989888 | bytes 3555328 | tf_op jit(solution)/shard_map/dot_general | solution.py:135
  172.8 2.7 %convolution_dynamic-update-slice_fusion.5 = f32[288,1024]{1,0:T(8,128)} fusion(f32[288,1024]{1,0:T(8,128)} %convolution_dynamic-update-slice_fusion.6, bf16[288,4096]{1,0:T(8,128)(2,1)S(1)} %copy-done.1, bf16[16,8,4096]{2,1,0:T(8,128)(2,1)} %all-to-all-done.2), kind=kOutput, calls=%fused_computation.22 | convolution fusion | flops 301989888 | bytes 3555328 | tf_op jit(solution)/shard_map/dot_general | solution.py:135
  175.5 1.4 convolution_dynamic-update-slice_fusion.4
  176.9 2.7 %convolution_dynamic-update-slice_fusion.3 = f32[288,1024]{1,0:T(8,128)} fusion(f32[288,1024]{1,0:T(8,128)} %convolution_dynamic-update-slice_fusion.4, bf16[288,4096]{1,0:T(8,128)(2,1)S(1)} %copy-done.1, bf16[128,4096]{1,0:T(8,128)(2,1)} %collective-permute-done.17), kind=kOutput, calls=%fused_computation.20 | convolution fusion | flops 301989888 | bytes 3555328 | tf_op jit(solution)/shard_map/dot_general | solution.py:135
  179.6 2.7 %convolution_dynamic-update-slice_fusion.2 = f32[288,1024]{1,0:T(8,128)} fusion(f32[288,1024]{1,0:T(8,128)} %convolution_dynamic-update-slice_fusion.3, bf16[288,4096]{1,0:T(8,128)(2,1)S(1)} %copy-done.1, bf16[128,4096]{1,0:T(8,128)(2,1)} %collective-permute-done.18), kind=kOutput, calls=%fused_computation.19 | convolution fusion | flops 301989888 | bytes 3555328 | tf_op jit(solution)/shard_map/dot_general | solution.py:135
  182.3 2.7 %convolution_dynamic-update-slice_fusion.1 = f32[288,1024]{1,0:T(8,128)} fusion(f32[288,1024]{1,0:T(8,128)} %convolution_dynamic-update-slice_fusion.2, bf16[288,4096]{1,0:T(8,128)(2,1)S(1)} %copy-done.1, bf16[128,4096]{1,0:T(8,128)(2,1)} %collective-permute-done.19), kind=kOutput, calls=%fused_computation.18 | convolution fusion | flops 301989888 | bytes 3555328 | tf_op jit(solution)/shard_map/dot_general | solution.py:135
  185.0 2.7 %convolution_dynamic-update-slice_fusion = f32[288,1024]{1,0:T(8,128)} fusion(f32[288,1024]{1,0:T(8,128)} %convolution_dynamic-update-slice_fusion.1, bf16[288,4096]{1,0:T(8,128)(2,1)S(1)} %copy-done.1, bf16[128,4096]{1,0:T(8,128)(2,1)} %collective-permute-done.20), kind=kOutput, calls=%fused_computation.17 | convolution fusion | flops 301989888 | bytes 3555328 | tf_op jit(solution)/shard_map/dot_general | solution.py:135
  187.7 4.4 %fusion.6 = bf16[1,1024,288]{1,2,0:T(8,128)(2,1)} fusion(s32[1024]{0:T(1024)S(1)} %constant_dynamic-update-slice_fusion.1, f32[288,1024]{1,0:T(8,128)} %convolution_dynamic-update-slice_fusion, bf16[1,1024,288]{1,2,0:T(8,128)(2,1)S(1)} %copy-done.16), kind=kOutput, calls=%fused_computation.10 | convolution fusion | flops 1213300736 | bytes 2363392 | tf_op jit(solution)/shard_map/dot_general | solution.py:146
  (101 shorter events, 9.4 us)
Async XLA Ops:
  6.5 3.8 %copy-start = (bf16[256,4096]{1,0:T(8,128)(2,1)S(1)}, bf16[256,4096]{1,0:T(8,128)(2,1)}, u32[]{:S(2)}) copy-start(bf16[256,4096]{1,0:T(8,128)(2,1)} %param.21) | copy-start | bytes 6291460
  6.5 150.0 %all-gather.2.cloned.1.call-start = ((), (), s32[]{:S(2)}) async-start(), calls=%async_computation.4 | async-start | bytes 2506752 | tf_op jit(solution)/shard_map/all_gather | solution.py:108
  10.3 14.8 %copy-start.4 = (bf16[288,128]{1,0:T(8,128)(2,1)S(1)}, bf16[288,128]{1,0:T(8,128)(2,1)}, u32[]{:S(2)}) copy-start(bf16[288,128]{1,0:T(8,128)(2,1)} %param.24) | copy-start | bytes 221188
  10.3 23.8 %copy-start.15 = (s32[4]{0:T(128)S(1)}, s32[4]{0:T(128)}, u32[]{:S(2)}) copy-start(s32[4]{0:T(128)} %constant.223.clone) | copy-start | bytes 52
  10.3 26.3 %copy-start.14 = (s32[4]{0:T(128)S(1)}, s32[4]{0:T(128)}, u32[]{:S(2)}) copy-start(s32[4]{0:T(128)} %constant.224.clone) | copy-start | bytes 52
  11.3 23.4 %collective-permute-start.1 = (bf16[32,4224]{1,0:T(8,128)(2,1)S(1)}, bf16[32,4224]{1,0:T(8,128)(2,1)S(1)}, u32[]{:S(2)}, u32[]{:S(2)}) collective-permute-start(bf16[32,4224]{1,0:T(8,128)(2,1)S(1)} %pad_maximum_fusion.refs_0_), channel_id=1, source_target_pairs={{0,2},{2,4},{4,6},{6,8},{8,10},{10,12},{12,14},{14,64},{64,66},{66... | collective-permute-start | bytes 811016 | tf_op jit(solution)/shard_map/ppermute | solution.py:113
  15.6 21.6 %collective-permute-start.2 = (bf16[32,4224]{1,0:T(8,128)(2,1)S(1)}, bf16[32,4224]{1,0:T(8,128)(2,1)S(1)}, u32[]{:S(2)}, u32[]{:S(2)}) collective-permute-start(bf16[32,4224]{1,0:T(8,128)(2,1)S(1)} %pad_maximum_fusion.refs_0_), channel_id=1, source_target_pairs={{0,78},{2,0},{4,2},{6,4},{8,6},{10,8},{12,10},{14,12},{64,14},{66,... | collective-permute-start | bytes 811016 | tf_op jit(solution)/shard_map/ppermute | solution.py:114
  25.2 16.6 %collective-permute-start = (bf16[288,128]{1,0:T(8,128)(2,1)S(1)}, bf16[288,128]{1,0:T(8,128)(2,1)}, u32[]{:S(2)}, u32[]{:S(2)}) collective-permute-start(bf16[288,128]{1,0:T(8,128)(2,1)S(1)} %copy-done.4), channel_id=1, source_target_pairs={{0,64},{64,0},{1,65},{65,1},{2,66},{66,2},{3,67},{67,3},{4,68},{68... | collective-permute-start | bytes 221192 | tf_op jit(solution)/shard_map/ppermute | solution.py:106
  34.7 10.5 %collective-permute-start.3 = (bf16[32,4224]{1,0:T(8,128)(2,1)S(1)}, bf16[32,4224]{1,0:T(8,128)(2,1)S(1)}, u32[]{:S(2)}, u32[]{:S(2)}) collective-permute-start(bf16[32,4224]{1,0:T(8,128)(2,1)S(1)} %collective-permute-done.1.refs_1_), channel_id=1, source_target_pairs={{0,2},{2,4},{4,6},{6,8},{8,10},{10,12},{12,14},{14,64},{64,66},{66... | collective-permute-start | bytes 811016 | tf_op jit(solution)/shard_map/ppermute | solution.py:113
  37.2 20.7 %collective-permute-start.4 = (bf16[32,4224]{1,0:T(8,128)(2,1)S(1)}, bf16[32,4224]{1,0:T(8,128)(2,1)S(1)}, u32[]{:S(2)}, u32[]{:S(2)}) collective-permute-start(bf16[32,4224]{1,0:T(8,128)(2,1)S(1)} %collective-permute-done.2.refs_2_), channel_id=1, source_target_pairs={{0,78},{2,0},{4,2},{6,4},{8,6},{10,8},{12,10},{14,12},{64,14},{66,... | collective-permute-start | bytes 811016 | tf_op jit(solution)/shard_map/ppermute | solution.py:114
  47.5 7.0 %copy-start.13 = (s32[4]{0:T(128)S(1)}, s32[4]{0:T(128)}, u32[]{:S(2)}) copy-start(s32[4]{0:T(128)} %constant.222.clone) | copy-start | bytes 52
  47.5 13.5 %copy-start.12 = (s32[4]{0:T(128)S(1)}, s32[4]{0:T(128)}, u32[]{:S(2)}) copy-start(s32[4]{0:T(128)} %constant.220.clone) | copy-start | bytes 52
  47.5 22.5 %copy-start.9 = (s32[4]{0:T(128)S(1)}, s32[4]{0:T(128)}, u32[]{:S(2)}) copy-start(s32[4]{0:T(128)} %get-tuple-element.8) | copy-start | bytes 52
  47.5 22.5 %copy-start.10 = (s32[4]{0:T(128)S(1)}, s32[4]{0:T(128)}, u32[]{:S(2)}) copy-start(s32[4]{0:T(128)} %get-tuple-element.5) | copy-start | bytes 52
  47.5 22.5 %copy-start.11 = (s32[16]{0:T(128)S(1)}, s32[16]{0:T(128)}, u32[]{:S(2)}) copy-start(s32[16]{0:T(128)} %constant.221.clone) | copy-start | bytes 196
  47.5 33.6 %all-to-all-start = ((bf16[16,8,4096]{2,1,0:T(8,128)(2,1)}), bf16[16,8,4096]{2,1,0:T(8,128)(2,1)}, u32[]{:S(2)}, u32[]{:S(2)}) async-start(bf16[16,8,4096]{2,1,0:T(8,128)(2,1)} %bitcast.10), calls=%async_computation | async-start | bytes 2097152 | tf_op jit(solution)/shard_map/all_to_all | solution.py:127
  54.5 8.9 %collective-permute-start.5 = (bf16[32,4224]{1,0:T(8,128)(2,1)S(1)}, bf16[32,4224]{1,0:T(8,128)(2,1)S(1)}, u32[]{:S(2)}, u32[]{:S(2)}) collective-permute-start(bf16[32,4224]{1,0:T(8,128)(2,1)S(1)} %collective-permute-done.3.refs_3_), channel_id=1, source_target_pairs={{0,2},{2,4},{4,6},{6,8},{8,10},{10,12},{12,14},{14,64},{64,66},{66... | collective-permute-start | bytes 811016 | tf_op jit(solution)/shard_map/ppermute | solution.py:113
  57.9 9.2 %collective-permute-start.6 = (bf16[32,4224]{1,0:T(8,128)(2,1)S(1)}, bf16[32,4224]{1,0:T(8,128)(2,1)S(1)}, u32[]{:S(2)}, u32[]{:S(2)}) collective-permute-start(bf16[32,4224]{1,0:T(8,128)(2,1)S(1)} %collective-permute-done.4.refs_0_), channel_id=1, source_target_pairs={{0,78},{2,0},{4,2},{6,4},{8,6},{10,8},{12,10},{14,12},{64,14},{66,... | collective-permute-start | bytes 811016 | tf_op jit(solution)/shard_map/ppermute | solution.py:114
  63.5 8.8 %collective-permute-start.7 = (bf16[32,4224]{1,0:T(8,128)(2,1)S(1)}, bf16[32,4224]{1,0:T(8,128)(2,1)S(1)}, u32[]{:S(2)}, u32[]{:S(2)}) collective-permute-start(bf16[32,4224]{1,0:T(8,128)(2,1)S(1)} %collective-permute-done.5.refs_1_), channel_id=1, source_target_pairs={{0,2},{2,4},{4,6},{6,8},{8,10},{10,12},{12,14},{14,64},{64,66},{66... | collective-permute-start | bytes 811016 | tf_op jit(solution)/shard_map/ppermute | solution.py:113
  67.2 8.4 %collective-permute-start.8 = (bf16[32,4224]{1,0:T(8,128)(2,1)S(1)}, bf16[32,4224]{1,0:T(8,128)(2,1)S(1)}, u32[]{:S(2)}, u32[]{:S(2)}) collective-permute-start(bf16[32,4224]{1,0:T(8,128)(2,1)S(1)} %collective-permute-done.6.refs_2_), channel_id=1, source_target_pairs={{0,78},{2,0},{4,2},{6,4},{8,6},{10,8},{12,10},{14,12},{64,14},{66,... | collective-permute-start | bytes 811016 | tf_op jit(solution)/shard_map/ppermute | solution.py:114
  72.3 15.4 %collective-permute-start.9 = (bf16[32,4224]{1,0:T(8,128)(2,1)S(1)}, bf16[32,4224]{1,0:T(8,128)(2,1)S(1)}, u32[]{:S(2)}, u32[]{:S(2)}) collective-permute-start(bf16[32,4224]{1,0:T(8,128)(2,1)S(1)} %collective-permute-done.7.refs_3_), channel_id=1, source_target_pairs={{0,2},{2,4},{4,6},{6,8},{8,10},{10,12},{12,14},{14,64},{64,66},{66... | collective-permute-start | bytes 811016 | tf_op jit(solution)/shard_map/ppermute | solution.py:113
  75.6 14.3 %collective-permute-start.10 = (bf16[32,4224]{1,0:T(8,128)(2,1)S(1)}, bf16[32,4224]{1,0:T(8,128)(2,1)}, u32[]{:S(2)}, u32[]{:S(2)}) collective-permute-start(bf16[32,4224]{1,0:T(8,128)(2,1)S(1)} %collective-permute-done.8.refs_0_), channel_id=1, source_target_pairs={{0,78},{2,0},{4,2},{6,4},{8,6},{10,8},{12,10},{14,12},{64,14},{66,... | collective-permute-start | bytes 811016 | tf_op jit(solution)/shard_map/ppermute | solution.py:114
  81.1 13.1 %copy-start.8 = (s32[16,4]{1,0:T(8,128)S(1)}, s32[16,4]{1,0:T(8,128)}, u32[]{:S(2)}) copy-start(s32[16,4]{1,0:T(8,128)} %get-tuple-element.19) | copy-start | bytes 772
  81.1 13.2 %copy-start.7 = (s32[16,4]{1,0:T(8,128)S(1)}, s32[16,4]{1,0:T(8,128)}, u32[]{:S(2)}) copy-start(s32[16,4]{1,0:T(8,128)} %get-tuple-element.20) | copy-start | bytes 772
  81.1 26.8 %all-to-all-start.1 = ((bf16[16,8,4096]{2,1,0:T(8,128)(2,1)}), bf16[16,8,4096]{2,1,0:T(8,128)(2,1)}, u32[]{:S(2)}, u32[]{:S(2)}) async-start(bf16[16,8,4096]{2,1,0:T(8,128)(2,1)} %bitcast.12), calls=%async_computation.1 | async-start | bytes 2097152 | tf_op jit(solution)/shard_map/all_to_all | solution.py:127
  87.7 8.8 %collective-permute-start.11 = (bf16[32,4224]{1,0:T(8,128)(2,1)S(1)}, bf16[32,4224]{1,0:T(8,128)(2,1)}, u32[]{:S(2)}, u32[]{:S(2)}) collective-permute-start(bf16[32,4224]{1,0:T(8,128)(2,1)S(1)} %collective-permute-done.9.refs_1_), channel_id=1, source_target_pairs={{0,2},{2,4},{4,6},{6,8},{8,10},{10,12},{12,14},{14,64},{64,66},{66... | collective-permute-start | bytes 811016 | tf_op jit(solution)/shard_map/ppermute | solution.py:113
  89.9 8.7 %collective-permute-start.12 = (bf16[32,4224]{1,0:T(8,128)(2,1)}, bf16[32,4224]{1,0:T(8,128)(2,1)S(1)}, u32[]{:S(2)}, u32[]{:S(2)}) collective-permute-start(bf16[32,4224]{1,0:T(8,128)(2,1)} %collective-permute-done.10.refs_2_), channel_id=1, source_target_pairs={{0,78},{2,0},{4,2},{6,4},{8,6},{10,8},{12,10},{14,12},{64,14},{66,... | collective-permute-start | bytes 811016 | tf_op jit(solution)/shard_map/ppermute | solution.py:114
  96.5 18.4 %collective-permute-start.13 = (bf16[32,4224]{1,0:T(8,128)(2,1)}, bf16[32,4224]{1,0:T(8,128)(2,1)S(1)}, u32[]{:S(2)}, u32[]{:S(2)}) collective-permute-start(bf16[32,4224]{1,0:T(8,128)(2,1)} %collective-permute-done.11.refs_3_), channel_id=1, source_target_pairs={{0,2},{2,4},{4,6},{6,8},{8,10},{10,12},{12,14},{14,64},{64,66},{66... | collective-permute-start | bytes 811016 | tf_op jit(solution)/shard_map/ppermute | solution.py:113
  98.6 18.2 %collective-permute-start.14 = (bf16[32,4224]{1,0:T(8,128)(2,1)S(1)}, bf16[32,4224]{1,0:T(8,128)(2,1)S(1)}, u32[]{:S(2)}, u32[]{:S(2)}) collective-permute-start(bf16[32,4224]{1,0:T(8,128)(2,1)S(1)} %collective-permute-done.12.refs_0_), channel_id=1, source_target_pairs={{0,78},{2,0},{4,2},{6,4},{8,6},{10,8},{12,10},{14,12},{64,14},{66,... | collective-permute-start | bytes 811016 | tf_op jit(solution)/shard_map/ppermute | solution.py:114
  107.9 6.8 %copy-start.6 = (s32[16,4]{1,0:T(8,128)S(1)}, s32[16,4]{1,0:T(8,128)}, u32[]{:S(2)}) copy-start(s32[16,4]{1,0:T(8,128)} %get-tuple-element.22) | copy-start | bytes 772
  107.9 13.5 %copy-start.5 = (s32[16,4]{1,0:T(8,128)S(1)}, s32[16,4]{1,0:T(8,128)}, u32[]{:S(2)}) copy-start(s32[16,4]{1,0:T(8,128)} %get-tuple-element.23) | copy-start | bytes 772
  108.0 18.7 %all-to-all-start.2 = ((bf16[16,8,4096]{2,1,0:T(8,128)(2,1)}), bf16[16,8,4096]{2,1,0:T(8,128)(2,1)}, u32[]{:S(2)}, u32[]{:S(2)}) async-start(bf16[16,8,4096]{2,1,0:T(8,128)(2,1)} %bitcast.14), calls=%async_computation.2 | async-start | bytes 2097152 | tf_op jit(solution)/shard_map/all_to_all | solution.py:127
  114.9 7.0 %collective-permute-start.15 = (bf16[16,4224]{1,0:T(8,128)(2,1)S(1)}, bf16[16,4224]{1,0:T(8,128)(2,1)S(1)}, u32[]{:S(2)}, u32[]{:S(2)}) collective-permute-start(bf16[16,4224]{1,0:T(8,128)(2,1)S(1)} %slice.10), channel_id=1, source_target_pairs={{0,2},{2,4},{4,6},{6,8},{8,10},{10,12},{12,14},{14,64},{64,66},{66... | collective-permute-start | bytes 405512 | tf_op jit(solution)/shard_map/ppermute | solution.py:118
  116.9 7.0 %collective-permute-start.16 = (bf16[16,4224]{1,0:T(8,128)(2,1)S(1)}, bf16[16,4224]{1,0:T(8,128)(2,1)S(1)}, u32[]{:S(2)}, u32[]{:S(2)}) collective-permute-start(bf16[16,4224]{1,0:T(8,128)(2,1)S(1)} %slice.11), channel_id=1, source_target_pairs={{0,78},{2,0},{4,2},{6,4},{8,6},{10,8},{12,10},{14,12},{64,14},{66,... | collective-permute-start | bytes 405512 | tf_op jit(solution)/shard_map/ppermute | solution.py:119
  126.2 7.4 %copy-start.2 = (s32[16,4,2]{2,1,0:T(4,128)S(1)}, s32[16,4,2]{2,1,0:T(4,128)}, u32[]{:S(2)}) copy-start(s32[16,4,2]{2,1,0:T(4,128)} %iota_add_fusion.4) | copy-start | bytes 1540
  126.2 7.6 %copy-start.3 = (s32[16,4,2]{2,1,0:T(4,128)S(1)}, s32[16,4,2]{2,1,0:T(4,128)}, u32[]{:S(2)}) copy-start(s32[16,4,2]{2,1,0:T(4,128)} %iota_add_fusion.3) | copy-start | bytes 1540
  126.7 22.5 %all-to-all-start.3 = ((bf16[16,8,4096]{2,1,0:T(8,128)(2,1)}), bf16[16,8,4096]{2,1,0:T(8,128)(2,1)S(1)}, u32[]{:S(2)}, u32[]{:S(2)}) async-start(bf16[16,8,4096]{2,1,0:T(8,128)(2,1)} %bitcast.16), calls=%async_computation.3 | async-start | bytes 2097152 | tf_op jit(solution)/shard_map/all_to_all | solution.py:127
  134.5 42.4 %collective-permute-start.17 = (bf16[128,4096]{1,0:T(8,128)(2,1)}, bf16[128,4096]{1,0:T(8,128)(2,1)}, u32[]{:S(2)}, u32[]{:S(2)}) collective-permute-start(bf16[128,4096]{1,0:T(8,128)(2,1)} %bitcast.11), channel_id=1, source_target_pairs={{0,1},{1,0},{2,3},{3,2},{4,5},{5,4},{6,7},{7,6},{8,9},{9,8},{10,11... | collective-permute-start | bytes 3145736 | tf_op jit(solution)/shard_map/ppermute | solution.py:131
  144.8 34.8 %collective-permute-start.18 = (bf16[128,4096]{1,0:T(8,128)(2,1)}, bf16[128,4096]{1,0:T(8,128)(2,1)}, u32[]{:S(2)}, u32[]{:S(2)}) collective-permute-start(bf16[128,4096]{1,0:T(8,128)(2,1)} %bitcast.13), channel_id=1, source_target_pairs={{0,1},{1,0},{2,3},{3,2},{4,5},{5,4},{6,7},{7,6},{8,9},{9,8},{10,11... | collective-permute-start | bytes 3145736 | tf_op jit(solution)/shard_map/ppermute | solution.py:131
  146.7 35.6 %collective-permute-start.19 = (bf16[128,4096]{1,0:T(8,128)(2,1)}, bf16[128,4096]{1,0:T(8,128)(2,1)}, u32[]{:S(2)}, u32[]{:S(2)}) collective-permute-start(bf16[128,4096]{1,0:T(8,128)(2,1)} %bitcast.15), channel_id=1, source_target_pairs={{0,1},{1,0},{2,3},{3,2},{4,5},{5,4},{6,7},{7,6},{8,9},{9,8},{10,11... | collective-permute-start | bytes 3145736 | tf_op jit(solution)/shard_map/ppermute | solution.py:131
  149.2 35.8 %collective-permute-start.20 = (bf16[128,4096]{1,0:T(8,128)(2,1)S(1)}, bf16[128,4096]{1,0:T(8,128)(2,1)}, u32[]{:S(2)}, u32[]{:S(2)}) collective-permute-start(bf16[128,4096]{1,0:T(8,128)(2,1)S(1)} %bitcast.57), channel_id=1, source_target_pairs={{0,1},{1,0},{2,3},{3,2},{4,5},{5,4},{6,7},{7,6},{8,9},{9,8},{10,11... | collective-permute-start | bytes 3145736 | tf_op jit(solution)/shard_map/ppermute | solution.py:131
  166.6 3.5 %copy-start.1 = (bf16[288,4096]{1,0:T(8,128)(2,1)S(1)}, bf16[288,4096]{1,0:T(8,128)(2,1)}, u32[]{:S(2)}) copy-start(bf16[288,4096]{1,0:T(8,128)(2,1)} %reshape.404) | copy-start | bytes 7077892
  185.0 2.7 %copy-start.16 = (bf16[1,1024,288]{1,2,0:T(8,128)(2,1)S(1)}, bf16[1,1024,288]{1,2,0:T(8,128)(2,1)}, u32[]{:S(2)}) copy-start(bf16[1,1024,288]{1,2,0:T(8,128)(2,1)} %param.25) | copy-start | bytes 1769476
Sparse Core Ops, SparseCore 0:
  43.6 70.2 all-gather.1

commit v2 on v0

v2 whole, which is shorter than its diff:
```python
import jax
import jax.numpy as jnp
from jax import lax
from jax.experimental import pallas as pl
from jax.experimental.pallas import tpu as pltpu
from jax.sharding import Mesh, PartitionSpec as P

AXES = ("x", "zhi", "y", "zlo", "core")
SIZES = (4, 2, 4, 8, 2)
RING = ("zhi", "zlo", "core")
PLANE = ("x", "y")
CODE_LANES = 128
IMG = 32
SLOTS = 1024
STEPS = 8
NT = (((1,), (1,)), ((), ()))
TN = (((0,), (0,)), ((), ()))
VMEM = pl.BlockSpec(memory_space=pltpu.VMEM)
SMEM = pl.BlockSpec(memory_space=pltpu.SMEM)


def gelu_slope(value):
    return (
        0.5 * (1.0 + lax.erf(value * 0.7071067811865476))
        + value * jnp.exp(-0.5 * value * value) * 0.3989422804014327
    )


def params(mib):
    return pltpu.CompilerParams(vmem_limit_bytes=mib * 1024 * 1024)


def pick_kernel(positions_ref, owners_ref, hidden_ref, out_ref):
    step = pl.program_id(0)
    row = lax.broadcasted_iota(jnp.int32, (IMG, IMG), 0)
    lane = lax.broadcasted_iota(jnp.int32, (IMG, IMG), 1)

    def column(ref):
        spread = jnp.broadcast_to(ref[...], (IMG, IMG))
        return spread, jnp.sum(jnp.where(row == lane, spread, 0), axis=1, keepdims=True)

    _, at = column(positions_ref)
    token = lax.broadcasted_iota(jnp.int32, (IMG, hidden_ref.shape[0]), 1)
    pick = jnp.where(token == at, 1.0, 0.0).astype(jnp.bfloat16)
    picked = jnp.dot(pick, hidden_ref[...], preferred_element_type=jnp.float32).astype(
        jnp.bfloat16
    )
    x, zhi = step // 2, step % 2
    for y in range(4):
        start = pl.multiple_of((x * 8 + y * 2 + zhi) * 128, 128)
        out_ref[:, pl.ds(start, 128)] = picked[:, y * 128 : (y + 1) * 128]

    @pl.when(step == 0)
    def _():
        spread, owner = column(owners_ref)
        same = jnp.where((spread == owner) & (lane < row), 1, 0)
        code = owner * 2 + jnp.sum(same, axis=1, keepdims=True)
        width = out_ref.shape[1] - CODE_LANES
        out_ref[:, width:] = jnp.broadcast_to(
            code.astype(jnp.float32), (IMG, CODE_LANES)
        ).astype(jnp.bfloat16)


def pick(grad_hidden, positions, owner_ids):
    tokens, width = grad_hidden.shape
    return pl.pallas_call(
        pick_kernel,
        grid=(8,),
        out_shape=jax.ShapeDtypeStruct((IMG, width + CODE_LANES), jnp.bfloat16),
        in_specs=[
            pl.BlockSpec((1, IMG), lambda i: (0, 0)),
            pl.BlockSpec((1, IMG), lambda i: (0, 0)),
            pl.BlockSpec((tokens, width // 8), lambda i: (0, i)),
        ],
        out_specs=pl.BlockSpec((IMG, width + CODE_LANES), lambda i: (0, 0)),
        compiler_params=params(8),
        cost_estimate=pl.CostEstimate(
            flops=2 * IMG * tokens * width, bytes_accessed=2 * tokens * width, transcendentals=0
        ),
    )(positions.reshape(1, IMG), owner_ids.reshape(1, IMG), grad_hidden)


def dispatch_kernel(zhi_ref, *refs):
    chunks, out_ref = refs[:-1], refs[-1]
    count = len(chunks)
    total, width = out_ref.shape
    target = lax.broadcasted_iota(jnp.int32, (IMG, total), 1)
    rank = target % 2
    member = (target // 2) % count
    plane = target // (2 * count)
    wanted = (((plane // 4) * 8 + zhi_ref[0] * 4 + plane % 4) * 2 + rank).astype(jnp.float32)
    picks = []
    for at, chunk in enumerate(chunks):
        code = chunk[:, width : width + 1].astype(jnp.float32)
        chosen = jnp.where((code == wanted) & (member == at), 1.0, 0.0)
        picks.append(chosen.astype(jnp.bfloat16))
    for start in range(0, width, 512):
        acc = None
        for chosen, chunk in zip(picks, chunks):
            part = lax.dot_general(
                chosen, chunk[:, start : start + 512], TN, preferred_element_type=jnp.float32
            )
            acc = part if acc is None else acc + part
        out_ref[:, start : start + 512] = acc.astype(out_ref.dtype)


def dispatch(chunks, zhi, width):
    total = IMG * len(chunks)
    return pl.pallas_call(
        dispatch_kernel,
        out_shape=jax.ShapeDtypeStruct((total, width), jnp.bfloat16),
        in_specs=[SMEM] + [VMEM] * len(chunks),
        out_specs=VMEM,
        compiler_params=params(8),
        cost_estimate=pl.CostEstimate(
            flops=2 * IMG * total * width * len(chunks),
            bytes_accessed=4 * total * width,
            transcendentals=0,
        ),
    )(zhi, *chunks)


def slope_kernel(place_ref, pre_ref, slope_ref, place_out):
    z, core = place_ref[0], place_ref[1]
    at = lax.broadcasted_iota(jnp.int32, (SLOTS, 1), 0)
    rank = at & 1
    chunk = ((at >> 7) & 3) * 4 + ((at >> 1) & 3)
    y = (at >> 3) & 3
    x = (at >> 5) & 3
    gatherer = jnp.where(at >= SLOTS // 2, 1 - core, core)
    distance = (chunk + 1) >> 1
    source = (z + 16 + jnp.where(gatherer == 0, -distance, distance)) & 15
    kept = (chunk == 0) | ((chunk & 1) == 1)
    from_core = jnp.where(kept, gatherer, 1 - gatherer)
    tensor = (source & 7) * 2 + from_core
    slot = (tensor * 32 + x * 8 + (source >> 3) * 4 + y) * 2 + rank
    final = lax.broadcasted_iota(jnp.int32, (SLOTS, SLOTS), 1)
    place = jnp.where(slot == final, 1.0, 0.0).astype(jnp.bfloat16)
    place_out[...] = place
    values = lax.dot_general(pre_ref[...], place, NT, preferred_element_type=jnp.float32)
    slope_ref[...] = gelu_slope(values)


def slopes(z, core, pre):
    return pl.pallas_call(
        slope_kernel,
        out_shape=(
            jax.ShapeDtypeStruct(pre.shape, jnp.float32),
            jax.ShapeDtypeStruct((SLOTS, SLOTS), jnp.bfloat16),
        ),
        in_specs=[SMEM, VMEM],
        out_specs=(VMEM, VMEM),
        compiler_params=params(24),
        cost_estimate=pl.CostEstimate(
            flops=2 * pre.shape[0] * SLOTS * SLOTS,
            bytes_accessed=4 * SLOTS * SLOTS,
            transcendentals=2 * pre.shape[0] * SLOTS,
        ),
    )(jnp.stack([z, core]).astype(jnp.int32), pre)


def project_kernel(weights_ref, *refs):
    parts, out_ref = refs[:-1], refs[-1]
    start = 0
    for part in parts:
        size = part.shape[0]
        out_ref[:, start : start + size] = lax.dot_general(
            weights_ref[...], part[...], NT, preferred_element_type=jnp.float32
        )
        start += size


def project(weights, parts):
    hidden, width = weights.shape
    total = sum(part.shape[0] for part in parts)
    return pl.pallas_call(
        project_kernel,
        out_shape=jax.ShapeDtypeStruct((hidden, total), jnp.float32),
        in_specs=[VMEM] * (1 + len(parts)),
        out_specs=VMEM,
        compiler_params=params(24),
        cost_estimate=pl.CostEstimate(
            flops=2 * hidden * width * total, bytes_accessed=2 * width * total, transcendentals=0
        ),
    )(weights, *parts)


def finish_kernel(weights_ref, part_ref, early_ref, slope_ref, place_ref, out_ref):
    early = early_ref.shape[1]
    last = lax.dot_general(
        weights_ref[...], part_ref[...], NT, preferred_element_type=jnp.float32
    )
    first = (slope_ref[:, :early] * early_ref[...]).astype(jnp.bfloat16)
    last = (slope_ref[:, early:] * last).astype(jnp.bfloat16)
    placed = jnp.dot(first, place_ref[:early], preferred_element_type=jnp.float32)
    placed += jnp.dot(last, place_ref[early:], preferred_element_type=jnp.float32)
    out_ref[...] = placed.astype(out_ref.dtype)


def finish(weights, part, early, slope, place):
    hidden, width = weights.shape
    return pl.pallas_call(
        finish_kernel,
        out_shape=jax.ShapeDtypeStruct((hidden, SLOTS), jnp.bfloat16),
        in_specs=[VMEM] * 5,
        out_specs=VMEM,
        compiler_params=params(24),
        cost_estimate=pl.CostEstimate(
            flops=2 * hidden * (width * part.shape[0] + SLOTS * SLOTS),
            bytes_accessed=2 * SLOTS * SLOTS,
            transcendentals=0,
        ),
    )(weights, part, early, slope, place)


def ring_pairs(other_core):
    pairs = []
    for z in range(16):
        for core in range(2):
            below = (z + (-1 if core == 0 else 1)) % 16
            sender = 1 - core if other_core else core
            pairs.append((below * 2 + sender, z * 2 + core))
    return pairs


def shards(grad_hidden, positions, owner_ids, w_proj, pre_act):
    zhi, zlo, core = (lax.axis_index(name) for name in ("zhi", "zlo", "core"))
    width = grad_hidden.shape[1]
    zhi_at = jnp.reshape(zhi, (1,)).astype(jnp.int32)
    swap = [(0, 1), (1, 0)]

    packed = pick(grad_hidden, positions, owner_ids)

    kept, crossed = [packed], [packed]
    for step in range(1, STEPS + 1):
        kept.append(lax.ppermute(kept[-1], RING, ring_pairs(False)))
        if step < STEPS:
            crossed.append(lax.ppermute(crossed[-1], RING, ring_pairs(step == 1)))
    chunks = [packed]
    for step in range(1, STEPS + 1):
        chunks.append(kept[step])
        if step < STEPS:
            chunks.append(crossed[step])

    other = lax.ppermute(w_proj, "zhi", swap)
    both = jnp.concatenate(
        [jnp.where(zhi == 0, w_proj, other), jnp.where(zhi == 0, other, w_proj)], axis=1
    )
    weights = lax.all_gather(both, PLANE, axis=1, tiled=True)

    slope, place = slopes(zhi * 8 + zlo, core, pre_act[0].T)

    own, peer = [], []
    for group in range(4):
        if group == 2:
            zhi_at, slope, place = lax.optimization_barrier((zhi_at, slope, place))
        outgoing = dispatch(chunks[4 * group : 4 * group + 4], zhi_at, width)
        received = lax.all_to_all(
            outgoing.reshape(16, 8, width), PLANE, split_axis=0, concat_axis=0, tiled=True
        ).reshape(4 * IMG, width)
        own.append(received)
        peer.append(lax.ppermute(received, "core", swap))

    early = project(weights, own + peer[:3])
    gradient = finish(weights, peer[3], early, slope, place)
    return gradient.T[None]


def solution(mesh):
    fine = Mesh(mesh.devices.reshape(SIZES), AXES)
    return jax.shard_map(
        shards,
        mesh=fine,
        in_specs=(
            P(AXES, None),
            P(AXES),
            P(AXES, None),
            P(("zlo", "core"), ("x", "zhi", "y")),
            P(("x", "zhi", "y"), None, ("zlo", "core")),
        ),
        out_specs=P(("x", "zhi", "y"), None, ("zlo", "core")),
        check_vma=False,
    )
```

time: 298 us -> 186 us (0.62)
  waiting for transfers between devices: 229 us -> 17.3 us
  starting transfers between devices: 0.04 us -> 117 us
  blocking collectives: 40 us -> 0 us
  Pallas kernels: 0 us -> 26.4 us
  matrix products: 8.15 us -> 0 us
  local copies, waits for them, and re-layouts: 2.05 us -> 9.71 us
    all_gather x2 -> x1, waiting for transfers between devices: 229 us -> 0.02 us  [shards(): weights = lax.all_gather(both, PLANE, axis=1, tiled=True)]
    ppermute x0 -> x20, starting transfers between devices: none -> 90.2 us  [the longest x8 31.4 us: shards(): kept.append(lax.ppermute(kept[-1], RING, ring_pairs(False)))]
    all_to_all x1 -> x0, blocking collectives: 40 us -> none  [shards(): lax.all_to_all(outgoing, 'dp', split_axis=0, concat_axis=0, tiled=True)]
    pallas_call x0 -> x8, Pallas kernels: none -> 26.4 us  [the longest x4 10.5 us: dispatch(): pl.pallas_call(dispatch_kernel, out_shape=jax.ShapeDtypeStruct((total, wi...]
    all_to_all x0 -> x4, starting transfers between devices: none -> 26.4 us  [shards(): lax.all_to_all(outgoing.reshape(16, 8, width), PLANE, split_axis=0, conca...]
    ppermute x0 -> x20, waiting for transfers between devices: none -> 17.2 us  [the longest x8 9.53 us: shards(): kept.append(lax.ppermute(kept[-1], RING, ring_pairs(False)))]
    unnamed x8 -> x24, local copies, waits for them, and re-layouts: 0.02 us -> 9.71 us
    dot_general x2 -> x0, matrix products: 8.15 us -> none  [the longest x1 7.81 us: shards(): lax.dot_general(lax.all_gather(received, 'tensor', axis=0, tiled=True), w...]
  transfers between devices with their start and end apart: 2 -> 25, of which waited for: 2 -> 9; matrix products, arithmetic and copies ran while one was open for 1% -> 0% of each run, Pallas kernels for 0% -> 11%
where the time goes in v2:
time: 186 us; the launch traced here: 185 us
  starting transfers between devices  117 us (63%)
  Pallas kernels  26.4 us (14%)
  waiting for transfers between devices  17.3 us (9%)
  between operations  13.8 us (7%)
  local copies, waits for them, and re-layouts  9.71 us (5%)
    ppermute x8, starting transfers between devices, shards(): kept.append(lax.ppermute(kept[-1], RING, ring_pairs(False)))  31.4 us
    all_to_all x4, starting transfers between devices, shards(): lax.all_to_all(outgoing.reshape(16, 8, width), PLANE, split_axis=0, conca...  26.4 us
    ppermute x7, starting transfers between devices, shards(): crossed.append(lax.ppermute(crossed[-1], RING, ring_pairs(step == 1)))  26.3 us
    ppermute x4, starting transfers between devices, shards(): peer.append(lax.ppermute(received, 'core', swap))  26.2 us
    pallas_call x4, Pallas kernels, dispatch(): pl.pallas_call(dispatch_kernel, out_shape=jax.ShapeDtypeStruct((total, wi...  10.5 us
    unnamed x24, local copies, waits for them, and re-layouts  9.71 us
    ppermute x8, waiting for transfers between devices, shards(): kept.append(lax.ppermute(kept[-1], RING, ring_pairs(False)))  9.53 us
    ppermute x7, waiting for transfers between devices, shards(): crossed.append(lax.ppermute(crossed[-1], RING, ring_pairs(step == 1)))  7.61 us
  transfers between devices with their start and end apart: 25, of which 9 were waited for; matrix products, arithmetic and copies ran while one was open for 0% of the time, Pallas kernels for 11%

profile of v2, /device:TPU:1, one launch (start us, length us, event | category | flops | bytes accessed | tf_op | source)
XLA Modules:
  0.0 184.6 jit_solution(5293141707681197969)
XLA Ops:
  6.5 1.6 copy-done.1
  8.1 0.7 copy-done.8
  9.4 1.9 %shard_map.56.refs_0_ = bf16[32,4224]{1,0:T(8,128)(2,1)S(1)} custom-call(s32[1,32]{1,0:T(1,128)S(1)} %bitcast.25, s32[1,32]{1,0:T(1,128)S(1)} %bitcast.26, bf16[256,4096]{1,0:T(8,128)(2,1)S(1)} %copy-done.1), custom_call_target="tpu_custom_call" | custom-call | flops 67108864 | bytes 2097152 | tf_op jit(solution)/shard_map/pallas_call | solution.py:66
  11.4 12.0 %collective-permute-start.7 = (bf16[32,4224]{1,0:T(8,128)(2,1)S(1)}, bf16[32,4224]{1,0:T(8,128)(2,1)S(1)}, u32[]{:S(2)}, u32[]{:S(2)}) collective-permute-start(bf16[32,4224]{1,0:T(8,128)(2,1)S(1)} %shard_map.56.refs_0_), channel_id=1, source_target_pairs={{78,0},{3,1},{0,2},{5,3},{2,4},{7,5},{4,6},{9,7},{6,8},{11,9},{8,1... | collective-permute-start | bytes 811016 | tf_op jit(solution)/shard_map/ppermute | solution.py:236
  23.3 1.9 %collective-permute-start.1 = (bf16[32,4224]{1,0:T(8,128)(2,1)S(1)}, bf16[32,4224]{1,0:T(8,128)(2,1)S(1)}, u32[]{:S(2)}, u32[]{:S(2)}) collective-permute-start(bf16[32,4224]{1,0:T(8,128)(2,1)S(1)} %shard_map.56.refs_0_), channel_id=1, source_target_pairs={{79,0},{2,1},{1,2},{4,3},{3,4},{6,5},{5,6},{8,7},{7,8},{10,9},{9,1... | collective-permute-start | bytes 811016 | tf_op jit(solution)/shard_map/ppermute | solution.py:238
  25.3 1.5 collective-permute-done.7.refs_1_
  26.7 5.0 %collective-permute-start.8 = (bf16[32,4224]{1,0:T(8,128)(2,1)S(1)}, bf16[32,4224]{1,0:T(8,128)(2,1)S(1)}, u32[]{:S(2)}, u32[]{:S(2)}) collective-permute-start(bf16[32,4224]{1,0:T(8,128)(2,1)S(1)} %collective-permute-done.7.refs_1_), channel_id=1, source_target_pairs={{78,0},{3,1},{0,2},{5,3},{2,4},{7,5},{4,6},{9,7},{6,8},{11,9},{8,1... | collective-permute-start | bytes 811016 | tf_op jit(solution)/shard_map/ppermute | solution.py:236
  31.7 6.2 %collective-permute-start = (bf16[288,128]{1,0:T(8,128)(2,1)S(1)}, bf16[288,128]{1,0:T(8,128)(2,1)S(1)}, u32[]{:S(2)}, u32[]{:S(2)}) collective-permute-start(bf16[288,128]{1,0:T(8,128)(2,1)S(1)} %copy-done.11), channel_id=1, source_target_pairs={{0,64},{64,0},{1,65},{65,1},{2,66},{66,2},{3,67},{67,3},{4,68},{68... | collective-permute-start | bytes 221192 | tf_op jit(solution)/shard_map/ppermute | solution.py:245
  38.0 2.3 %shard_map.58 = bf16[128,4096]{1,0:T(8,128)(2,1)} custom-call(s32[1]{0:T(128)} %bitcast.zhi_ref, bf16[32,4224]{1,0:T(8,128)(2,1)S(1)} %shard_map.56.refs_0_, bf16[32,4224]{1,0:T(8,128)(2,1)S(1)} %collective-permute-done.7.refs_1_, bf16[32,4224]{1,0:T(8,128)(2,1)S(1)} %collective-permute-done.1.refs_2_, bf16[32,4224]{1,0:T(8,128)(2,1)S(1)} %collective-permute-done.8.refs_3_), custom_call_target="tpu_custom_call" | custom-call | flops 134217728 | bytes 2097152 | tf_op jit(solution)/shard_map/pallas_call | solution.py:109
  40.4 6.8 %all-to-all-start.1 = ((bf16[16,8,4096]{2,1,0:T(8,128)(2,1)}), bf16[16,8,4096]{2,1,0:T(8,128)(2,1)S(1)}, u32[]{:S(2)}, u32[]{:S(2)}) async-start(bf16[16,8,4096]{2,1,0:T(8,128)(2,1)} %bitcast.9), calls=%async_computation.1 | async-start | bytes 2097152 | tf_op jit(solution)/shard_map/all_to_all | solution.py:258
  47.3 0.7 pad_maximum_fusion
  47.9 3.9 %collective-permute-start.2 = (bf16[32,4224]{1,0:T(8,128)(2,1)S(1)}, bf16[32,4224]{1,0:T(8,128)(2,1)S(1)}, u32[]{:S(2)}, u32[]{:S(2)}) collective-permute-start(bf16[32,4224]{1,0:T(8,128)(2,1)S(1)} %collective-permute-done.1.refs_2_), channel_id=1, source_target_pairs={{78,0},{3,1},{0,2},{5,3},{2,4},{7,5},{4,6},{9,7},{6,8},{11,9},{8,1... | collective-permute-start | bytes 811016 | tf_op jit(solution)/shard_map/ppermute | solution.py:238
  51.8 1.9 %collective-permute-start.9 = (bf16[32,4224]{1,0:T(8,128)(2,1)S(1)}, bf16[32,4224]{1,0:T(8,128)(2,1)S(1)}, u32[]{:S(2)}, u32[]{:S(2)}) collective-permute-start(bf16[32,4224]{1,0:T(8,128)(2,1)S(1)} %collective-permute-done.8.refs_3_), channel_id=1, source_target_pairs={{78,0},{3,1},{0,2},{5,3},{2,4},{7,5},{4,6},{9,7},{6,8},{11,9},{8,1... | collective-permute-start | bytes 811016 | tf_op jit(solution)/shard_map/ppermute | solution.py:236
  53.8 1.7 collective-permute-done.2.refs_0_
  55.4 5.1 %collective-permute-start.3 = (bf16[32,4224]{1,0:T(8,128)(2,1)S(1)}, bf16[32,4224]{1,0:T(8,128)(2,1)S(1)}, u32[]{:S(2)}, u32[]{:S(2)}) collective-permute-start(bf16[32,4224]{1,0:T(8,128)(2,1)S(1)} %collective-permute-done.2.refs_0_), channel_id=1, source_target_pairs={{78,0},{3,1},{0,2},{5,3},{2,4},{7,5},{4,6},{9,7},{6,8},{11,9},{8,1... | collective-permute-start | bytes 811016 | tf_op jit(solution)/shard_map/ppermute | solution.py:238
  60.5 2.9 %collective-permute-start.10 = (bf16[32,4224]{1,0:T(8,128)(2,1)S(1)}, bf16[32,4224]{1,0:T(8,128)(2,1)S(1)}, u32[]{:S(2)}, u32[]{:S(2)}) collective-permute-start(bf16[32,4224]{1,0:T(8,128)(2,1)S(1)} %collective-permute-done.9.refs_1_), channel_id=1, source_target_pairs={{78,0},{3,1},{0,2},{5,3},{2,4},{7,5},{4,6},{9,7},{6,8},{11,9},{8,1... | collective-permute-start | bytes 811016 | tf_op jit(solution)/shard_map/ppermute | solution.py:236
  63.9 4.1 %collective-permute-done.10.refs_3_ = bf16[32,4224]{1,0:T(8,128)(2,1)S(1)} collective-permute-done((bf16[32,4224]{1,0:T(8,128)(2,1)S(1)}, bf16[32,4224]{1,0:T(8,128)(2,1)S(1)}, u32[]{:S(2)}, u32[]{:S(2)}) %collective-permute-start.10) | collective-permute-done | bytes 270368 | tf_op jit(solution)/shard_map/ppermute | solution.py:236
  68.0 2.3 %shard_map.59 = bf16[128,4096]{1,0:T(8,128)(2,1)} custom-call(s32[1]{0:T(128)} %bitcast.zhi_ref, bf16[32,4224]{1,0:T(8,128)(2,1)S(1)} %collective-permute-done.2.refs_0_, bf16[32,4224]{1,0:T(8,128)(2,1)S(1)} %collective-permute-done.9.refs_1_, bf16[32,4224]{1,0:T(8,128)(2,1)S(1)} %collective-permute-done.3.refs_2_, ...), custom_call_target="tpu_custom_call" | custom-call | flops 134217728 | bytes 2097152 | tf_op jit(solution)/shard_map/pallas_call | solution.py:109
  70.4 6.8 %all-to-all-start.2 = ((bf16[16,8,4096]{2,1,0:T(8,128)(2,1)}), bf16[16,8,4096]{2,1,0:T(8,128)(2,1)S(1)}, u32[]{:S(2)}, u32[]{:S(2)}) async-start(bf16[16,8,4096]{2,1,0:T(8,128)(2,1)} %bitcast.11), calls=%async_computation.2 | async-start | bytes 2097152 | tf_op jit(solution)/shard_map/all_to_all | solution.py:258
  77.2 3.8 %collective-permute-start.4 = (bf16[32,4224]{1,0:T(8,128)(2,1)S(1)}, bf16[32,4224]{1,0:T(8,128)(2,1)}, u32[]{:S(2)}, u32[]{:S(2)}) collective-permute-start(bf16[32,4224]{1,0:T(8,128)(2,1)S(1)} %collective-permute-done.3.refs_2_), channel_id=1, source_target_pairs={{78,0},{3,1},{0,2},{5,3},{2,4},{7,5},{4,6},{9,7},{6,8},{11,9},{8,1... | collective-permute-start | bytes 811016 | tf_op jit(solution)/shard_map/ppermute | solution.py:238
  81.0 1.9 %collective-permute-start.11 = (bf16[32,4224]{1,0:T(8,128)(2,1)S(1)}, bf16[32,4224]{1,0:T(8,128)(2,1)}, u32[]{:S(2)}, u32[]{:S(2)}) collective-permute-start(bf16[32,4224]{1,0:T(8,128)(2,1)S(1)} %collective-permute-done.10.refs_3_), channel_id=1, source_target_pairs={{78,0},{3,1},{0,2},{5,3},{2,4},{7,5},{4,6},{9,7},{6,8},{11,9},{8,1... | collective-permute-start | bytes 811016 | tf_op jit(solution)/shard_map/ppermute | solution.py:236
  82.9 1.6 collective-permute-done.4.refs_0_
  84.5 5.0 %collective-permute-start.5 = (bf16[32,4224]{1,0:T(8,128)(2,1)}, bf16[32,4224]{1,0:T(8,128)(2,1)S(1)}, u32[]{:S(2)}, u32[]{:S(2)}) collective-permute-start(bf16[32,4224]{1,0:T(8,128)(2,1)} %collective-permute-done.4.refs_0_), channel_id=1, source_target_pairs={{78,0},{3,1},{0,2},{5,3},{2,4},{7,5},{4,6},{9,7},{6,8},{11,9},{8,1... | collective-permute-start | bytes 811016 | tf_op jit(solution)/shard_map/ppermute | solution.py:238
  89.5 3.1 %collective-permute-start.12 = (bf16[32,4224]{1,0:T(8,128)(2,1)}, bf16[32,4224]{1,0:T(8,128)(2,1)S(1)}, u32[]{:S(2)}, u32[]{:S(2)}) collective-permute-start(bf16[32,4224]{1,0:T(8,128)(2,1)} %collective-permute-done.11.refs_1_), channel_id=1, source_target_pairs={{78,0},{3,1},{0,2},{5,3},{2,4},{7,5},{4,6},{9,7},{6,8},{11,9},{8,1... | collective-permute-start | bytes 811016 | tf_op jit(solution)/shard_map/ppermute | solution.py:236
  92.6 1.1 copy-done.10
  93.7 2.5 %shard_map.55 = (f32[288,1024]{1,0:T(8,128)S(1)}, bf16[1024,1024]{1,0:T(8,128)(2,1)S(1)}) custom-call(s32[2]{0:T(128)S(1)} %pad_add_fusion.place_ref, bf16[288,1024]{1,0:T(8,128)(2,1)S(1)} %bitcast.27), custom_call_target="tpu_custom_call" | custom-call | flops 603979776 | bytes 4194304 | tf_op jit(solution)/shard_map/pallas_call | solution.py:145
  96.2 1.4 copy-done.2
  97.6 1.1 copy-done.4
  98.6 0.7 copy-done.6
  99.3 1.0 copy-done.7
  100.3 3.4 %shard_map.60 = bf16[128,4096]{1,0:T(8,128)(2,1)} custom-call(s32[1]{0:T(128)} %bitcast.zhi_ref, bf16[32,4224]{1,0:T(8,128)(2,1)} %collective-permute-done.4.refs_0_, bf16[32,4224]{1,0:T(8,128)(2,1)} %collective-permute-done.11.refs_1_, bf16[32,4224]{1,0:T(8,128)(2,1)S(1)} %collective-permute-done.5.refs_2_, bf16[32,4224]{1,0:T(8,128)(2,1)S(1)} %copy-done.7), custom_call_target="tpu_custom_call" | custom-call | flops 134217728 | bytes 2097152 | tf_op jit(solution)/shard_map/pallas_call | solution.py:109
  103.7 6.5 %all-to-all-start.3 = ((bf16[16,8,4096]{2,1,0:T(8,128)(2,1)}), bf16[16,8,4096]{2,1,0:T(8,128)(2,1)S(1)}, u32[]{:S(2)}, u32[]{:S(2)}) async-start(bf16[16,8,4096]{2,1,0:T(8,128)(2,1)} %bitcast.13), calls=%async_computation.3 | async-start | bytes 2097152 | tf_op jit(solution)/shard_map/all_to_all | solution.py:258
  110.2 2.7 %collective-permute-start.6 = (bf16[32,4224]{1,0:T(8,128)(2,1)S(1)}, bf16[32,4224]{1,0:T(8,128)(2,1)S(1)}, u32[]{:S(2)}, u32[]{:S(2)}) collective-permute-start(bf16[32,4224]{1,0:T(8,128)(2,1)S(1)} %collective-permute-done.5.refs_2_), channel_id=1, source_target_pairs={{78,0},{3,1},{0,2},{5,3},{2,4},{7,5},{4,6},{9,7},{6,8},{11,9},{8,1... | collective-permute-start | bytes 811016 | tf_op jit(solution)/shard_map/ppermute | solution.py:238
  112.9 1.9 %collective-permute-start.13 = (bf16[32,4224]{1,0:T(8,128)(2,1)}, bf16[32,4224]{1,0:T(8,128)(2,1)S(1)}, u32[]{:S(2)}, u32[]{:S(2)}) collective-permute-start(bf16[32,4224]{1,0:T(8,128)(2,1)} %copy-done.6), channel_id=1, source_target_pairs={{78,0},{3,1},{0,2},{5,3},{2,4},{7,5},{4,6},{9,7},{6,8},{11,9},{8,1... | collective-permute-start | bytes 811016 | tf_op jit(solution)/shard_map/ppermute | solution.py:236
  114.9 3.0 %collective-permute-done.6.refs_0_ = bf16[32,4224]{1,0:T(8,128)(2,1)S(1)} collective-permute-done((bf16[32,4224]{1,0:T(8,128)(2,1)S(1)}, bf16[32,4224]{1,0:T(8,128)(2,1)S(1)}, u32[]{:S(2)}, u32[]{:S(2)}) %collective-permute-start.6) | collective-permute-done | bytes 270368 | tf_op jit(solution)/shard_map/ppermute | solution.py:238
  117.8 3.9 %collective-permute-start.14 = (bf16[32,4224]{1,0:T(8,128)(2,1)S(1)}, bf16[32,4224]{1,0:T(8,128)(2,1)S(1)}, u32[]{:S(2)}, u32[]{:S(2)}) collective-permute-start(bf16[32,4224]{1,0:T(8,128)(2,1)S(1)} %collective-permute-done.6.refs_0_), channel_id=1, source_target_pairs={{78,0},{3,1},{0,2},{5,3},{2,4},{7,5},{4,6},{9,7},{6,8},{11,9},{8,1... | collective-permute-start | bytes 811016 | tf_op jit(solution)/shard_map/ppermute | solution.py:238
  121.7 2.8 %collective-permute-start.15 = (bf16[32,4224]{1,0:T(8,128)(2,1)S(1)}, bf16[32,4224]{1,0:T(8,128)(2,1)S(1)}, u32[]{:S(2)}, u32[]{:S(2)}) collective-permute-start(bf16[32,4224]{1,0:T(8,128)(2,1)S(1)} %collective-permute-done.13.refs_1_), channel_id=1, source_target_pairs={{78,0},{3,1},{0,2},{5,3},{2,4},{7,5},{4,6},{9,7},{6,8},{11,9},{8,1... | collective-permute-start | bytes 811016 | tf_op jit(solution)/shard_map/ppermute | solution.py:236
  124.5 0.9 collective-permute-done.14.refs_2_
  125.4 3.9 %collective-permute-done.15.refs_3_ = bf16[32,4224]{1,0:T(8,128)(2,1)S(1)} collective-permute-done((bf16[32,4224]{1,0:T(8,128)(2,1)S(1)}, bf16[32,4224]{1,0:T(8,128)(2,1)S(1)}, u32[]{:S(2)}, u32[]{:S(2)}) %collective-permute-start.15) | collective-permute-done | bytes 270368 | tf_op jit(solution)/shard_map/ppermute | solution.py:236
  129.3 2.4 %shard_map.57 = bf16[128,4096]{1,0:T(8,128)(2,1)} custom-call(s32[1]{0:T(128)} %bitcast.zhi_ref, bf16[32,4224]{1,0:T(8,128)(2,1)S(1)} %collective-permute-done.6.refs_0_, bf16[32,4224]{1,0:T(8,128)(2,1)S(1)} %collective-permute-done.13.refs_1_, bf16[32,4224]{1,0:T(8,128)(2,1)S(1)} %collective-permute-done.14.refs_2_, ...), custom_call_target="tpu_custom_call" | custom-call | flops 134217728 | bytes 2097152 | tf_op jit(solution)/shard_map/pallas_call | solution.py:109
  131.7 6.4 %all-to-all-start = ((bf16[16,8,4096]{2,1,0:T(8,128)(2,1)}), bf16[16,8,4096]{2,1,0:T(8,128)(2,1)}, u32[]{:S(2)}, u32[]{:S(2)}) async-start(bf16[16,8,4096]{2,1,0:T(8,128)(2,1)} %bitcast.7), calls=%async_computation | async-start | bytes 2097152 | tf_op jit(solution)/shard_map/all_to_all | solution.py:258
  138.1 13.1 %collective-permute-start.17 = (bf16[128,4096]{1,0:T(8,128)(2,1)S(1)}, bf16[128,4096]{1,0:T(8,128)(2,1)}, u32[]{:S(2)}, u32[]{:S(2)}) collective-permute-start(bf16[128,4096]{1,0:T(8,128)(2,1)S(1)} %bitcast.19), channel_id=1, source_target_pairs={{0,1},{1,0},{2,3},{3,2},{4,5},{5,4},{6,7},{7,6},{8,9},{9,8},{10,11... | collective-permute-start | bytes 3145736 | tf_op jit(solution)/shard_map/ppermute | solution.py:262
  151.2 1.9 %collective-permute-start.18 = (bf16[128,4096]{1,0:T(8,128)(2,1)S(1)}, bf16[128,4096]{1,0:T(8,128)(2,1)}, u32[]{:S(2)}, u32[]{:S(2)}) collective-permute-start(bf16[128,4096]{1,0:T(8,128)(2,1)S(1)} %bitcast.21), channel_id=1, source_target_pairs={{0,1},{1,0},{2,3},{3,2},{4,5},{5,4},{6,7},{7,6},{8,9},{9,8},{10,11... | collective-permute-start | bytes 3145736 | tf_op jit(solution)/shard_map/ppermute | solution.py:262
  153.2 2.4 %collective-permute-start.19 = (bf16[128,4096]{1,0:T(8,128)(2,1)S(1)}, bf16[128,4096]{1,0:T(8,128)(2,1)}, u32[]{:S(2)}, u32[]{:S(2)}) collective-permute-start(bf16[128,4096]{1,0:T(8,128)(2,1)S(1)} %bitcast.23), channel_id=1, source_target_pairs={{0,1},{1,0},{2,3},{3,2},{4,5},{5,4},{6,7},{7,6},{8,9},{9,8},{10,11... | collective-permute-start | bytes 3145736 | tf_op jit(solution)/shard_map/ppermute | solution.py:262
  155.6 8.8 %collective-permute-start.16 = (bf16[128,4096]{1,0:T(8,128)(2,1)}, bf16[128,4096]{1,0:T(8,128)(2,1)}, u32[]{:S(2)}, u32[]{:S(2)}) collective-permute-start(bf16[128,4096]{1,0:T(8,128)(2,1)} %bitcast.8.refs_3_), channel_id=1, source_target_pairs={{0,1},{1,0},{2,3},{3,2},{4,5},{5,4},{6,7},{7,6},{8,9},{9,8},{10,11... | collective-permute-start | bytes 3145736 | tf_op jit(solution)/shard_map/ppermute | solution.py:262
  164.4 1.7 copy-done
  166.1 6.7 %shard_map.61.early_ref = f32[288,896]{1,0:T(8,128)S(1)} custom-call(bf16[288,4096]{1,0:T(8,128)(2,1)S(1)} %copy-done, bf16[128,4096]{1,0:T(8,128)(2,1)S(1)} %bitcast.20, bf16[128,4096]{1,0:T(8,128)(2,1)S(1)} %bitcast.22, bf16[128,4096]{1,0:T(8,128)(2,1)S(1)} %bitcast.24, bf16[128,4096]{1,0:T(8,128)(2,1)} %bitcast.8.refs_3_, ...), custom_call_target="tpu_custom_call" | custom-call | flops 2113929216 | bytes 7340032 | tf_op jit(solution)/shard_map/pallas_call | solution.py:176
  172.9 4.9 %shard_map.62 = bf16[288,1024]{1,0:T(8,128)(2,1)} custom-call(bf16[288,4096]{1,0:T(8,128)(2,1)S(1)} %copy-done, bf16[128,4096]{1,0:T(8,128)(2,1)} %collective-permute-done.16.part_ref, f32[288,896]{1,0:T(8,128)S(1)} %shard_map.61.early_ref, f32[288,1024]{1,0:T(8,128)S(1)} %copy-done.5, bf16[1024,1024]{1,0:T(8,128)(2,1)S(1)} %copy-done.3), custom_call_target="tpu_custom_call" | custom-call | flops 905969664 | bytes 2097152 | tf_op jit(solution)/shard_map/pallas_call | solution.py:202
  (38 shorter events, 1.4 us)
Async XLA Ops:
  6.5 1.6 copy-start.1
  8.1 0.7 copy-start.8
  8.8 0.7 copy-start.9
  9.4 22.3 %copy-start.11 = (bf16[288,128]{1,0:T(8,128)(2,1)S(1)}, bf16[288,128]{1,0:T(8,128)(2,1)}, u32[]{:S(2)}) copy-start(bf16[288,128]{1,0:T(8,128)(2,1)} %param.8) | copy-start | bytes 221188
  11.4 15.3 %collective-permute-start.7 = (bf16[32,4224]{1,0:T(8,128)(2,1)S(1)}, bf16[32,4224]{1,0:T(8,128)(2,1)S(1)}, u32[]{:S(2)}, u32[]{:S(2)}) collective-permute-start(bf16[32,4224]{1,0:T(8,128)(2,1)S(1)} %shard_map.56.refs_0_), channel_id=1, source_target_pairs={{78,0},{3,1},{0,2},{5,3},{2,4},{7,5},{4,6},{9,7},{6,8},{11,9},{8,1... | collective-permute-start | bytes 811016 | tf_op jit(solution)/shard_map/ppermute | solution.py:236
  23.3 14.7 %collective-permute-start.1 = (bf16[32,4224]{1,0:T(8,128)(2,1)S(1)}, bf16[32,4224]{1,0:T(8,128)(2,1)S(1)}, u32[]{:S(2)}, u32[]{:S(2)}) collective-permute-start(bf16[32,4224]{1,0:T(8,128)(2,1)S(1)} %shard_map.56.refs_0_), channel_id=1, source_target_pairs={{79,0},{2,1},{1,2},{4,3},{3,4},{6,5},{5,6},{8,7},{7,8},{10,9},{9,1... | collective-permute-start | bytes 811016 | tf_op jit(solution)/shard_map/ppermute | solution.py:238
  26.7 11.3 %collective-permute-start.8 = (bf16[32,4224]{1,0:T(8,128)(2,1)S(1)}, bf16[32,4224]{1,0:T(8,128)(2,1)S(1)}, u32[]{:S(2)}, u32[]{:S(2)}) collective-permute-start(bf16[32,4224]{1,0:T(8,128)(2,1)S(1)} %collective-permute-done.7.refs_1_), channel_id=1, source_target_pairs={{78,0},{3,1},{0,2},{5,3},{2,4},{7,5},{4,6},{9,7},{6,8},{11,9},{8,1... | collective-permute-start | bytes 811016 | tf_op jit(solution)/shard_map/ppermute | solution.py:236
  31.7 15.5 %collective-permute-start = (bf16[288,128]{1,0:T(8,128)(2,1)S(1)}, bf16[288,128]{1,0:T(8,128)(2,1)S(1)}, u32[]{:S(2)}, u32[]{:S(2)}) collective-permute-start(bf16[288,128]{1,0:T(8,128)(2,1)S(1)} %copy-done.11), channel_id=1, source_target_pairs={{0,64},{64,0},{1,65},{65,1},{2,66},{66,2},{3,67},{67,3},{4,68},{68... | collective-permute-start | bytes 221192 | tf_op jit(solution)/shard_map/ppermute | solution.py:245
  40.4 30.0 %all-to-all-start.1 = ((bf16[16,8,4096]{2,1,0:T(8,128)(2,1)}), bf16[16,8,4096]{2,1,0:T(8,128)(2,1)S(1)}, u32[]{:S(2)}, u32[]{:S(2)}) async-start(bf16[16,8,4096]{2,1,0:T(8,128)(2,1)} %bitcast.9), calls=%async_computation.1 | async-start | bytes 2097152 | tf_op jit(solution)/shard_map/all_to_all | solution.py:258
  47.1 117.3 %all-gather.2.cloned.1.call-start = ((), (), s32[]{:S(2)}) async-start(), calls=%async_computation.4 | async-start | bytes 2506752 | tf_op jit(solution)/shard_map/all_gather | solution.py:249
  47.9 7.5 %collective-permute-start.2 = (bf16[32,4224]{1,0:T(8,128)(2,1)S(1)}, bf16[32,4224]{1,0:T(8,128)(2,1)S(1)}, u32[]{:S(2)}, u32[]{:S(2)}) collective-permute-start(bf16[32,4224]{1,0:T(8,128)(2,1)S(1)} %collective-permute-done.1.refs_2_), channel_id=1, source_target_pairs={{78,0},{3,1},{0,2},{5,3},{2,4},{7,5},{4,6},{9,7},{6,8},{11,9},{8,1... | collective-permute-start | bytes 811016 | tf_op jit(solution)/shard_map/ppermute | solution.py:238
  51.8 8.7 %collective-permute-start.9 = (bf16[32,4224]{1,0:T(8,128)(2,1)S(1)}, bf16[32,4224]{1,0:T(8,128)(2,1)S(1)}, u32[]{:S(2)}, u32[]{:S(2)}) collective-permute-start(bf16[32,4224]{1,0:T(8,128)(2,1)S(1)} %collective-permute-done.8.refs_3_), channel_id=1, source_target_pairs={{78,0},{3,1},{0,2},{5,3},{2,4},{7,5},{4,6},{9,7},{6,8},{11,9},{8,1... | collective-permute-start | bytes 811016 | tf_op jit(solution)/shard_map/ppermute | solution.py:236
  55.4 8.5 %collective-permute-start.3 = (bf16[32,4224]{1,0:T(8,128)(2,1)S(1)}, bf16[32,4224]{1,0:T(8,128)(2,1)S(1)}, u32[]{:S(2)}, u32[]{:S(2)}) collective-permute-start(bf16[32,4224]{1,0:T(8,128)(2,1)S(1)} %collective-permute-done.2.refs_0_), channel_id=1, source_target_pairs={{78,0},{3,1},{0,2},{5,3},{2,4},{7,5},{4,6},{9,7},{6,8},{11,9},{8,1... | collective-permute-start | bytes 811016 | tf_op jit(solution)/shard_map/ppermute | solution.py:238
  60.5 7.5 %collective-permute-start.10 = (bf16[32,4224]{1,0:T(8,128)(2,1)S(1)}, bf16[32,4224]{1,0:T(8,128)(2,1)S(1)}, u32[]{:S(2)}, u32[]{:S(2)}) collective-permute-start(bf16[32,4224]{1,0:T(8,128)(2,1)S(1)} %collective-permute-done.9.refs_1_), channel_id=1, source_target_pairs={{78,0},{3,1},{0,2},{5,3},{2,4},{7,5},{4,6},{9,7},{6,8},{11,9},{8,1... | collective-permute-start | bytes 811016 | tf_op jit(solution)/shard_map/ppermute | solution.py:236
  70.4 33.3 %all-to-all-start.2 = ((bf16[16,8,4096]{2,1,0:T(8,128)(2,1)}), bf16[16,8,4096]{2,1,0:T(8,128)(2,1)S(1)}, u32[]{:S(2)}, u32[]{:S(2)}) async-start(bf16[16,8,4096]{2,1,0:T(8,128)(2,1)} %bitcast.11), calls=%async_computation.2 | async-start | bytes 2097152 | tf_op jit(solution)/shard_map/all_to_all | solution.py:258
  77.2 7.3 %collective-permute-start.4 = (bf16[32,4224]{1,0:T(8,128)(2,1)S(1)}, bf16[32,4224]{1,0:T(8,128)(2,1)}, u32[]{:S(2)}, u32[]{:S(2)}) collective-permute-start(bf16[32,4224]{1,0:T(8,128)(2,1)S(1)} %collective-permute-done.3.refs_2_), channel_id=1, source_target_pairs={{78,0},{3,1},{0,2},{5,3},{2,4},{7,5},{4,6},{9,7},{6,8},{11,9},{8,1... | collective-permute-start | bytes 811016 | tf_op jit(solution)/shard_map/ppermute | solution.py:238
  81.0 8.5 %collective-permute-start.11 = (bf16[32,4224]{1,0:T(8,128)(2,1)S(1)}, bf16[32,4224]{1,0:T(8,128)(2,1)}, u32[]{:S(2)}, u32[]{:S(2)}) collective-permute-start(bf16[32,4224]{1,0:T(8,128)(2,1)S(1)} %collective-permute-done.10.refs_3_), channel_id=1, source_target_pairs={{78,0},{3,1},{0,2},{5,3},{2,4},{7,5},{4,6},{9,7},{6,8},{11,9},{8,1... | collective-permute-start | bytes 811016 | tf_op jit(solution)/shard_map/ppermute | solution.py:236
  84.5 14.2 %collective-permute-start.5 = (bf16[32,4224]{1,0:T(8,128)(2,1)}, bf16[32,4224]{1,0:T(8,128)(2,1)S(1)}, u32[]{:S(2)}, u32[]{:S(2)}) collective-permute-start(bf16[32,4224]{1,0:T(8,128)(2,1)} %collective-permute-done.4.refs_0_), channel_id=1, source_target_pairs={{78,0},{3,1},{0,2},{5,3},{2,4},{7,5},{4,6},{9,7},{6,8},{11,9},{8,1... | collective-permute-start | bytes 811016 | tf_op jit(solution)/shard_map/ppermute | solution.py:238
  89.5 9.1 %collective-permute-start.12 = (bf16[32,4224]{1,0:T(8,128)(2,1)}, bf16[32,4224]{1,0:T(8,128)(2,1)S(1)}, u32[]{:S(2)}, u32[]{:S(2)}) collective-permute-start(bf16[32,4224]{1,0:T(8,128)(2,1)} %collective-permute-done.11.refs_1_), channel_id=1, source_target_pairs={{78,0},{3,1},{0,2},{5,3},{2,4},{7,5},{4,6},{9,7},{6,8},{11,9},{8,1... | collective-permute-start | bytes 811016 | tf_op jit(solution)/shard_map/ppermute | solution.py:236
  92.6 1.1 copy-start.10
  96.2 1.4 copy-start.2
  97.6 1.1 copy-start.4
  98.6 0.7 copy-start.6
  99.3 1.0 copy-start.7
  103.7 28.0 %all-to-all-start.3 = ((bf16[16,8,4096]{2,1,0:T(8,128)(2,1)}), bf16[16,8,4096]{2,1,0:T(8,128)(2,1)S(1)}, u32[]{:S(2)}, u32[]{:S(2)}) async-start(bf16[16,8,4096]{2,1,0:T(8,128)(2,1)} %bitcast.13), calls=%async_computation.3 | async-start | bytes 2097152 | tf_op jit(solution)/shard_map/all_to_all | solution.py:258
  110.2 7.6 %collective-permute-start.6 = (bf16[32,4224]{1,0:T(8,128)(2,1)S(1)}, bf16[32,4224]{1,0:T(8,128)(2,1)S(1)}, u32[]{:S(2)}, u32[]{:S(2)}) collective-permute-start(bf16[32,4224]{1,0:T(8,128)(2,1)S(1)} %collective-permute-done.5.refs_2_), channel_id=1, source_target_pairs={{78,0},{3,1},{0,2},{5,3},{2,4},{7,5},{4,6},{9,7},{6,8},{11,9},{8,1... | collective-permute-start | bytes 811016 | tf_op jit(solution)/shard_map/ppermute | solution.py:238
  112.9 8.8 %collective-permute-start.13 = (bf16[32,4224]{1,0:T(8,128)(2,1)}, bf16[32,4224]{1,0:T(8,128)(2,1)S(1)}, u32[]{:S(2)}, u32[]{:S(2)}) collective-permute-start(bf16[32,4224]{1,0:T(8,128)(2,1)} %copy-done.6), channel_id=1, source_target_pairs={{78,0},{3,1},{0,2},{5,3},{2,4},{7,5},{4,6},{9,7},{6,8},{11,9},{8,1... | collective-permute-start | bytes 811016 | tf_op jit(solution)/shard_map/ppermute | solution.py:236
  117.8 7.6 %collective-permute-start.14 = (bf16[32,4224]{1,0:T(8,128)(2,1)S(1)}, bf16[32,4224]{1,0:T(8,128)(2,1)S(1)}, u32[]{:S(2)}, u32[]{:S(2)}) collective-permute-start(bf16[32,4224]{1,0:T(8,128)(2,1)S(1)} %collective-permute-done.6.refs_0_), channel_id=1, source_target_pairs={{78,0},{3,1},{0,2},{5,3},{2,4},{7,5},{4,6},{9,7},{6,8},{11,9},{8,1... | collective-permute-start | bytes 811016 | tf_op jit(solution)/shard_map/ppermute | solution.py:238
  121.7 7.6 %collective-permute-start.15 = (bf16[32,4224]{1,0:T(8,128)(2,1)S(1)}, bf16[32,4224]{1,0:T(8,128)(2,1)S(1)}, u32[]{:S(2)}, u32[]{:S(2)}) collective-permute-start(bf16[32,4224]{1,0:T(8,128)(2,1)S(1)} %collective-permute-done.13.refs_1_), channel_id=1, source_target_pairs={{78,0},{3,1},{0,2},{5,3},{2,4},{7,5},{4,6},{9,7},{6,8},{11,9},{8,1... | collective-permute-start | bytes 811016 | tf_op jit(solution)/shard_map/ppermute | solution.py:236
  131.7 23.9 %all-to-all-start = ((bf16[16,8,4096]{2,1,0:T(8,128)(2,1)}), bf16[16,8,4096]{2,1,0:T(8,128)(2,1)}, u32[]{:S(2)}, u32[]{:S(2)}) async-start(bf16[16,8,4096]{2,1,0:T(8,128)(2,1)} %bitcast.7), calls=%async_computation | async-start | bytes 2097152 | tf_op jit(solution)/shard_map/all_to_all | solution.py:258
  138.1 26.2 %collective-permute-start.17 = (bf16[128,4096]{1,0:T(8,128)(2,1)S(1)}, bf16[128,4096]{1,0:T(8,128)(2,1)}, u32[]{:S(2)}, u32[]{:S(2)}) collective-permute-start(bf16[128,4096]{1,0:T(8,128)(2,1)S(1)} %bitcast.19), channel_id=1, source_target_pairs={{0,1},{1,0},{2,3},{3,2},{4,5},{5,4},{6,7},{7,6},{8,9},{9,8},{10,11... | collective-permute-start | bytes 3145736 | tf_op jit(solution)/shard_map/ppermute | solution.py:262
  151.2 13.1 %collective-permute-start.18 = (bf16[128,4096]{1,0:T(8,128)(2,1)S(1)}, bf16[128,4096]{1,0:T(8,128)(2,1)}, u32[]{:S(2)}, u32[]{:S(2)}) collective-permute-start(bf16[128,4096]{1,0:T(8,128)(2,1)S(1)} %bitcast.21), channel_id=1, source_target_pairs={{0,1},{1,0},{2,3},{3,2},{4,5},{5,4},{6,7},{7,6},{8,9},{9,8},{10,11... | collective-permute-start | bytes 3145736 | tf_op jit(solution)/shard_map/ppermute | solution.py:262
  153.2 11.2 %collective-permute-start.19 = (bf16[128,4096]{1,0:T(8,128)(2,1)S(1)}, bf16[128,4096]{1,0:T(8,128)(2,1)}, u32[]{:S(2)}, u32[]{:S(2)}) collective-permute-start(bf16[128,4096]{1,0:T(8,128)(2,1)S(1)} %bitcast.23), channel_id=1, source_target_pairs={{0,1},{1,0},{2,3},{3,2},{4,5},{5,4},{6,7},{7,6},{8,9},{9,8},{10,11... | collective-permute-start | bytes 3145736 | tf_op jit(solution)/shard_map/ppermute | solution.py:262
  155.6 17.2 %collective-permute-start.16 = (bf16[128,4096]{1,0:T(8,128)(2,1)}, bf16[128,4096]{1,0:T(8,128)(2,1)}, u32[]{:S(2)}, u32[]{:S(2)}) collective-permute-start(bf16[128,4096]{1,0:T(8,128)(2,1)} %bitcast.8.refs_3_), channel_id=1, source_target_pairs={{0,1},{1,0},{2,3},{3,2},{4,5},{5,4},{6,7},{7,6},{8,9},{9,8},{10,11... | collective-permute-start | bytes 3145736 | tf_op jit(solution)/shard_map/ppermute | solution.py:262
  164.4 1.7 copy-start
  166.1 6.8 %copy-start.3 = (bf16[1024,1024]{1,0:T(8,128)(2,1)S(1)}, bf16[1024,1024]{1,0:T(8,128)(2,1)}, u32[]{:S(2)}) copy-start(bf16[1024,1024]{1,0:T(8,128)(2,1)} %copy-done.2) | copy-start | bytes 6291460
  166.1 6.8 %copy-start.5 = (f32[288,1024]{1,0:T(8,128)S(1)}, f32[288,1024]{1,0:T(8,128)}, u32[]{:S(2)}) copy-start(f32[288,1024]{1,0:T(8,128)} %copy-done.4) | copy-start | bytes 3538948
Sparse Core Ops, SparseCore 0:
  50.9 78.7 all-gather.1

commit v3 on v0

v3 whole, which is shorter than its diff:
```python
import functools

import jax
import jax.numpy as jnp
import numpy as np
from jax import lax
from jax.experimental import pallas as pl
from jax.experimental.pallas import tpu as pltpu
from jax.sharding import Mesh, PartitionSpec as P

AXES = ("x", "zhi", "y", "zlo", "core")
SIZES = (4, 2, 4, 8, 2)
RING = ("zhi", "zlo", "core")
PLANE = ("x", "y")
CODE_LANES = 128
TILE = 256
IMG = 32
SLOTS = 1024
MINE = SLOTS // 2
STEPS = 8
GROUPS = (8, 8)
WEIGHTS_BY = 2
NT = (((1,), (1,)), ((), ()))
TN = (((0,), (0,)), ((), ()))
VMEM = pl.BlockSpec(memory_space=pltpu.VMEM)
SMEM = pl.BlockSpec(memory_space=pltpu.SMEM)


def gelu_slope(value):
    return (
        0.5 * (1.0 + lax.erf(value * 0.7071067811865476))
        + value * jnp.exp(-0.5 * value * value) * 0.3989422804014327
    )


def params(mib):
    return pltpu.CompilerParams(vmem_limit_bytes=mib * 1024 * 1024)


def pick_kernel(positions_hbm, owners_hbm, hidden_hbm, out_ref, positions, owners, hidden, sems):
    tiles = hidden.shape[0]
    tile = hidden.shape[2]
    copies = [
        pltpu.make_async_copy(positions_hbm, positions, sems.at[tiles]),
        pltpu.make_async_copy(owners_hbm, owners, sems.at[tiles + 1]),
    ]
    for at in range(tiles):
        source = hidden_hbm.at[:, at * tile : (at + 1) * tile]
        copies.append(pltpu.make_async_copy(source, hidden.at[at], sems.at[at]))
    for copy in copies:
        copy.start()
    row = lax.broadcasted_iota(jnp.int32, (IMG, IMG), 0)
    lane = lax.broadcasted_iota(jnp.int32, (IMG, IMG), 1)

    def column(ref):
        spread = jnp.broadcast_to(ref[...], (IMG, IMG))
        return spread, jnp.sum(jnp.where(row == lane, spread, 0), axis=1, keepdims=True)

    copies[0].wait()
    _, place = column(positions)
    token = lax.broadcasted_iota(jnp.int32, (IMG, hidden.shape[1]), 1)
    pick = jnp.where(token == place, 1.0, 0.0).astype(jnp.bfloat16)
    copies[1].wait()
    spread, owner = column(owners)
    same = jnp.where((spread == owner) & (lane < row), 1, 0)
    code = owner * 2 + jnp.sum(same, axis=1, keepdims=True)
    width = out_ref.shape[1] - CODE_LANES
    out_ref[:, width:] = jnp.broadcast_to(code.astype(jnp.float32), (IMG, CODE_LANES)).astype(
        jnp.bfloat16
    )
    for at in range(tiles):
        copies[2 + at].wait()
        picked = jnp.dot(pick, hidden[at], preferred_element_type=jnp.float32)
        picked = picked.astype(jnp.bfloat16)
        x, zhi = at // 2, at % 2
        for y in range(4):
            start = (x * 8 + y * 2 + zhi) * 128
            out_ref[:, start : start + 128] = picked[:, y * 128 : (y + 1) * 128]


def pick(grad_hidden, positions, owner_ids):
    tokens, width = grad_hidden.shape
    tiles = 8
    return pl.pallas_call(
        pick_kernel,
        out_shape=jax.ShapeDtypeStruct((IMG, width + CODE_LANES), jnp.bfloat16),
        in_specs=[pl.BlockSpec(memory_space=pltpu.HBM)] * 3,
        out_specs=VMEM,
        scratch_shapes=[
            pltpu.VMEM((1, IMG), jnp.int32),
            pltpu.VMEM((1, IMG), jnp.int32),
            pltpu.VMEM((tiles, tokens, width // tiles), jnp.bfloat16),
            pltpu.SemaphoreType.DMA((tiles + 2,)),
        ],
        compiler_params=params(60),
        cost_estimate=pl.CostEstimate(
            flops=2 * IMG * tokens * width, bytes_accessed=2 * tokens * width, transcendentals=0
        ),
    )(positions.reshape(1, IMG), owner_ids.reshape(1, IMG), grad_hidden)


def dispatch_kernel(zhi_ref, *refs):
    chunks, out_ref = refs[:-1], refs[-1]
    width = chunks[0].shape[1] - CODE_LANES
    height = 2 * len(chunks)
    size = 4 * IMG
    target = lax.broadcasted_iota(jnp.int32, (IMG, size), 1)
    rank = target & 1
    member = (target >> 1) & 3
    plane = target >> 3
    wanted = (((plane >> 2) * 8 + zhi_ref[0] * 4 + (plane & 3)) * 2 + rank).astype(jnp.float32)
    for first in range(0, len(chunks), 4):
        group = chunks[first : first + 4]
        picks = []
        for at, chunk in enumerate(group):
            code = chunk[:, width : width + 1].astype(jnp.float32)
            picks.append(jnp.where((code == wanted) & (member == at), 1.0, 0.0))
        pick = jnp.concatenate(picks, axis=0).T.astype(jnp.bfloat16)
        for tile in range(width // TILE):
            columns = slice(tile * TILE, (tile + 1) * TILE)
            rows = jnp.concatenate([chunk[:, columns] for chunk in group], axis=0)
            moved = jnp.dot(pick, rows, preferred_element_type=jnp.float32).astype(out_ref.dtype)
            top = tile * height + 2 * first
            out_ref[:, top : top + 8, :] = moved.reshape(16, 8, TILE)


def dispatch(chunks, zhi, width):
    count = len(chunks)
    height = 2 * count * (width // TILE)
    return pl.pallas_call(
        dispatch_kernel,
        out_shape=jax.ShapeDtypeStruct((16, height, TILE), jnp.bfloat16),
        in_specs=[SMEM] + [VMEM] * count,
        out_specs=VMEM,
        compiler_params=params(16),
        cost_estimate=pl.CostEstimate(
            flops=2 * 4 * IMG * IMG * count * width,
            bytes_accessed=2 * 16 * height * TILE,
            transcendentals=0,
        ),
    )(zhi, *chunks)


def arrival_table():
    table = []
    first = 0
    for count in GROUPS:
        for plane in range(16):
            for block in range(first, first + count):
                kept = 1 if block == 0 or block % 2 == 1 else 0
                info = (block + 1) // 2 + 16 * kept + 256 * ((plane // 4) * 8 + plane % 4)
                table += [info, info + 64]
        first += count
    return np.array(table, np.int32).reshape(MINE, 1)


def slope_kernel(at_ref, table_ref, pre_ref, pre_other_ref, slope_ref, here_ref, there_ref):
    z, core = at_ref[0], at_ref[1]
    info = table_ref[...]
    distance = info & 15
    kept = (info >> 4) & 1
    rank = (info >> 6) & 1
    plane = info >> 8
    final = lax.broadcasted_iota(jnp.int32, (MINE, SLOTS), 1)

    def places(gatherer):
        source = (z + 16 + jnp.where(gatherer == 0, -distance, distance)) & 15
        from_core = jnp.where(kept == 1, gatherer, 1 - gatherer)
        tensor = (source & 7) * 2 + from_core
        slot = (tensor * 32 + plane + (source >> 3) * 4) * 2 + rank
        return jnp.where(slot == final, 1.0, 0.0).astype(jnp.bfloat16)

    here = places(core)
    here_ref[...] = here
    there_ref[...] = places(1 - core)
    hidden = pre_ref.shape[0]
    for start, ref in ((0, pre_ref), (hidden, pre_other_ref)):
        values = lax.dot_general(ref[...], here, NT, preferred_element_type=jnp.float32)
        slope_ref[start : start + hidden, :] = gelu_slope(values)


def slopes(z, core, pre, pre_other):
    hidden = pre.shape[0]
    place = jax.ShapeDtypeStruct((MINE, SLOTS), jnp.bfloat16)
    return pl.pallas_call(
        slope_kernel,
        out_shape=(jax.ShapeDtypeStruct((2 * hidden, MINE), jnp.float32), place, place),
        in_specs=[SMEM, VMEM, VMEM, VMEM],
        out_specs=(VMEM, VMEM, VMEM),
        compiler_params=params(16),
        cost_estimate=pl.CostEstimate(
            flops=4 * hidden * MINE * SLOTS,
            bytes_accessed=4 * SLOTS * SLOTS,
            transcendentals=4 * hidden * MINE,
        ),
    )(jnp.stack([z, core]).astype(jnp.int32), jnp.asarray(arrival_table()), pre, pre_other)


def project_kernel(first, core_ref, weights_ref, slope_ref, rows_ref, here_ref, there_ref):
    hidden, count = here_ref.shape
    tiles = weights_ref.shape[0] // 2
    mine, other = core_ref[0] * tiles, (1 - core_ref[0]) * tiles
    height = count // 16
    projected = None
    for tile in range(tiles):
        rows = rows_ref[:, tile * height : (tile + 1) * height, :].reshape(count, TILE)
        weights = jnp.concatenate([weights_ref[mine + tile], weights_ref[other + tile]], axis=0)
        part = lax.dot_general(weights, rows, NT, preferred_element_type=jnp.float32)
        projected = part if projected is None else projected + part
    gradient = (slope_ref[:, first : first + count] * projected).astype(jnp.bfloat16)
    here_ref[...] = gradient[:hidden]
    there_ref[...] = gradient[hidden:]


def project(core, weights, slope, rows, first, count):
    tiles, hidden, _ = weights.shape
    half = jax.ShapeDtypeStruct((hidden, count), jnp.bfloat16)
    return pl.pallas_call(
        functools.partial(project_kernel, first),
        out_shape=(half, half),
        in_specs=[SMEM] + [VMEM] * 3,
        out_specs=(VMEM, VMEM),
        compiler_params=params(24),
        cost_estimate=pl.CostEstimate(
            flops=2 * hidden * tiles * TILE * count,
            bytes_accessed=2 * weights.size,
            transcendentals=0,
        ),
    )(core, weights, slope, rows)


def place_kernel(first, *refs):
    here_ref, there_ref, here_place_ref, there_place_ref = refs[-5:-1]
    out_ref = refs[-1]
    span = slice(first, first + here_ref.shape[1])
    placed = jnp.dot(here_ref[...], here_place_ref[span, :], preferred_element_type=jnp.float32)
    placed += jnp.dot(there_ref[...], there_place_ref[span, :], preferred_element_type=jnp.float32)
    if len(refs) > 5:
        placed += refs[0][...].astype(jnp.float32)
    out_ref[...] = placed.astype(out_ref.dtype)


def put(here, there, here_place, there_place, first, base):
    hidden = here.shape[0]
    operands = base + [here, there, here_place, there_place]
    return pl.pallas_call(
        functools.partial(place_kernel, first),
        out_shape=jax.ShapeDtypeStruct((hidden, SLOTS), jnp.bfloat16),
        in_specs=[VMEM] * len(operands),
        out_specs=VMEM,
        compiler_params=params(16),
        cost_estimate=pl.CostEstimate(
            flops=4 * hidden * here.shape[1] * SLOTS,
            bytes_accessed=4 * SLOTS * here.shape[1],
            transcendentals=0,
        ),
    )(*operands)


def ring_pairs(other_core):
    pairs = []
    for z in range(16):
        for core in range(2):
            below = (z + (-1 if core == 0 else 1)) % 16
            sender = 1 - core if other_core else core
            pairs.append((below * 2 + sender, z * 2 + core))
    return pairs


def shards(grad_hidden, positions, owner_ids, w_proj, pre_act):
    zhi, zlo, core = (lax.axis_index(name) for name in ("zhi", "zlo", "core"))
    width = grad_hidden.shape[1]
    zhi_at = jnp.reshape(zhi, (1,)).astype(jnp.int32)
    core_at = jnp.reshape(core, (1,)).astype(jnp.int32)
    swap = [(0, 1), (1, 0)]

    packed = pick(grad_hidden, positions, owner_ids)

    other = lax.ppermute(w_proj, "zhi", swap)
    both = jnp.concatenate(
        [jnp.where(zhi == 0, w_proj, other), jnp.where(zhi == 0, other, w_proj)], axis=1
    )

    kept, crossed = [packed], [packed]
    for step in range(1, STEPS + 1):
        kept.append(lax.ppermute(kept[-1], RING, ring_pairs(False)))
        if step < STEPS:
            crossed.append(lax.ppermute(crossed[-1], RING, ring_pairs(step == 1)))
        if step == WEIGHTS_BY:
            kept[-1], crossed[-1], both = lax.optimization_barrier((kept[-1], crossed[-1], both))
            weights = lax.all_gather(both, ("core",) + PLANE, axis=0, tiled=False)
    chunks = [packed]
    for step in range(1, STEPS + 1):
        chunks.append(kept[step])
        if step < STEPS:
            chunks.append(crossed[step])

    pre = pre_act[0].T
    slope, here_place, there_place = slopes(
        zhi * 8 + zlo, core, pre, lax.ppermute(pre, "core", swap)
    )

    placed = []
    first = 0
    for count in GROUPS:
        outgoing = dispatch(chunks[first : first + count], zhi_at, width)
        received = lax.all_to_all(outgoing, PLANE, split_axis=0, concat_axis=0, tiled=True)
        here, there = project(core_at, weights, slope, received, first * IMG, count * IMG)
        there = lax.ppermute(there, "core", swap)
        placed = [put(here, there, here_place, there_place, first * IMG, placed)]
        first += count
    return placed[0].T[None]


def solution(mesh):
    fine = Mesh(mesh.devices.reshape(SIZES), AXES)
    return jax.shard_map(
        shards,
        mesh=fine,
        in_specs=(
            P(AXES, None),
            P(AXES),
            P(AXES, None),
            P(("zlo", "core"), ("x", "zhi", "y")),
            P(("x", "zhi", "y"), None, ("zlo", "core")),
        ),
        out_specs=P(("x", "zhi", "y"), None, ("zlo", "core")),
        check_vma=False,
    )
```

time: 298 us -> 166 us (0.56)
  waiting for transfers between devices: 229 us -> 22.8 us
  starting transfers between devices: 0.04 us -> 101 us
  blocking collectives: 40 us -> 0 us
  Pallas kernels: 0 us -> 16.8 us
  local copies, waits for them, and re-layouts: 2.05 us -> 10.5 us
  matrix products: 8.15 us -> 0 us
    all_gather x2 -> x1, waiting for transfers between devices: 229 us -> 0.01 us  [shards(): weights = lax.all_gather(both, ('core',) + PLANE, axis=0, tiled=False)]
    ppermute x0 -> x19, starting transfers between devices: none -> 87.4 us  [the longest x8 30 us: shards(): kept.append(lax.ppermute(kept[-1], RING, ring_pairs(False)))]
    all_to_all x1 -> x0, blocking collectives: 40 us -> none  [shards(): lax.all_to_all(outgoing, 'dp', split_axis=0, concat_axis=0, tiled=True)]
    ppermute x0 -> x19, waiting for transfers between devices: none -> 22.8 us  [the longest x8 11.8 us: shards(): kept.append(lax.ppermute(kept[-1], RING, ring_pairs(False)))]
    pallas_call x0 -> x8, Pallas kernels: none -> 16.8 us  [the longest x2 5.23 us: project(): pl.pallas_call(functools.partial(project_kernel, first), out_shape=(half,...]
    all_to_all x0 -> x2, starting transfers between devices: none -> 13.3 us  [shards(): lax.all_to_all(outgoing, PLANE, split_axis=0, concat_axis=0, tiled=True)]
    unnamed x8 -> x26, local copies, waits for them, and re-layouts: 0.02 us -> 10.5 us
    dot_general x2 -> x0, matrix products: 8.15 us -> none  [the longest x1 7.81 us: shards(): lax.dot_general(lax.all_gather(received, 'tensor', axis=0, tiled=True), w...]
  transfers between devices with their start and end apart: 2 -> 22, of which waited for: 2 -> 12; matrix products, arithmetic and copies ran while one was open for 1% -> 0% of each run, Pallas kernels for 0% -> 8%
where the time goes in v3:
time: 166 us; the launch traced here: 165 us
  starting transfers between devices  101 us (61%)
  waiting for transfers between devices  22.8 us (14%)
  Pallas kernels  16.8 us (10%)
  between operations  13.7 us (8%)
  local copies, waits for them, and re-layouts  10.5 us (6%)
    ppermute x8, starting transfers between devices, shards(): kept.append(lax.ppermute(kept[-1], RING, ring_pairs(False)))  30 us
    ppermute x7, starting transfers between devices, shards(): crossed.append(lax.ppermute(crossed[-1], RING, ring_pairs(step == 1)))  29.7 us
    all_to_all x2, starting transfers between devices, shards(): lax.all_to_all(outgoing, PLANE, split_axis=0, concat_axis=0, tiled=True)  13.3 us
    ppermute x8, waiting for transfers between devices, shards(): kept.append(lax.ppermute(kept[-1], RING, ring_pairs(False)))  11.8 us
    unnamed x26, local copies, waits for them, and re-layouts  10.5 us
    ppermute x2, starting transfers between devices, shards(): there = lax.ppermute(there, 'core', swap)  10.5 us
    ppermute x1, starting transfers between devices, shards(): other = lax.ppermute(w_proj, 'zhi', swap)  9.45 us
    ppermute x7, waiting for transfers between devices, shards(): crossed.append(lax.ppermute(crossed[-1], RING, ring_pairs(step == 1)))  8.16 us
  transfers between devices with their start and end apart: 22, of which 12 were waited for; matrix products, arithmetic and copies ran while one was open for 0% of the time, Pallas kernels for 8%

profile of v3, /device:TPU:1, one launch (start us, length us, event | category | flops | bytes accessed | tf_op | source)
XLA Modules:
  0.0 165.3 jit_solution(11077234369430563466)
XLA Ops:
  6.5 3.1 %shard_map.64.refs_0_ = bf16[32,4224]{1,0:T(8,128)(2,1)} custom-call(s32[1,32]{1,0:T(1,128)} %bitcast.16, s32[1,32]{1,0:T(1,128)} %bitcast.17, bf16[256,4096]{1,0:T(8,128)(2,1)} %hidden_hbm.1), custom_call_target="tpu_custom_call" | custom-call | flops 67108864 | bytes 2097152 | tf_op jit(solution)/shard_map/pallas_call | solution.py:84
  9.6 4.9 %collective-permute-start.2 = (bf16[32,4224]{1,0:T(8,128)(2,1)}, bf16[32,4224]{1,0:T(8,128)(2,1)S(1)}, u32[]{:S(2)}, u32[]{:S(2)}) collective-permute-start(bf16[32,4224]{1,0:T(8,128)(2,1)} %shard_map.64.refs_0_), channel_id=1, source_target_pairs={{79,0},{2,1},{1,2},{4,3},{3,4},{6,5},{5,6},{8,7},{7,8},{10,9},{9,1... | collective-permute-start | bytes 811016 | tf_op jit(solution)/shard_map/ppermute | solution.py:288
  14.5 8.9 %collective-permute-start = (bf16[32,4224]{1,0:T(8,128)(2,1)}, bf16[32,4224]{1,0:T(8,128)(2,1)S(1)}, u32[]{:S(2)}, u32[]{:S(2)}) collective-permute-start(bf16[32,4224]{1,0:T(8,128)(2,1)} %shard_map.64.refs_0_), channel_id=1, source_target_pairs={{78,0},{3,1},{0,2},{5,3},{2,4},{7,5},{4,6},{9,7},{6,8},{11,9},{8,1... | collective-permute-start | bytes 811016 | tf_op jit(solution)/shard_map/ppermute | solution.py:286
  23.5 9.5 %collective-permute-start.4 = (bf16[288,128]{1,0:T(8,128)(2,1)S(1)}, bf16[288,128]{1,0:T(8,128)(2,1)S(1)}, u32[]{:S(2)}, u32[]{:S(2)}) collective-permute-start(bf16[288,128]{1,0:T(8,128)(2,1)S(1)} %copy-done.12), channel_id=1, source_target_pairs={{0,64},{64,0},{1,65},{65,1},{2,66},{66,2},{3,67},{67,3},{4,68},{68... | collective-permute-start | bytes 221192 | tf_op jit(solution)/shard_map/ppermute | solution.py:279
  33.0 1.9 %collective-permute-start.3 = (bf16[32,4224]{1,0:T(8,128)(2,1)S(1)}, bf16[32,4224]{1,0:T(8,128)(2,1)S(1)}, u32[]{:S(2)}, u32[]{:S(2)}) collective-permute-start(bf16[32,4224]{1,0:T(8,128)(2,1)S(1)} %collective-permute-done.2.refs_2_), channel_id=1, source_target_pairs={{78,0},{3,1},{0,2},{5,3},{2,4},{7,5},{4,6},{9,7},{6,8},{11,9},{8,1... | collective-permute-start | bytes 811016 | tf_op jit(solution)/shard_map/ppermute | solution.py:288
  34.9 1.9 %collective-permute-start.1 = (bf16[32,4224]{1,0:T(8,128)(2,1)S(1)}, bf16[32,4224]{1,0:T(8,128)(2,1)S(1)}, u32[]{:S(2)}, u32[]{:S(2)}) collective-permute-start(bf16[32,4224]{1,0:T(8,128)(2,1)S(1)} %collective-permute-done.refs_1_), channel_id=1, source_target_pairs={{78,0},{3,1},{0,2},{5,3},{2,4},{7,5},{4,6},{9,7},{6,8},{11,9},{8,1... | collective-permute-start | bytes 811016 | tf_op jit(solution)/shard_map/ppermute | solution.py:286
  36.8 0.9 collective-permute-done.4
  37.7 0.7 pad_maximum_fusion
  38.4 4.9 %collective-permute-done.3.refs_4_ = bf16[32,4224]{1,0:T(8,128)(2,1)S(1)} collective-permute-done((bf16[32,4224]{1,0:T(8,128)(2,1)S(1)}, bf16[32,4224]{1,0:T(8,128)(2,1)S(1)}, u32[]{:S(2)}, u32[]{:S(2)}) %collective-permute-start.3) | collective-permute-done | bytes 270368 | tf_op jit(solution)/shard_map/ppermute | solution.py:288
  43.3 2.6 %collective-permute-done.1.refs_3_ = bf16[32,4224]{1,0:T(8,128)(2,1)S(1)} collective-permute-done((bf16[32,4224]{1,0:T(8,128)(2,1)S(1)}, bf16[32,4224]{1,0:T(8,128)(2,1)S(1)}, u32[]{:S(2)}, u32[]{:S(2)}) %collective-permute-start.1) | collective-permute-done | bytes 270368 | tf_op jit(solution)/shard_map/ppermute | solution.py:286
  46.0 4.0 %collective-permute-start.6 = (bf16[32,4224]{1,0:T(8,128)(2,1)S(1)}, bf16[32,4224]{1,0:T(8,128)(2,1)S(1)}, u32[]{:S(2)}, u32[]{:S(2)}) collective-permute-start(bf16[32,4224]{1,0:T(8,128)(2,1)S(1)} %collective-permute-done.1.refs_3_), channel_id=1, source_target_pairs={{78,0},{3,1},{0,2},{5,3},{2,4},{7,5},{4,6},{9,7},{6,8},{11,9},{8,1... | collective-permute-start | bytes 811016 | tf_op jit(solution)/shard_map/ppermute | solution.py:286
  50.0 1.9 %collective-permute-start.7 = (bf16[32,4224]{1,0:T(8,128)(2,1)S(1)}, bf16[32,4224]{1,0:T(8,128)(2,1)S(1)}, u32[]{:S(2)}, u32[]{:S(2)}) collective-permute-start(bf16[32,4224]{1,0:T(8,128)(2,1)S(1)} %collective-permute-done.3.refs_4_), channel_id=1, source_target_pairs={{78,0},{3,1},{0,2},{5,3},{2,4},{7,5},{4,6},{9,7},{6,8},{11,9},{8,1... | collective-permute-start | bytes 811016 | tf_op jit(solution)/shard_map/ppermute | solution.py:288
  51.9 1.6 collective-permute-done.6.refs_5_
  53.5 4.9 %collective-permute-start.8 = (bf16[32,4224]{1,0:T(8,128)(2,1)S(1)}, bf16[32,4224]{1,0:T(8,128)(2,1)S(1)}, u32[]{:S(2)}, u32[]{:S(2)}) collective-permute-start(bf16[32,4224]{1,0:T(8,128)(2,1)S(1)} %collective-permute-done.6.refs_5_), channel_id=1, source_target_pairs={{78,0},{3,1},{0,2},{5,3},{2,4},{7,5},{4,6},{9,7},{6,8},{11,9},{8,1... | collective-permute-start | bytes 811016 | tf_op jit(solution)/shard_map/ppermute | solution.py:286
  58.4 3.4 %collective-permute-done.8.refs_7_ = bf16[32,4224]{1,0:T(8,128)(2,1)S(1)} collective-permute-done((bf16[32,4224]{1,0:T(8,128)(2,1)S(1)}, bf16[32,4224]{1,0:T(8,128)(2,1)S(1)}, u32[]{:S(2)}, u32[]{:S(2)}) %collective-permute-start.8) | collective-permute-done | bytes 270368 | tf_op jit(solution)/shard_map/ppermute | solution.py:286
  61.8 1.0 copy-done.6
  62.7 2.2 %shard_map.66 = bf16[16,256,256]{2,1,0:T(8,128)(2,1)} custom-call(s32[1]{0:T(128)} %bitcast.8.zhi_ref, bf16[32,4224]{1,0:T(8,128)(2,1)S(1)} %copy-done.6, bf16[32,4224]{1,0:T(8,128)(2,1)S(1)} %collective-permute-done.refs_1_, bf16[32,4224]{1,0:T(8,128)(2,1)S(1)} %collective-permute-done.2.refs_2_, bf16[32,4224]{1,0:T(8,128)(2,1)S(1)} %collective-permute-done.1.refs_3_, ...), custom_call_target="tpu_custom_call" | custom-call | flops 268435456 | bytes 2097152 | tf_op jit(solution)/shard_map/pallas_call | solution.py:130
  64.9 6.8 %all-to-all-start = ((bf16[16,256,256]{2,1,0:T(8,128)(2,1)}), bf16[16,256,256]{2,1,0:T(8,128)(2,1)S(1)}, u32[]{:S(2)}, u32[]{:S(2)}) async-start(bf16[16,256,256]{2,1,0:T(8,128)(2,1)} %shard_map.66), calls=%async_computation | async-start | bytes 4194304 | tf_op jit(solution)/shard_map/all_to_all | solution.py:307
  71.6 5.0 %collective-permute-start.10 = (bf16[32,4224]{1,0:T(8,128)(2,1)S(1)}, bf16[32,4224]{1,0:T(8,128)(2,1)S(1)}, u32[]{:S(2)}, u32[]{:S(2)}) collective-permute-start(bf16[32,4224]{1,0:T(8,128)(2,1)S(1)} %collective-permute-done.7.refs_6_), channel_id=1, source_target_pairs={{78,0},{3,1},{0,2},{5,3},{2,4},{7,5},{4,6},{9,7},{6,8},{11,9},{8,1... | collective-permute-start | bytes 811016 | tf_op jit(solution)/shard_map/ppermute | solution.py:288
  76.7 1.9 %collective-permute-start.11 = (bf16[32,4224]{1,0:T(8,128)(2,1)S(1)}, bf16[32,4224]{1,0:T(8,128)(2,1)S(1)}, u32[]{:S(2)}, u32[]{:S(2)}) collective-permute-start(bf16[32,4224]{1,0:T(8,128)(2,1)S(1)} %collective-permute-done.8.refs_7_), channel_id=1, source_target_pairs={{78,0},{3,1},{0,2},{5,3},{2,4},{7,5},{4,6},{9,7},{6,8},{11,9},{8,1... | collective-permute-start | bytes 811016 | tf_op jit(solution)/shard_map/ppermute | solution.py:286
  78.6 1.5 collective-permute-done.10.refs_0_
  80.1 5.3 %collective-permute-start.12 = (bf16[32,4224]{1,0:T(8,128)(2,1)S(1)}, bf16[32,4224]{1,0:T(8,128)(2,1)S(1)}, u32[]{:S(2)}, u32[]{:S(2)}) collective-permute-start(bf16[32,4224]{1,0:T(8,128)(2,1)S(1)} %collective-permute-done.10.refs_0_), channel_id=1, source_target_pairs={{78,0},{3,1},{0,2},{5,3},{2,4},{7,5},{4,6},{9,7},{6,8},{11,9},{8,1... | collective-permute-start | bytes 811016 | tf_op jit(solution)/shard_map/ppermute | solution.py:288
  85.4 2.9 %collective-permute-start.13 = (bf16[32,4224]{1,0:T(8,128)(2,1)S(1)}, bf16[32,4224]{1,0:T(8,128)(2,1)S(1)}, u32[]{:S(2)}, u32[]{:S(2)}) collective-permute-start(bf16[32,4224]{1,0:T(8,128)(2,1)S(1)} %collective-permute-done.11.refs_1_), channel_id=1, source_target_pairs={{78,0},{3,1},{0,2},{5,3},{2,4},{7,5},{4,6},{9,7},{6,8},{11,9},{8,1... | collective-permute-start | bytes 811016 | tf_op jit(solution)/shard_map/ppermute | solution.py:286
  88.3 0.5 collective-permute-done.12.refs_2_
  88.8 5.3 %collective-permute-start.14 = (bf16[32,4224]{1,0:T(8,128)(2,1)S(1)}, bf16[32,4224]{1,0:T(8,128)(2,1)S(1)}, u32[]{:S(2)}, u32[]{:S(2)}) collective-permute-start(bf16[32,4224]{1,0:T(8,128)(2,1)S(1)} %collective-permute-done.12.refs_2_), channel_id=1, source_target_pairs={{78,0},{3,1},{0,2},{5,3},{2,4},{7,5},{4,6},{9,7},{6,8},{11,9},{8,1... | collective-permute-start | bytes 811016 | tf_op jit(solution)/shard_map/ppermute | solution.py:288
  94.1 2.9 %collective-permute-start.15 = (bf16[32,4224]{1,0:T(8,128)(2,1)S(1)}, bf16[32,4224]{1,0:T(8,128)(2,1)S(1)}, u32[]{:S(2)}, u32[]{:S(2)}) collective-permute-start(bf16[32,4224]{1,0:T(8,128)(2,1)S(1)} %collective-permute-done.13.refs_3_), channel_id=1, source_target_pairs={{78,0},{3,1},{0,2},{5,3},{2,4},{7,5},{4,6},{9,7},{6,8},{11,9},{8,1... | collective-permute-start | bytes 811016 | tf_op jit(solution)/shard_map/ppermute | solution.py:286
  97.0 0.5 collective-permute-done.14.refs_4_
  97.5 5.3 %collective-permute-start.16 = (bf16[32,4224]{1,0:T(8,128)(2,1)S(1)}, bf16[32,4224]{1,0:T(8,128)(2,1)S(1)}, u32[]{:S(2)}, u32[]{:S(2)}) collective-permute-start(bf16[32,4224]{1,0:T(8,128)(2,1)S(1)} %collective-permute-done.14.refs_4_), channel_id=1, source_target_pairs={{78,0},{3,1},{0,2},{5,3},{2,4},{7,5},{4,6},{9,7},{6,8},{11,9},{8,1... | collective-permute-start | bytes 811016 | tf_op jit(solution)/shard_map/ppermute | solution.py:288
  102.8 2.6 %collective-permute-start.17 = (bf16[32,4224]{1,0:T(8,128)(2,1)S(1)}, bf16[32,4224]{1,0:T(8,128)(2,1)S(1)}, u32[]{:S(2)}, u32[]{:S(2)}) collective-permute-start(bf16[32,4224]{1,0:T(8,128)(2,1)S(1)} %collective-permute-done.15.refs_5_), channel_id=1, source_target_pairs={{78,0},{3,1},{0,2},{5,3},{2,4},{7,5},{4,6},{9,7},{6,8},{11,9},{8,1... | collective-permute-start | bytes 811016 | tf_op jit(solution)/shard_map/ppermute | solution.py:286
  105.4 0.8 collective-permute-done.16.refs_6_
  106.2 4.2 %collective-permute-done.17.refs_7_ = bf16[32,4224]{1,0:T(8,128)(2,1)S(1)} collective-permute-done((bf16[32,4224]{1,0:T(8,128)(2,1)S(1)}, bf16[32,4224]{1,0:T(8,128)(2,1)S(1)}, u32[]{:S(2)}, u32[]{:S(2)}) %collective-permute-start.17) | collective-permute-done | bytes 270368 | tf_op jit(solution)/shard_map/ppermute | solution.py:286
  110.4 2.2 %shard_map.69 = bf16[16,256,256]{2,1,0:T(8,128)(2,1)} custom-call(s32[1]{0:T(128)} %bitcast.8.zhi_ref, bf16[32,4224]{1,0:T(8,128)(2,1)S(1)} %collective-permute-done.10.refs_0_, bf16[32,4224]{1,0:T(8,128)(2,1)S(1)} %collective-permute-done.11.refs_1_, bf16[32,4224]{1,0:T(8,128)(2,1)S(1)} %collective-permute-done.12.refs_2_, ...), custom_call_target="tpu_custom_call" | custom-call | flops 268435456 | bytes 2097152 | tf_op jit(solution)/shard_map/pallas_call | solution.py:130
  112.6 6.5 %all-to-all-start.1 = ((bf16[16,256,256]{2,1,0:T(8,128)(2,1)}), bf16[16,256,256]{2,1,0:T(8,128)(2,1)}, u32[]{:S(2)}, u32[]{:S(2)}) async-start(bf16[16,256,256]{2,1,0:T(8,128)(2,1)} %shard_map.69), calls=%async_computation.1 | async-start | bytes 4194304 | tf_op jit(solution)/shard_map/all_to_all | solution.py:307
  119.2 7.7 %collective-permute-start.5 = (bf16[288,1024]{1,0:T(8,128)(2,1)S(1)}, bf16[288,1024]{1,0:T(8,128)(2,1)S(1)}, u32[]{:S(2)}, u32[]{:S(2)}) collective-permute-start(bf16[288,1024]{1,0:T(8,128)(2,1)S(1)} %bitcast.14), channel_id=1, source_target_pairs={{0,1},{1,0},{2,3},{3,2},{4,5},{5,4},{6,7},{7,6},{8,9},{9,8},{10,11... | collective-permute-start | bytes 1769480 | tf_op jit(solution)/shard_map/ppermute | solution.py:300
  127.0 1.5 collective-permute-done.5.pre_other_ref
  128.5 0.8 copy-done.9
  129.3 1.1 copy-done.8
  130.4 1.1 copy-done.10
  131.5 2.4 %shard_map.65 = (f32[576,512]{1,0:T(8,128)S(1)}, bf16[512,1024]{1,0:T(8,128)(2,1)S(1)}, bf16[512,1024]{1,0:T(8,128)(2,1)S(1)}) custom-call(s32[2]{0:T(128)S(1)} %pad_add_fusion.at_ref, s32[512,1]{1,0:T(8,128)S(1)} %copy-done.11, bf16[288,1024]{1,0:T(8,128)(2,1)S(1)} %bitcast.15, bf16[288,1024]{1,0:T(8,128)(2,1)S(1)} %copy-done.10), custom_call_target="tpu_custom_call" | custom-call | flops 603979776 | bytes 4194304 | tf_op jit(solution)/shard_map/pallas_call | solution.py:185
  133.8 0.9 copy-done.2
  134.8 1.0 copy-done.4
  135.8 2.3 %copy-done = bf16[9216,256]{1,0:T(8,128)(2,1)S(1)} copy-done((bf16[9216,256]{1,0:T(8,128)(2,1)S(1)}, bf16[9216,256]{1,0:T(8,128)(2,1)}, u32[]{:S(2)}) %copy-start) | copy-done | bytes 4718616
  138.1 2.1 %shard_map.67 = (bf16[288,256]{1,0:T(8,128)(2,1)S(1)}, bf16[288,256]{1,0:T(8,128)(2,1)}) custom-call(s32[1]{0:T(128)} %bitcast.core_ref, bf16[32,288,256]{2,1,0:T(8,128)(2,1)S(1)} %bitcast.12, f32[576,512]{1,0:T(8,128)S(1)} %get-tuple-element.16.slope_ref, bf16[16,256,256]{2,1,0:T(8,128)(2,1)S(1)} %all-to-all-done.rows_ref), custom_call_target="tpu_custom_call" | custom-call | flops 1207959552 | bytes 4718592 | tf_op jit(solution)/shard_map/pallas_call | solution.py:218
  140.2 2.3 %collective-permute-start.9 = (bf16[288,256]{1,0:T(8,128)(2,1)}, bf16[288,256]{1,0:T(8,128)(2,1)S(1)}, u32[]{:S(2)}, u32[]{:S(2)}) collective-permute-start(bf16[288,256]{1,0:T(8,128)(2,1)} %get-tuple-element.20), channel_id=1, source_target_pairs={{0,1},{1,0},{2,3},{3,2},{4,5},{5,4},{6,7},{7,6},{8,9},{9,8},{10,11... | collective-permute-start | bytes 442376 | tf_op jit(solution)/shard_map/ppermute | solution.py:309
  142.5 2.3 %copy-done.1 = bf16[9216,256]{1,0:T(8,128)(2,1)S(1)} copy-done((bf16[9216,256]{1,0:T(8,128)(2,1)S(1)}, bf16[9216,256]{1,0:T(8,128)(2,1)}, u32[]{:S(2)}) %copy-start.1) | copy-done | bytes 4718616
  144.8 3.2 %shard_map.70 = (bf16[288,256]{1,0:T(8,128)(2,1)S(1)}, bf16[288,256]{1,0:T(8,128)(2,1)S(1)}) custom-call(s32[1]{0:T(128)} %bitcast.core_ref, bf16[32,288,256]{2,1,0:T(8,128)(2,1)S(1)} %bitcast.13, f32[576,512]{1,0:T(8,128)S(1)} %get-tuple-element.16.slope_ref, bf16[16,256,256]{2,1,0:T(8,128)(2,1)} %all-to-all-done.1.rows_ref), custom_call_target="tpu_custom_call" | custom-call | flops 1207959552 | bytes 4718592 | tf_op jit(solution)/shard_map/pallas_call | solution.py:218
  148.0 8.2 %collective-permute-start.18 = (bf16[288,256]{1,0:T(8,128)(2,1)S(1)}, bf16[288,256]{1,0:T(8,128)(2,1)S(1)}, u32[]{:S(2)}, u32[]{:S(2)}) collective-permute-start(bf16[288,256]{1,0:T(8,128)(2,1)S(1)} %get-tuple-element.24), channel_id=1, source_target_pairs={{0,1},{1,0},{2,3},{3,2},{4,5},{5,4},{6,7},{7,6},{8,9},{9,8},{10,11... | collective-permute-start | bytes 442376 | tf_op jit(solution)/shard_map/ppermute | solution.py:309
  157.2 1.3 shard_map.71
  (34 shorter events, 1.1 us)
Async XLA Ops:
  6.5 17.0 %copy-start.12 = (bf16[288,128]{1,0:T(8,128)(2,1)S(1)}, bf16[288,128]{1,0:T(8,128)(2,1)}, u32[]{:S(2)}) copy-start(bf16[288,128]{1,0:T(8,128)(2,1)} %param.9) | copy-start | bytes 221188
  6.5 129.2 %all-gather.3.cloned.1.call-start = ((), (), s32[]{:S(2)}) async-start(), calls=%async_computation.2 | async-start | bytes 4866048 | tf_op jit(solution)/shard_map/all_gather | solution.py:291
  9.6 23.4 %collective-permute-start.2 = (bf16[32,4224]{1,0:T(8,128)(2,1)}, bf16[32,4224]{1,0:T(8,128)(2,1)S(1)}, u32[]{:S(2)}, u32[]{:S(2)}) collective-permute-start(bf16[32,4224]{1,0:T(8,128)(2,1)} %shard_map.64.refs_0_), channel_id=1, source_target_pairs={{79,0},{2,1},{1,2},{4,3},{3,4},{6,5},{5,6},{8,7},{7,8},{10,9},{9,1... | collective-permute-start | bytes 811016 | tf_op jit(solution)/shard_map/ppermute | solution.py:288
  14.5 20.4 %collective-permute-start = (bf16[32,4224]{1,0:T(8,128)(2,1)}, bf16[32,4224]{1,0:T(8,128)(2,1)S(1)}, u32[]{:S(2)}, u32[]{:S(2)}) collective-permute-start(bf16[32,4224]{1,0:T(8,128)(2,1)} %shard_map.64.refs_0_), channel_id=1, source_target_pairs={{78,0},{3,1},{0,2},{5,3},{2,4},{7,5},{4,6},{9,7},{6,8},{11,9},{8,1... | collective-permute-start | bytes 811016 | tf_op jit(solution)/shard_map/ppermute | solution.py:286
  23.5 14.2 %collective-permute-start.4 = (bf16[288,128]{1,0:T(8,128)(2,1)S(1)}, bf16[288,128]{1,0:T(8,128)(2,1)S(1)}, u32[]{:S(2)}, u32[]{:S(2)}) collective-permute-start(bf16[288,128]{1,0:T(8,128)(2,1)S(1)} %copy-done.12), channel_id=1, source_target_pairs={{0,64},{64,0},{1,65},{65,1},{2,66},{66,2},{3,67},{67,3},{4,68},{68... | collective-permute-start | bytes 221192 | tf_op jit(solution)/shard_map/ppermute | solution.py:279
  33.0 10.4 %collective-permute-start.3 = (bf16[32,4224]{1,0:T(8,128)(2,1)S(1)}, bf16[32,4224]{1,0:T(8,128)(2,1)S(1)}, u32[]{:S(2)}, u32[]{:S(2)}) collective-permute-start(bf16[32,4224]{1,0:T(8,128)(2,1)S(1)} %collective-permute-done.2.refs_2_), channel_id=1, source_target_pairs={{78,0},{3,1},{0,2},{5,3},{2,4},{7,5},{4,6},{9,7},{6,8},{11,9},{8,1... | collective-permute-start | bytes 811016 | tf_op jit(solution)/shard_map/ppermute | solution.py:288
  34.9 11.0 %collective-permute-start.1 = (bf16[32,4224]{1,0:T(8,128)(2,1)S(1)}, bf16[32,4224]{1,0:T(8,128)(2,1)S(1)}, u32[]{:S(2)}, u32[]{:S(2)}) collective-permute-start(bf16[32,4224]{1,0:T(8,128)(2,1)S(1)} %collective-permute-done.refs_1_), channel_id=1, source_target_pairs={{78,0},{3,1},{0,2},{5,3},{2,4},{7,5},{4,6},{9,7},{6,8},{11,9},{8,1... | collective-permute-start | bytes 811016 | tf_op jit(solution)/shard_map/ppermute | solution.py:286
  46.0 7.5 %collective-permute-start.6 = (bf16[32,4224]{1,0:T(8,128)(2,1)S(1)}, bf16[32,4224]{1,0:T(8,128)(2,1)S(1)}, u32[]{:S(2)}, u32[]{:S(2)}) collective-permute-start(bf16[32,4224]{1,0:T(8,128)(2,1)S(1)} %collective-permute-done.1.refs_3_), channel_id=1, source_target_pairs={{78,0},{3,1},{0,2},{5,3},{2,4},{7,5},{4,6},{9,7},{6,8},{11,9},{8,1... | collective-permute-start | bytes 811016 | tf_op jit(solution)/shard_map/ppermute | solution.py:286
  50.0 8.4 %collective-permute-start.7 = (bf16[32,4224]{1,0:T(8,128)(2,1)S(1)}, bf16[32,4224]{1,0:T(8,128)(2,1)S(1)}, u32[]{:S(2)}, u32[]{:S(2)}) collective-permute-start(bf16[32,4224]{1,0:T(8,128)(2,1)S(1)} %collective-permute-done.3.refs_4_), channel_id=1, source_target_pairs={{78,0},{3,1},{0,2},{5,3},{2,4},{7,5},{4,6},{9,7},{6,8},{11,9},{8,1... | collective-permute-start | bytes 811016 | tf_op jit(solution)/shard_map/ppermute | solution.py:288
  53.5 8.3 %collective-permute-start.8 = (bf16[32,4224]{1,0:T(8,128)(2,1)S(1)}, bf16[32,4224]{1,0:T(8,128)(2,1)S(1)}, u32[]{:S(2)}, u32[]{:S(2)}) collective-permute-start(bf16[32,4224]{1,0:T(8,128)(2,1)S(1)} %collective-permute-done.6.refs_5_), channel_id=1, source_target_pairs={{78,0},{3,1},{0,2},{5,3},{2,4},{7,5},{4,6},{9,7},{6,8},{11,9},{8,1... | collective-permute-start | bytes 811016 | tf_op jit(solution)/shard_map/ppermute | solution.py:286
  61.8 1.0 copy-start.6
  64.9 47.7 %all-to-all-start = ((bf16[16,256,256]{2,1,0:T(8,128)(2,1)}), bf16[16,256,256]{2,1,0:T(8,128)(2,1)S(1)}, u32[]{:S(2)}, u32[]{:S(2)}) async-start(bf16[16,256,256]{2,1,0:T(8,128)(2,1)} %shard_map.66), calls=%async_computation | async-start | bytes 4194304 | tf_op jit(solution)/shard_map/all_to_all | solution.py:307
  71.6 8.4 %collective-permute-start.10 = (bf16[32,4224]{1,0:T(8,128)(2,1)S(1)}, bf16[32,4224]{1,0:T(8,128)(2,1)S(1)}, u32[]{:S(2)}, u32[]{:S(2)}) collective-permute-start(bf16[32,4224]{1,0:T(8,128)(2,1)S(1)} %collective-permute-done.7.refs_6_), channel_id=1, source_target_pairs={{78,0},{3,1},{0,2},{5,3},{2,4},{7,5},{4,6},{9,7},{6,8},{11,9},{8,1... | collective-permute-start | bytes 811016 | tf_op jit(solution)/shard_map/ppermute | solution.py:288
  76.7 8.7 %collective-permute-start.11 = (bf16[32,4224]{1,0:T(8,128)(2,1)S(1)}, bf16[32,4224]{1,0:T(8,128)(2,1)S(1)}, u32[]{:S(2)}, u32[]{:S(2)}) collective-permute-start(bf16[32,4224]{1,0:T(8,128)(2,1)S(1)} %collective-permute-done.8.refs_7_), channel_id=1, source_target_pairs={{78,0},{3,1},{0,2},{5,3},{2,4},{7,5},{4,6},{9,7},{6,8},{11,9},{8,1... | collective-permute-start | bytes 811016 | tf_op jit(solution)/shard_map/ppermute | solution.py:286
  80.1 8.7 %collective-permute-start.12 = (bf16[32,4224]{1,0:T(8,128)(2,1)S(1)}, bf16[32,4224]{1,0:T(8,128)(2,1)S(1)}, u32[]{:S(2)}, u32[]{:S(2)}) collective-permute-start(bf16[32,4224]{1,0:T(8,128)(2,1)S(1)} %collective-permute-done.10.refs_0_), channel_id=1, source_target_pairs={{78,0},{3,1},{0,2},{5,3},{2,4},{7,5},{4,6},{9,7},{6,8},{11,9},{8,1... | collective-permute-start | bytes 811016 | tf_op jit(solution)/shard_map/ppermute | solution.py:288
  85.4 8.7 %collective-permute-start.13 = (bf16[32,4224]{1,0:T(8,128)(2,1)S(1)}, bf16[32,4224]{1,0:T(8,128)(2,1)S(1)}, u32[]{:S(2)}, u32[]{:S(2)}) collective-permute-start(bf16[32,4224]{1,0:T(8,128)(2,1)S(1)} %collective-permute-done.11.refs_1_), channel_id=1, source_target_pairs={{78,0},{3,1},{0,2},{5,3},{2,4},{7,5},{4,6},{9,7},{6,8},{11,9},{8,1... | collective-permute-start | bytes 811016 | tf_op jit(solution)/shard_map/ppermute | solution.py:286
  88.8 8.7 %collective-permute-start.14 = (bf16[32,4224]{1,0:T(8,128)(2,1)S(1)}, bf16[32,4224]{1,0:T(8,128)(2,1)S(1)}, u32[]{:S(2)}, u32[]{:S(2)}) collective-permute-start(bf16[32,4224]{1,0:T(8,128)(2,1)S(1)} %collective-permute-done.12.refs_2_), channel_id=1, source_target_pairs={{78,0},{3,1},{0,2},{5,3},{2,4},{7,5},{4,6},{9,7},{6,8},{11,9},{8,1... | collective-permute-start | bytes 811016 | tf_op jit(solution)/shard_map/ppermute | solution.py:288
  94.1 8.7 %collective-permute-start.15 = (bf16[32,4224]{1,0:T(8,128)(2,1)S(1)}, bf16[32,4224]{1,0:T(8,128)(2,1)S(1)}, u32[]{:S(2)}, u32[]{:S(2)}) collective-permute-start(bf16[32,4224]{1,0:T(8,128)(2,1)S(1)} %collective-permute-done.13.refs_3_), channel_id=1, source_target_pairs={{78,0},{3,1},{0,2},{5,3},{2,4},{7,5},{4,6},{9,7},{6,8},{11,9},{8,1... | collective-permute-start | bytes 811016 | tf_op jit(solution)/shard_map/ppermute | solution.py:286
  97.5 8.7 %collective-permute-start.16 = (bf16[32,4224]{1,0:T(8,128)(2,1)S(1)}, bf16[32,4224]{1,0:T(8,128)(2,1)S(1)}, u32[]{:S(2)}, u32[]{:S(2)}) collective-permute-start(bf16[32,4224]{1,0:T(8,128)(2,1)S(1)} %collective-permute-done.14.refs_4_), channel_id=1, source_target_pairs={{78,0},{3,1},{0,2},{5,3},{2,4},{7,5},{4,6},{9,7},{6,8},{11,9},{8,1... | collective-permute-start | bytes 811016 | tf_op jit(solution)/shard_map/ppermute | solution.py:288
  102.8 7.6 %collective-permute-start.17 = (bf16[32,4224]{1,0:T(8,128)(2,1)S(1)}, bf16[32,4224]{1,0:T(8,128)(2,1)S(1)}, u32[]{:S(2)}, u32[]{:S(2)}) collective-permute-start(bf16[32,4224]{1,0:T(8,128)(2,1)S(1)} %collective-permute-done.15.refs_5_), channel_id=1, source_target_pairs={{78,0},{3,1},{0,2},{5,3},{2,4},{7,5},{4,6},{9,7},{6,8},{11,9},{8,1... | collective-permute-start | bytes 811016 | tf_op jit(solution)/shard_map/ppermute | solution.py:286
  112.6 6.6 %copy-start.7 = (bf16[1,1024,288]{1,2,0:T(8,128)(2,1)S(1)}, bf16[1,1024,288]{1,2,0:T(8,128)(2,1)}, u32[]{:S(2)}) copy-start(bf16[1,1024,288]{1,2,0:T(8,128)(2,1)} %param.10) | copy-start | bytes 1769476
  112.6 16.7 %copy-start.11 = (s32[512,1]{1,0:T(8,128)S(1)}, s32[512,1]{1,0:T(8,128)}, u32[]{:S(2)}) copy-start(s32[512,1]{1,0:T(8,128)} %constant.18.clone.table_ref) | copy-start | bytes 6148
  112.6 29.8 %all-to-all-start.1 = ((bf16[16,256,256]{2,1,0:T(8,128)(2,1)}), bf16[16,256,256]{2,1,0:T(8,128)(2,1)}, u32[]{:S(2)}, u32[]{:S(2)}) async-start(bf16[16,256,256]{2,1,0:T(8,128)(2,1)} %shard_map.69), calls=%async_computation.1 | async-start | bytes 4194304 | tf_op jit(solution)/shard_map/all_to_all | solution.py:307
  119.2 9.3 %collective-permute-start.5 = (bf16[288,1024]{1,0:T(8,128)(2,1)S(1)}, bf16[288,1024]{1,0:T(8,128)(2,1)S(1)}, u32[]{:S(2)}, u32[]{:S(2)}) collective-permute-start(bf16[288,1024]{1,0:T(8,128)(2,1)S(1)} %bitcast.14), channel_id=1, source_target_pairs={{0,1},{1,0},{2,3},{3,2},{4,5},{5,4},{6,7},{7,6},{8,9},{9,8},{10,11... | collective-permute-start | bytes 1769480 | tf_op jit(solution)/shard_map/ppermute | solution.py:300
  128.5 0.8 copy-start.9
  129.3 1.1 copy-start.8
  130.4 1.1 copy-start.10
  133.8 1.0 copy-start.2
  134.8 1.0 copy-start.4
  135.8 2.3 %copy-start = (bf16[9216,256]{1,0:T(8,128)(2,1)S(1)}, bf16[9216,256]{1,0:T(8,128)(2,1)}, u32[]{:S(2)}) copy-start(bf16[9216,256]{1,0:T(8,128)(2,1)} %all-gather.3.cloned.1.call-done) | copy-start | bytes 14155780
  140.2 16.0 %collective-permute-start.9 = (bf16[288,256]{1,0:T(8,128)(2,1)}, bf16[288,256]{1,0:T(8,128)(2,1)S(1)}, u32[]{:S(2)}, u32[]{:S(2)}) collective-permute-start(bf16[288,256]{1,0:T(8,128)(2,1)} %get-tuple-element.20), channel_id=1, source_target_pairs={{0,1},{1,0},{2,3},{3,2},{4,5},{5,4},{6,7},{7,6},{8,9},{9,8},{10,11... | collective-permute-start | bytes 442376 | tf_op jit(solution)/shard_map/ppermute | solution.py:309
  142.5 2.3 %copy-start.1 = (bf16[9216,256]{1,0:T(8,128)(2,1)S(1)}, bf16[9216,256]{1,0:T(8,128)(2,1)}, u32[]{:S(2)}) copy-start(bf16[9216,256]{1,0:T(8,128)(2,1)} %all-gather.3.cloned.1.call-done) | copy-start | bytes 14155780
  144.8 11.4 %copy-start.3 = (bf16[512,1024]{1,0:T(8,128)(2,1)S(1)}, bf16[512,1024]{1,0:T(8,128)(2,1)}, u32[]{:S(2)}) copy-start(bf16[512,1024]{1,0:T(8,128)(2,1)} %copy-done.2) | copy-start | bytes 3145732
  144.8 11.4 %copy-start.5 = (bf16[512,1024]{1,0:T(8,128)(2,1)S(1)}, bf16[512,1024]{1,0:T(8,128)(2,1)}, u32[]{:S(2)}) copy-start(bf16[512,1024]{1,0:T(8,128)(2,1)} %copy-done.4) | copy-start | bytes 3145732
  148.0 9.2 %collective-permute-start.18 = (bf16[288,256]{1,0:T(8,128)(2,1)S(1)}, bf16[288,256]{1,0:T(8,128)(2,1)S(1)}, u32[]{:S(2)}, u32[]{:S(2)}) collective-permute-start(bf16[288,256]{1,0:T(8,128)(2,1)S(1)} %get-tuple-element.24), channel_id=1, source_target_pairs={{0,1},{1,0},{2,3},{3,2},{4,5},{5,4},{6,7},{7,6},{8,9},{9,8},{10,11... | collective-permute-start | bytes 442376 | tf_op jit(solution)/shard_map/ppermute | solution.py:309
Sparse Core Ops, SparseCore 0:
  46.1 74.8 all-gather.2

commit v4 on v3

--- a/solution.py
+++ b/solution.py
@@ -229,6 +229,45 @@
     )(core, weights, slope, rows)
 
 
+def half_kernel(core_ref, weights_ref, slope_ref, rows_ref, out_ref):
+    count = out_ref.shape[1]
+    height = count // 16
+    projected = None
+    for tile in range(weights_ref.shape[0]):
+        rows = rows_ref[:, tile * height : (tile + 1) * height, :].reshape(count, TILE)
+        part = lax.dot_general(weights_ref[tile], rows, NT, preferred_element_type=jnp.float32)
+        projected = part if projected is None else projected + part
+    out_ref[...] = (slope_ref[...] * projected).astype(jnp.bfloat16)
+
+
+def project_half(core, weights, slope, rows, first, count, other):
+    planes, hidden, _ = weights.shape
+
+    def half_of(i, core):
+        return ((1 - core[0]) if other else core[0], 0, 0)
+
+    return pl.pallas_call(
+        half_kernel,
+        out_shape=jax.ShapeDtypeStruct((hidden, count), jnp.bfloat16),
+        grid_spec=pltpu.PrefetchScalarGridSpec(
+            num_scalar_prefetch=1,
+            grid=(1,),
+            in_specs=[
+                pl.BlockSpec((planes // 2, hidden, TILE), half_of),
+                pl.BlockSpec((hidden, count), lambda i, core: (int(other), first // count)),
+                pl.BlockSpec(rows.shape, lambda i, core: (0, 0, 0)),
+            ],
+            out_specs=pl.BlockSpec((hidden, count), lambda i, core: (0, 0)),
+        ),
+        compiler_params=params(24),
+        cost_estimate=pl.CostEstimate(
+            flops=hidden * planes * TILE * count,
+            bytes_accessed=weights.size + 2 * rows.size,
+            transcendentals=0,
+        ),
+    )(core, weights, slope, rows)
+
+
 def place_kernel(first, *refs):
     here_ref, there_ref, here_place_ref, there_place_ref = refs[-5:-1]
     out_ref = refs[-1]
@@ -305,8 +344,13 @@
     for count in GROUPS:
         outgoing = dispatch(chunks[first : first + count], zhi_at, width)
         received = lax.all_to_all(outgoing, PLANE, split_axis=0, concat_axis=0, tiled=True)
-        here, there = project(core_at, weights, slope, received, first * IMG, count * IMG)
-        there = lax.ppermute(there, "core", swap)
+        at = (core_at, weights, slope, received, first * IMG, count * IMG)
+        if first == 0:
+            here, there = project(*at)
+            there = lax.ppermute(there, "core", swap)
+        else:
+            there = lax.ppermute(project_half(*at, True), "core", swap)
+            here = project_half(*at, False)
         placed = [put(here, there, here_place, there_place, first * IMG, placed)]
         first += count
     return placed[0].T[None]

time: 166 us -> 167 us (level)
  local copies, waits for them, and re-layouts: 10.5 us -> 14.9 us
  Pallas kernels: 16.8 us -> 14.8 us
  starting transfers between devices: 101 us -> 99 us
    ppermute x2 -> x1, starting transfers between devices: 10.5 us -> 2.27 us  [shards(): there = lax.ppermute(there, 'core', swap)]
    ppermute x0 -> x1, starting transfers between devices: none -> 6.66 us  [shards(): there = lax.ppermute(project_half(*at, True), 'core', swap)]
    unnamed x26 -> x32, local copies, waits for them, and re-layouts: 10.5 us -> 14.9 us
    pallas_call x2 -> x1, Pallas kernels: 5.23 us -> 2.08 us  [project(): pl.pallas_call(functools.partial(project_kernel, first), out_shape=(half,...]
  transfers between devices with their start and end apart: 22 -> 22, of which waited for: 12 -> 11; matrix products, arithmetic and copies ran while one was open for 0% -> 0% of each run, Pallas kernels for 8% -> 6%
where the time goes in v4:
time: 167 us; the launch traced here: 166 us
  starting transfers between devices  99 us (59%)
  waiting for transfers between devices  22.3 us (13%)
  local copies, waits for them, and re-layouts  14.9 us (9%)
  Pallas kernels  14.8 us (9%)
  between operations  13.8 us (8%)
    ppermute x8, starting transfers between devices, shards(): kept.append(lax.ppermute(kept[-1], RING, ring_pairs(False)))  30 us
    ppermute x7, starting transfers between devices, shards(): crossed.append(lax.ppermute(crossed[-1], RING, ring_pairs(step == 1)))  29.7 us
    unnamed x32, local copies, waits for them, and re-layouts  14.9 us
    all_to_all x2, starting transfers between devices, shards(): lax.all_to_all(outgoing, PLANE, split_axis=0, concat_axis=0, tiled=True)  13.1 us
    ppermute x8, waiting for transfers between devices, shards(): kept.append(lax.ppermute(kept[-1], RING, ring_pairs(False)))  11.8 us
    ppermute x1, starting transfers between devices, shards(): other = lax.ppermute(w_proj, 'zhi', swap)  9.45 us
    ppermute x7, waiting for transfers between devices, shards(): crossed.append(lax.ppermute(crossed[-1], RING, ring_pairs(step == 1)))  8.16 us
    ppermute x1, starting transfers between devices, shards(): lax.ppermute(pre, 'core', swap)  7.71 us
  transfers between devices with their start and end apart: 22, of which 11 were waited for; matrix products, arithmetic and copies ran while one was open for 0% of the time, Pallas kernels for 6%

profile of v4, /device:TPU:1, one launch (start us, length us, event | category | flops | bytes accessed | tf_op | source)
XLA Modules:
  0.0 165.6 jit_solution(2910851107796844540)
XLA Ops:
  6.5 3.1 %shard_map.64.refs_0_ = bf16[32,4224]{1,0:T(8,128)(2,1)} custom-call(s32[1,32]{1,0:T(1,128)} %bitcast.17, s32[1,32]{1,0:T(1,128)} %bitcast.18, bf16[256,4096]{1,0:T(8,128)(2,1)} %hidden_hbm.1), custom_call_target="tpu_custom_call" | custom-call | flops 67108864 | bytes 2097152 | tf_op jit(solution)/shard_map/pallas_call | solution.py:84
  9.6 4.9 %collective-permute-start.2 = (bf16[32,4224]{1,0:T(8,128)(2,1)}, bf16[32,4224]{1,0:T(8,128)(2,1)S(1)}, u32[]{:S(2)}, u32[]{:S(2)}) collective-permute-start(bf16[32,4224]{1,0:T(8,128)(2,1)} %shard_map.64.refs_0_), channel_id=1, source_target_pairs={{79,0},{2,1},{1,2},{4,3},{3,4},{6,5},{5,6},{8,7},{7,8},{10,9},{9,1... | collective-permute-start | bytes 811016 | tf_op jit(solution)/shard_map/ppermute | solution.py:327
  14.5 8.9 %collective-permute-start = (bf16[32,4224]{1,0:T(8,128)(2,1)}, bf16[32,4224]{1,0:T(8,128)(2,1)S(1)}, u32[]{:S(2)}, u32[]{:S(2)}) collective-permute-start(bf16[32,4224]{1,0:T(8,128)(2,1)} %shard_map.64.refs_0_), channel_id=1, source_target_pairs={{78,0},{3,1},{0,2},{5,3},{2,4},{7,5},{4,6},{9,7},{6,8},{11,9},{8,1... | collective-permute-start | bytes 811016 | tf_op jit(solution)/shard_map/ppermute | solution.py:325
  23.5 9.5 %collective-permute-start.4 = (bf16[288,128]{1,0:T(8,128)(2,1)S(1)}, bf16[288,128]{1,0:T(8,128)(2,1)S(1)}, u32[]{:S(2)}, u32[]{:S(2)}) collective-permute-start(bf16[288,128]{1,0:T(8,128)(2,1)S(1)} %copy-done.15), channel_id=1, source_target_pairs={{0,64},{64,0},{1,65},{65,1},{2,66},{66,2},{3,67},{67,3},{4,68},{68... | collective-permute-start | bytes 221192 | tf_op jit(solution)/shard_map/ppermute | solution.py:318
  33.0 1.9 %collective-permute-start.3 = (bf16[32,4224]{1,0:T(8,128)(2,1)S(1)}, bf16[32,4224]{1,0:T(8,128)(2,1)S(1)}, u32[]{:S(2)}, u32[]{:S(2)}) collective-permute-start(bf16[32,4224]{1,0:T(8,128)(2,1)S(1)} %collective-permute-done.2.refs_2_), channel_id=1, source_target_pairs={{78,0},{3,1},{0,2},{5,3},{2,4},{7,5},{4,6},{9,7},{6,8},{11,9},{8,1... | collective-permute-start | bytes 811016 | tf_op jit(solution)/shard_map/ppermute | solution.py:327
  34.9 1.9 %collective-permute-start.1 = (bf16[32,4224]{1,0:T(8,128)(2,1)S(1)}, bf16[32,4224]{1,0:T(8,128)(2,1)S(1)}, u32[]{:S(2)}, u32[]{:S(2)}) collective-permute-start(bf16[32,4224]{1,0:T(8,128)(2,1)S(1)} %collective-permute-done.refs_1_), channel_id=1, source_target_pairs={{78,0},{3,1},{0,2},{5,3},{2,4},{7,5},{4,6},{9,7},{6,8},{11,9},{8,1... | collective-permute-start | bytes 811016 | tf_op jit(solution)/shard_map/ppermute | solution.py:325
  36.8 0.9 collective-permute-done.4
  38.4 4.9 %collective-permute-done.3.refs_4_ = bf16[32,4224]{1,0:T(8,128)(2,1)S(1)} collective-permute-done((bf16[32,4224]{1,0:T(8,128)(2,1)S(1)}, bf16[32,4224]{1,0:T(8,128)(2,1)S(1)}, u32[]{:S(2)}, u32[]{:S(2)}) %collective-permute-start.3) | collective-permute-done | bytes 270368 | tf_op jit(solution)/shard_map/ppermute | solution.py:327
  43.3 2.6 %collective-permute-done.1.refs_3_ = bf16[32,4224]{1,0:T(8,128)(2,1)S(1)} collective-permute-done((bf16[32,4224]{1,0:T(8,128)(2,1)S(1)}, bf16[32,4224]{1,0:T(8,128)(2,1)S(1)}, u32[]{:S(2)}, u32[]{:S(2)}) %collective-permute-start.1) | collective-permute-done | bytes 270368 | tf_op jit(solution)/shard_map/ppermute | solution.py:325
  46.0 4.0 %collective-permute-start.6 = (bf16[32,4224]{1,0:T(8,128)(2,1)S(1)}, bf16[32,4224]{1,0:T(8,128)(2,1)S(1)}, u32[]{:S(2)}, u32[]{:S(2)}) collective-permute-start(bf16[32,4224]{1,0:T(8,128)(2,1)S(1)} %collective-permute-done.1.refs_3_), channel_id=1, source_target_pairs={{78,0},{3,1},{0,2},{5,3},{2,4},{7,5},{4,6},{9,7},{6,8},{11,9},{8,1... | collective-permute-start | bytes 811016 | tf_op jit(solution)/shard_map/ppermute | solution.py:325
  50.0 1.9 %collective-permute-start.7 = (bf16[32,4224]{1,0:T(8,128)(2,1)S(1)}, bf16[32,4224]{1,0:T(8,128)(2,1)S(1)}, u32[]{:S(2)}, u32[]{:S(2)}) collective-permute-start(bf16[32,4224]{1,0:T(8,128)(2,1)S(1)} %collective-permute-done.3.refs_4_), channel_id=1, source_target_pairs={{78,0},{3,1},{0,2},{5,3},{2,4},{7,5},{4,6},{9,7},{6,8},{11,9},{8,1... | collective-permute-start | bytes 811016 | tf_op jit(solution)/shard_map/ppermute | solution.py:327
  51.9 1.6 collective-permute-done.6.refs_5_
  53.5 4.9 %collective-permute-start.8 = (bf16[32,4224]{1,0:T(8,128)(2,1)S(1)}, bf16[32,4224]{1,0:T(8,128)(2,1)S(1)}, u32[]{:S(2)}, u32[]{:S(2)}) collective-permute-start(bf16[32,4224]{1,0:T(8,128)(2,1)S(1)} %collective-permute-done.6.refs_5_), channel_id=1, source_target_pairs={{78,0},{3,1},{0,2},{5,3},{2,4},{7,5},{4,6},{9,7},{6,8},{11,9},{8,1... | collective-permute-start | bytes 811016 | tf_op jit(solution)/shard_map/ppermute | solution.py:325
  58.4 3.4 %collective-permute-done.8.refs_7_ = bf16[32,4224]{1,0:T(8,128)(2,1)S(1)} collective-permute-done((bf16[32,4224]{1,0:T(8,128)(2,1)S(1)}, bf16[32,4224]{1,0:T(8,128)(2,1)S(1)}, u32[]{:S(2)}, u32[]{:S(2)}) %collective-permute-start.8) | collective-permute-done | bytes 270368 | tf_op jit(solution)/shard_map/ppermute | solution.py:325
  61.8 1.0 copy-done.9
  62.7 2.2 %shard_map.66 = bf16[16,256,256]{2,1,0:T(8,128)(2,1)} custom-call(s32[1]{0:T(128)} %bitcast.8.zhi_ref, bf16[32,4224]{1,0:T(8,128)(2,1)S(1)} %copy-done.9, bf16[32,4224]{1,0:T(8,128)(2,1)S(1)} %collective-permute-done.refs_1_, bf16[32,4224]{1,0:T(8,128)(2,1)S(1)} %collective-permute-done.2.refs_2_, bf16[32,4224]{1,0:T(8,128)(2,1)S(1)} %collective-permute-done.1.refs_3_, ...), custom_call_target="tpu_custom_call" | custom-call | flops 268435456 | bytes 2097152 | tf_op jit(solution)/shard_map/pallas_call | solution.py:130
  64.9 6.8 %all-to-all-start = ((bf16[16,256,256]{2,1,0:T(8,128)(2,1)}), bf16[16,256,256]{2,1,0:T(8,128)(2,1)S(1)}, u32[]{:S(2)}, u32[]{:S(2)}) async-start(bf16[16,256,256]{2,1,0:T(8,128)(2,1)} %shard_map.66), calls=%async_computation | async-start | bytes 4194304 | tf_op jit(solution)/shard_map/all_to_all | solution.py:346
  71.7 5.0 %collective-permute-start.10 = (bf16[32,4224]{1,0:T(8,128)(2,1)S(1)}, bf16[32,4224]{1,0:T(8,128)(2,1)S(1)}, u32[]{:S(2)}, u32[]{:S(2)}) collective-permute-start(bf16[32,4224]{1,0:T(8,128)(2,1)S(1)} %collective-permute-done.7.refs_6_), channel_id=1, source_target_pairs={{78,0},{3,1},{0,2},{5,3},{2,4},{7,5},{4,6},{9,7},{6,8},{11,9},{8,1... | collective-permute-start | bytes 811016 | tf_op jit(solution)/shard_map/ppermute | solution.py:327
  76.7 1.9 %collective-permute-start.11 = (bf16[32,4224]{1,0:T(8,128)(2,1)S(1)}, bf16[32,4224]{1,0:T(8,128)(2,1)S(1)}, u32[]{:S(2)}, u32[]{:S(2)}) collective-permute-start(bf16[32,4224]{1,0:T(8,128)(2,1)S(1)} %collective-permute-done.8.refs_7_), channel_id=1, source_target_pairs={{78,0},{3,1},{0,2},{5,3},{2,4},{7,5},{4,6},{9,7},{6,8},{11,9},{8,1... | collective-permute-start | bytes 811016 | tf_op jit(solution)/shard_map/ppermute | solution.py:325
  78.7 1.5 collective-permute-done.10.refs_0_
  80.1 5.3 %collective-permute-start.12 = (bf16[32,4224]{1,0:T(8,128)(2,1)S(1)}, bf16[32,4224]{1,0:T(8,128)(2,1)S(1)}, u32[]{:S(2)}, u32[]{:S(2)}) collective-permute-start(bf16[32,4224]{1,0:T(8,128)(2,1)S(1)} %collective-permute-done.10.refs_0_), channel_id=1, source_target_pairs={{78,0},{3,1},{0,2},{5,3},{2,4},{7,5},{4,6},{9,7},{6,8},{11,9},{8,1... | collective-permute-start | bytes 811016 | tf_op jit(solution)/shard_map/ppermute | solution.py:327
  85.4 2.9 %collective-permute-start.13 = (bf16[32,4224]{1,0:T(8,128)(2,1)S(1)}, bf16[32,4224]{1,0:T(8,128)(2,1)S(1)}, u32[]{:S(2)}, u32[]{:S(2)}) collective-permute-start(bf16[32,4224]{1,0:T(8,128)(2,1)S(1)} %collective-permute-done.11.refs_1_), channel_id=1, source_target_pairs={{78,0},{3,1},{0,2},{5,3},{2,4},{7,5},{4,6},{9,7},{6,8},{11,9},{8,1... | collective-permute-start | bytes 811016 | tf_op jit(solution)/shard_map/ppermute | solution.py:325
  88.8 5.3 %collective-permute-start.14 = (bf16[32,4224]{1,0:T(8,128)(2,1)S(1)}, bf16[32,4224]{1,0:T(8,128)(2,1)S(1)}, u32[]{:S(2)}, u32[]{:S(2)}) collective-permute-start(bf16[32,4224]{1,0:T(8,128)(2,1)S(1)} %collective-permute-done.12.refs_2_), channel_id=1, source_target_pairs={{78,0},{3,1},{0,2},{5,3},{2,4},{7,5},{4,6},{9,7},{6,8},{11,9},{8,1... | collective-permute-start | bytes 811016 | tf_op jit(solution)/shard_map/ppermute | solution.py:327
  94.1 2.9 %collective-permute-start.15 = (bf16[32,4224]{1,0:T(8,128)(2,1)S(1)}, bf16[32,4224]{1,0:T(8,128)(2,1)S(1)}, u32[]{:S(2)}, u32[]{:S(2)}) collective-permute-start(bf16[32,4224]{1,0:T(8,128)(2,1)S(1)} %collective-permute-done.13.refs_3_), channel_id=1, source_target_pairs={{78,0},{3,1},{0,2},{5,3},{2,4},{7,5},{4,6},{9,7},{6,8},{11,9},{8,1... | collective-permute-start | bytes 811016 | tf_op jit(solution)/shard_map/ppermute | solution.py:325
  97.5 5.3 %collective-permute-start.16 = (bf16[32,4224]{1,0:T(8,128)(2,1)S(1)}, bf16[32,4224]{1,0:T(8,128)(2,1)S(1)}, u32[]{:S(2)}, u32[]{:S(2)}) collective-permute-start(bf16[32,4224]{1,0:T(8,128)(2,1)S(1)} %collective-permute-done.14.refs_4_), channel_id=1, source_target_pairs={{78,0},{3,1},{0,2},{5,3},{2,4},{7,5},{4,6},{9,7},{6,8},{11,9},{8,1... | collective-permute-start | bytes 811016 | tf_op jit(solution)/shard_map/ppermute | solution.py:327
  102.8 2.6 %collective-permute-start.17 = (bf16[32,4224]{1,0:T(8,128)(2,1)S(1)}, bf16[32,4224]{1,0:T(8,128)(2,1)S(1)}, u32[]{:S(2)}, u32[]{:S(2)}) collective-permute-start(bf16[32,4224]{1,0:T(8,128)(2,1)S(1)} %collective-permute-done.15.refs_5_), channel_id=1, source_target_pairs={{78,0},{3,1},{0,2},{5,3},{2,4},{7,5},{4,6},{9,7},{6,8},{11,9},{8,1... | collective-permute-start | bytes 811016 | tf_op jit(solution)/shard_map/ppermute | solution.py:325
  106.2 4.2 %collective-permute-done.17.refs_7_ = bf16[32,4224]{1,0:T(8,128)(2,1)S(1)} collective-permute-done((bf16[32,4224]{1,0:T(8,128)(2,1)S(1)}, bf16[32,4224]{1,0:T(8,128)(2,1)S(1)}, u32[]{:S(2)}, u32[]{:S(2)}) %collective-permute-start.17) | collective-permute-done | bytes 270368 | tf_op jit(solution)/shard_map/ppermute | solution.py:325
  110.4 0.8 shard_map.69
  111.3 1.4 copy-done.2
  112.7 1.4 copy-done.3
  114.0 6.4 %all-to-all-start.1 = ((bf16[16,256,256]{2,1,0:T(8,128)(2,1)}), bf16[16,256,256]{2,1,0:T(8,128)(2,1)S(1)}, u32[]{:S(2)}, u32[]{:S(2)}) async-start(bf16[16,256,256]{2,1,0:T(8,128)(2,1)} %copy-done.2), calls=%async_computation.1 | async-start | bytes 4194304 | tf_op jit(solution)/shard_map/all_to_all | solution.py:346
  120.4 7.7 %collective-permute-start.5 = (bf16[288,1024]{1,0:T(8,128)(2,1)S(1)}, bf16[288,1024]{1,0:T(8,128)(2,1)S(1)}, u32[]{:S(2)}, u32[]{:S(2)}) collective-permute-start(bf16[288,1024]{1,0:T(8,128)(2,1)S(1)} %bitcast.15), channel_id=1, source_target_pairs={{0,1},{1,0},{2,3},{3,2},{4,5},{5,4},{6,7},{7,6},{8,9},{9,8},{10,11... | collective-permute-start | bytes 1769480 | tf_op jit(solution)/shard_map/ppermute | solution.py:339
  128.2 1.5 collective-permute-done.5.pre_other_ref
  129.7 0.8 copy-done.12
  130.6 1.1 copy-done.11
  131.6 1.1 copy-done.13
  132.7 2.4 %shard_map.65 = (f32[576,512]{1,0:T(8,128)S(1)}, bf16[512,1024]{1,0:T(8,128)(2,1)S(1)}, bf16[512,1024]{1,0:T(8,128)(2,1)S(1)}) custom-call(s32[2]{0:T(128)S(1)} %pad_add_fusion.at_ref, s32[512,1]{1,0:T(8,128)S(1)} %copy-done.14, bf16[288,1024]{1,0:T(8,128)(2,1)S(1)} %bitcast.16, bf16[288,1024]{1,0:T(8,128)(2,1)S(1)} %copy-done.13), custom_call_target="tpu_custom_call" | custom-call | flops 603979776 | bytes 4194304 | tf_op jit(solution)/shard_map/pallas_call | solution.py:185
  135.1 1.0 copy-done.5
  136.0 1.0 copy-done.7
  137.0 2.3 %copy-done = bf16[9216,256]{1,0:T(8,128)(2,1)S(1)} copy-done((bf16[9216,256]{1,0:T(8,128)(2,1)S(1)}, bf16[9216,256]{1,0:T(8,128)(2,1)}, u32[]{:S(2)}) %copy-start) | copy-done | bytes 4718616
  139.4 1.6 copy-done.4
  141.0 2.1 %shard_map.67 = (bf16[288,256]{1,0:T(8,128)(2,1)S(1)}, bf16[288,256]{1,0:T(8,128)(2,1)}) custom-call(s32[1]{0:T(128)} %bitcast.core_ref, bf16[32,288,256]{2,1,0:T(8,128)(2,1)S(1)} %bitcast.12, f32[576,512]{1,0:T(8,128)S(1)} %get-tuple-element.14.slope_ref, bf16[16,256,256]{2,1,0:T(8,128)(2,1)S(1)} %copy-done.4), custom_call_target="tpu_custom_call" | custom-call | flops 1207959552 | bytes 4718592 | tf_op jit(solution)/shard_map/pallas_call | solution.py:218
  143.0 2.3 %collective-permute-start.9 = (bf16[288,256]{1,0:T(8,128)(2,1)}, bf16[288,256]{1,0:T(8,128)(2,1)}, u32[]{:S(2)}, u32[]{:S(2)}) collective-permute-start(bf16[288,256]{1,0:T(8,128)(2,1)} %get-tuple-element.18), channel_id=1, source_target_pairs={{0,1},{1,0},{2,3},{3,2},{4,5},{5,4},{6,7},{7,6},{8,9},{9,8},{10,11... | collective-permute-start | bytes 442376 | tf_op jit(solution)/shard_map/ppermute | solution.py:350
  145.3 2.3 %copy-done.1 = bf16[9216,256]{1,0:T(8,128)(2,1)S(1)} copy-done((bf16[9216,256]{1,0:T(8,128)(2,1)S(1)}, bf16[9216,256]{1,0:T(8,128)(2,1)}, u32[]{:S(2)}) %copy-start.1) | copy-done | bytes 4718616
  148.5 6.7 %collective-permute-start.18 = (bf16[288,256]{1,0:T(8,128)(2,1)S(1)}, bf16[288,256]{1,0:T(8,128)(2,1)S(1)}, u32[]{:S(2)}, u32[]{:S(2)}) collective-permute-start(bf16[288,256]{1,0:T(8,128)(2,1)S(1)} %shard_map.71), channel_id=1, source_target_pairs={{0,1},{1,0},{2,3},{3,2},{4,5},{5,4},{6,7},{7,6},{8,9},{9,8},{10,11... | collective-permute-start | bytes 442376 | tf_op jit(solution)/shard_map/ppermute | solution.py:352
  155.2 0.8 shard_map.70.refs_1_
  156.0 1.4 shard_map.68.refs_0_
  157.4 1.3 shard_map.72
  (41 shorter events, 3.4 us)
Async XLA Ops:
  6.5 17.0 %copy-start.15 = (bf16[288,128]{1,0:T(8,128)(2,1)S(1)}, bf16[288,128]{1,0:T(8,128)(2,1)}, u32[]{:S(2)}) copy-start(bf16[288,128]{1,0:T(8,128)(2,1)} %param.9) | copy-start | bytes 221188
  6.5 130.5 %all-gather.3.cloned.1.call-start = ((), (), s32[]{:S(2)}) async-start(), calls=%async_computation.2 | async-start | bytes 4866048 | tf_op jit(solution)/shard_map/all_gather | solution.py:330
  9.6 23.4 %collective-permute-start.2 = (bf16[32,4224]{1,0:T(8,128)(2,1)}, bf16[32,4224]{1,0:T(8,128)(2,1)S(1)}, u32[]{:S(2)}, u32[]{:S(2)}) collective-permute-start(bf16[32,4224]{1,0:T(8,128)(2,1)} %shard_map.64.refs_0_), channel_id=1, source_target_pairs={{79,0},{2,1},{1,2},{4,3},{3,4},{6,5},{5,6},{8,7},{7,8},{10,9},{9,1... | collective-permute-start | bytes 811016 | tf_op jit(solution)/shard_map/ppermute | solution.py:327
  14.5 20.4 %collective-permute-start = (bf16[32,4224]{1,0:T(8,128)(2,1)}, bf16[32,4224]{1,0:T(8,128)(2,1)S(1)}, u32[]{:S(2)}, u32[]{:S(2)}) collective-permute-start(bf16[32,4224]{1,0:T(8,128)(2,1)} %shard_map.64.refs_0_), channel_id=1, source_target_pairs={{78,0},{3,1},{0,2},{5,3},{2,4},{7,5},{4,6},{9,7},{6,8},{11,9},{8,1... | collective-permute-start | bytes 811016 | tf_op jit(solution)/shard_map/ppermute | solution.py:325
  23.5 14.2 %collective-permute-start.4 = (bf16[288,128]{1,0:T(8,128)(2,1)S(1)}, bf16[288,128]{1,0:T(8,128)(2,1)S(1)}, u32[]{:S(2)}, u32[]{:S(2)}) collective-permute-start(bf16[288,128]{1,0:T(8,128)(2,1)S(1)} %copy-done.15), channel_id=1, source_target_pairs={{0,64},{64,0},{1,65},{65,1},{2,66},{66,2},{3,67},{67,3},{4,68},{68... | collective-permute-start | bytes 221192 | tf_op jit(solution)/shard_map/ppermute | solution.py:318
  33.0 10.4 %collective-permute-start.3 = (bf16[32,4224]{1,0:T(8,128)(2,1)S(1)}, bf16[32,4224]{1,0:T(8,128)(2,1)S(1)}, u32[]{:S(2)}, u32[]{:S(2)}) collective-permute-start(bf16[32,4224]{1,0:T(8,128)(2,1)S(1)} %collective-permute-done.2.refs_2_), channel_id=1, source_target_pairs={{78,0},{3,1},{0,2},{5,3},{2,4},{7,5},{4,6},{9,7},{6,8},{11,9},{8,1... | collective-permute-start | bytes 811016 | tf_op jit(solution)/shard_map/ppermute | solution.py:327
  34.9 11.0 %collective-permute-start.1 = (bf16[32,4224]{1,0:T(8,128)(2,1)S(1)}, bf16[32,4224]{1,0:T(8,128)(2,1)S(1)}, u32[]{:S(2)}, u32[]{:S(2)}) collective-permute-start(bf16[32,4224]{1,0:T(8,128)(2,1)S(1)} %collective-permute-done.refs_1_), channel_id=1, source_target_pairs={{78,0},{3,1},{0,2},{5,3},{2,4},{7,5},{4,6},{9,7},{6,8},{11,9},{8,1... | collective-permute-start | bytes 811016 | tf_op jit(solution)/shard_map/ppermute | solution.py:325
  46.0 7.5 %collective-permute-start.6 = (bf16[32,4224]{1,0:T(8,128)(2,1)S(1)}, bf16[32,4224]{1,0:T(8,128)(2,1)S(1)}, u32[]{:S(2)}, u32[]{:S(2)}) collective-permute-start(bf16[32,4224]{1,0:T(8,128)(2,1)S(1)} %collective-permute-done.1.refs_3_), channel_id=1, source_target_pairs={{78,0},{3,1},{0,2},{5,3},{2,4},{7,5},{4,6},{9,7},{6,8},{11,9},{8,1... | collective-permute-start | bytes 811016 | tf_op jit(solution)/shard_map/ppermute | solution.py:325
  50.0 8.4 %collective-permute-start.7 = (bf16[32,4224]{1,0:T(8,128)(2,1)S(1)}, bf16[32,4224]{1,0:T(8,128)(2,1)S(1)}, u32[]{:S(2)}, u32[]{:S(2)}) collective-permute-start(bf16[32,4224]{1,0:T(8,128)(2,1)S(1)} %collective-permute-done.3.refs_4_), channel_id=1, source_target_pairs={{78,0},{3,1},{0,2},{5,3},{2,4},{7,5},{4,6},{9,7},{6,8},{11,9},{8,1... | collective-permute-start | bytes 811016 | tf_op jit(solution)/shard_map/ppermute | solution.py:327
  53.5 8.3 %collective-permute-start.8 = (bf16[32,4224]{1,0:T(8,128)(2,1)S(1)}, bf16[32,4224]{1,0:T(8,128)(2,1)S(1)}, u32[]{:S(2)}, u32[]{:S(2)}) collective-permute-start(bf16[32,4224]{1,0:T(8,128)(2,1)S(1)} %collective-permute-done.6.refs_5_), channel_id=1, source_target_pairs={{78,0},{3,1},{0,2},{5,3},{2,4},{7,5},{4,6},{9,7},{6,8},{11,9},{8,1... | collective-permute-start | bytes 811016 | tf_op jit(solution)/shard_map/ppermute | solution.py:325
  61.8 1.0 copy-start.9
  64.9 47.7 %all-to-all-start = ((bf16[16,256,256]{2,1,0:T(8,128)(2,1)}), bf16[16,256,256]{2,1,0:T(8,128)(2,1)S(1)}, u32[]{:S(2)}, u32[]{:S(2)}) async-start(bf16[16,256,256]{2,1,0:T(8,128)(2,1)} %shard_map.66), calls=%async_computation | async-start | bytes 4194304 | tf_op jit(solution)/shard_map/all_to_all | solution.py:346
  71.7 8.4 %collective-permute-start.10 = (bf16[32,4224]{1,0:T(8,128)(2,1)S(1)}, bf16[32,4224]{1,0:T(8,128)(2,1)S(1)}, u32[]{:S(2)}, u32[]{:S(2)}) collective-permute-start(bf16[32,4224]{1,0:T(8,128)(2,1)S(1)} %collective-permute-done.7.refs_6_), channel_id=1, source_target_pairs={{78,0},{3,1},{0,2},{5,3},{2,4},{7,5},{4,6},{9,7},{6,8},{11,9},{8,1... | collective-permute-start | bytes 811016 | tf_op jit(solution)/shard_map/ppermute | solution.py:327
  76.7 8.7 %collective-permute-start.11 = (bf16[32,4224]{1,0:T(8,128)(2,1)S(1)}, bf16[32,4224]{1,0:T(8,128)(2,1)S(1)}, u32[]{:S(2)}, u32[]{:S(2)}) collective-permute-start(bf16[32,4224]{1,0:T(8,128)(2,1)S(1)} %collective-permute-done.8.refs_7_), channel_id=1, source_target_pairs={{78,0},{3,1},{0,2},{5,3},{2,4},{7,5},{4,6},{9,7},{6,8},{11,9},{8,1... | collective-permute-start | bytes 811016 | tf_op jit(solution)/shard_map/ppermute | solution.py:325
  80.1 8.7 %collective-permute-start.12 = (bf16[32,4224]{1,0:T(8,128)(2,1)S(1)}, bf16[32,4224]{1,0:T(8,128)(2,1)S(1)}, u32[]{:S(2)}, u32[]{:S(2)}) collective-permute-start(bf16[32,4224]{1,0:T(8,128)(2,1)S(1)} %collective-permute-done.10.refs_0_), channel_id=1, source_target_pairs={{78,0},{3,1},{0,2},{5,3},{2,4},{7,5},{4,6},{9,7},{6,8},{11,9},{8,1... | collective-permute-start | bytes 811016 | tf_op jit(solution)/shard_map/ppermute | solution.py:327
  85.4 8.7 %collective-permute-start.13 = (bf16[32,4224]{1,0:T(8,128)(2,1)S(1)}, bf16[32,4224]{1,0:T(8,128)(2,1)S(1)}, u32[]{:S(2)}, u32[]{:S(2)}) collective-permute-start(bf16[32,4224]{1,0:T(8,128)(2,1)S(1)} %collective-permute-done.11.refs_1_), channel_id=1, source_target_pairs={{78,0},{3,1},{0,2},{5,3},{2,4},{7,5},{4,6},{9,7},{6,8},{11,9},{8,1... | collective-permute-start | bytes 811016 | tf_op jit(solution)/shard_map/ppermute | solution.py:325
  88.8 8.7 %collective-permute-start.14 = (bf16[32,4224]{1,0:T(8,128)(2,1)S(1)}, bf16[32,4224]{1,0:T(8,128)(2,1)S(1)}, u32[]{:S(2)}, u32[]{:S(2)}) collective-permute-start(bf16[32,4224]{1,0:T(8,128)(2,1)S(1)} %collective-permute-done.12.refs_2_), channel_id=1, source_target_pairs={{78,0},{3,1},{0,2},{5,3},{2,4},{7,5},{4,6},{9,7},{6,8},{11,9},{8,1... | collective-permute-start | bytes 811016 | tf_op jit(solution)/shard_map/ppermute | solution.py:327
  94.1 8.7 %collective-permute-start.15 = (bf16[32,4224]{1,0:T(8,128)(2,1)S(1)}, bf16[32,4224]{1,0:T(8,128)(2,1)S(1)}, u32[]{:S(2)}, u32[]{:S(2)}) collective-permute-start(bf16[32,4224]{1,0:T(8,128)(2,1)S(1)} %collective-permute-done.13.refs_3_), channel_id=1, source_target_pairs={{78,0},{3,1},{0,2},{5,3},{2,4},{7,5},{4,6},{9,7},{6,8},{11,9},{8,1... | collective-permute-start | bytes 811016 | tf_op jit(solution)/shard_map/ppermute | solution.py:325
  97.5 8.7 %collective-permute-start.16 = (bf16[32,4224]{1,0:T(8,128)(2,1)S(1)}, bf16[32,4224]{1,0:T(8,128)(2,1)S(1)}, u32[]{:S(2)}, u32[]{:S(2)}) collective-permute-start(bf16[32,4224]{1,0:T(8,128)(2,1)S(1)} %collective-permute-done.14.refs_4_), channel_id=1, source_target_pairs={{78,0},{3,1},{0,2},{5,3},{2,4},{7,5},{4,6},{9,7},{6,8},{11,9},{8,1... | collective-permute-start | bytes 811016 | tf_op jit(solution)/shard_map/ppermute | solution.py:327
  102.8 7.6 %collective-permute-start.17 = (bf16[32,4224]{1,0:T(8,128)(2,1)S(1)}, bf16[32,4224]{1,0:T(8,128)(2,1)S(1)}, u32[]{:S(2)}, u32[]{:S(2)}) collective-permute-start(bf16[32,4224]{1,0:T(8,128)(2,1)S(1)} %collective-permute-done.15.refs_5_), channel_id=1, source_target_pairs={{78,0},{3,1},{0,2},{5,3},{2,4},{7,5},{4,6},{9,7},{6,8},{11,9},{8,1... | collective-permute-start | bytes 811016 | tf_op jit(solution)/shard_map/ppermute | solution.py:325
  111.3 1.4 copy-start.2
  112.6 7.8 %copy-start.10 = (bf16[1,1024,288]{1,2,0:T(8,128)(2,1)S(1)}, bf16[1,1024,288]{1,2,0:T(8,128)(2,1)}, u32[]{:S(2)}) copy-start(bf16[1,1024,288]{1,2,0:T(8,128)(2,1)} %param.10) | copy-start | bytes 1769476
  112.6 17.9 %copy-start.14 = (s32[512,1]{1,0:T(8,128)S(1)}, s32[512,1]{1,0:T(8,128)}, u32[]{:S(2)}) copy-start(s32[512,1]{1,0:T(8,128)} %constant.18.clone.table_ref) | copy-start | bytes 6148
  112.6 1.4 copy-start.3
  114.0 31.3 %all-to-all-start.1 = ((bf16[16,256,256]{2,1,0:T(8,128)(2,1)}), bf16[16,256,256]{2,1,0:T(8,128)(2,1)S(1)}, u32[]{:S(2)}, u32[]{:S(2)}) async-start(bf16[16,256,256]{2,1,0:T(8,128)(2,1)} %copy-done.2), calls=%async_computation.1 | async-start | bytes 4194304 | tf_op jit(solution)/shard_map/all_to_all | solution.py:346
  120.4 9.3 %collective-permute-start.5 = (bf16[288,1024]{1,0:T(8,128)(2,1)S(1)}, bf16[288,1024]{1,0:T(8,128)(2,1)S(1)}, u32[]{:S(2)}, u32[]{:S(2)}) collective-permute-start(bf16[288,1024]{1,0:T(8,128)(2,1)S(1)} %bitcast.15), channel_id=1, source_target_pairs={{0,1},{1,0},{2,3},{3,2},{4,5},{5,4},{6,7},{7,6},{8,9},{9,8},{10,11... | collective-permute-start | bytes 1769480 | tf_op jit(solution)/shard_map/ppermute | solution.py:339
  129.7 0.8 copy-start.12
  130.6 1.1 copy-start.11
  131.6 1.1 copy-start.13
  135.1 1.0 copy-start.5
  136.0 1.0 copy-start.7
  137.0 2.3 %copy-start = (bf16[9216,256]{1,0:T(8,128)(2,1)S(1)}, bf16[9216,256]{1,0:T(8,128)(2,1)}, u32[]{:S(2)}) copy-start(bf16[9216,256]{1,0:T(8,128)(2,1)} %all-gather.3.cloned.1.call-done) | copy-start | bytes 14155780
  139.4 1.6 copy-start.4
  143.0 12.9 %collective-permute-start.9 = (bf16[288,256]{1,0:T(8,128)(2,1)}, bf16[288,256]{1,0:T(8,128)(2,1)}, u32[]{:S(2)}, u32[]{:S(2)}) collective-permute-start(bf16[288,256]{1,0:T(8,128)(2,1)} %get-tuple-element.18), channel_id=1, source_target_pairs={{0,1},{1,0},{2,3},{3,2},{4,5},{5,4},{6,7},{7,6},{8,9},{9,8},{10,11... | collective-permute-start | bytes 442376 | tf_op jit(solution)/shard_map/ppermute | solution.py:350
  145.3 2.3 %copy-start.1 = (bf16[9216,256]{1,0:T(8,128)(2,1)S(1)}, bf16[9216,256]{1,0:T(8,128)(2,1)}, u32[]{:S(2)}) copy-start(bf16[9216,256]{1,0:T(8,128)(2,1)} %all-gather.3.cloned.1.call-done) | copy-start | bytes 14155780
  148.5 7.5 %copy-start.6 = (bf16[512,1024]{1,0:T(8,128)(2,1)S(1)}, bf16[512,1024]{1,0:T(8,128)(2,1)}, u32[]{:S(2)}) copy-start(bf16[512,1024]{1,0:T(8,128)(2,1)} %copy-done.5) | copy-start | bytes 3145732
  148.5 7.5 %copy-start.8 = (bf16[512,1024]{1,0:T(8,128)(2,1)S(1)}, bf16[512,1024]{1,0:T(8,128)(2,1)}, u32[]{:S(2)}) copy-start(bf16[512,1024]{1,0:T(8,128)(2,1)} %copy-done.7) | copy-start | bytes 3145732
  148.5 8.9 %collective-permute-start.18 = (bf16[288,256]{1,0:T(8,128)(2,1)S(1)}, bf16[288,256]{1,0:T(8,128)(2,1)S(1)}, u32[]{:S(2)}, u32[]{:S(2)}) collective-permute-start(bf16[288,256]{1,0:T(8,128)(2,1)S(1)} %shard_map.71), channel_id=1, source_target_pairs={{0,1},{1,0},{2,3},{3,2},{4,5},{5,4},{6,7},{7,6},{8,9},{9,8},{10,11... | collective-permute-start | bytes 442376 | tf_op jit(solution)/shard_map/ppermute | solution.py:352
Sparse Core Ops, SparseCore 0:
  46.1 73.2 all-gather.2
